TPU v7x, 32 devices: a whole 2x2x4 slice. The times are simulated.
32 devices in a mesh: section: 2 (over core), tensor: 2 (over x), dp: 8 (over z, y).
Axes of the slice: x: 2, y: 2, z: 4, core: 2. Of those that a mesh axis runs over, the one named last changes fastest.
Arguments:
- enc_in: bfloat16 [2, 784, 768], P(None, 'dp'), may hold values from -6 to 6
- keep_index: int32 [2, 16, 49], P(None, 'dp'), may hold values from 0 to 195, as said below
- image_count: int32 [2, 8], P(None, 'dp'), may hold values from 1 to 2
- enc_vec: bfloat16 [6, 768], replicated, may hold values from -0.8 to 1.5
- enc_qkv: bfloat16 [768, 3, 768], P(None, None, 'tensor'), may hold values from -0.21875 to 0.21875
- enc_qv_bias: bfloat16 [2, 768], P(None, 'tensor'), may hold values from -0.5 to 0.5
- enc_out_w: bfloat16 [768, 768], P('tensor'), may hold values from -0.875 to 0.875
- enc_fc1: bfloat16 [768, 3072], P(None, 'tensor'), may hold values from -0.21875 to 0.21875
- enc_fc1_bias: bfloat16 [3072], P('tensor'), may hold values from -1.5 to 1.5
- enc_fc2: bfloat16 [3072, 768], P('tensor'), may hold values from -0.109375 to 0.109375
- bridge_w: bfloat16 [768, 512], replicated, may hold values from -0.21875 to 0.21875
- dec_vec: bfloat16 [8, 512], replicated, may hold values from -4 to 4
- dec_pos: bfloat16 [196, 512], replicated, may hold values from -3 to 3
- dec_qkv: bfloat16 [512, 3, 512], P(None, None, 'tensor'), may hold values from -0.25 to 0.25
- dec_qv_bias: bfloat16 [2, 512], P(None, 'tensor'), may hold values from -0.5 to 0.5
- dec_out_w: bfloat16 [512, 512], P('tensor'), may hold values from -1.5 to 1.5
- dec_fc1: bfloat16 [512, 2048], P(None, 'tensor'), may hold values from -0.25 to 0.25
- dec_fc1_bias: bfloat16 [2048], P('tensor'), may hold values from -1.5 to 1.5
- dec_fc2: bfloat16 [2048, 512], P('tensor'), may hold values from -0.125 to 0.125
- dec_cot: bfloat16 [2, 3136, 512], P(None, 'dp'), may hold values from -6 to 6
Outputs:
- enc_out: bfloat16 [2, 784, 768], P(None, 'dp')
- dec_out: bfloat16 [2, 3136, 512], P('section', 'dp')
- grad_in: float32 [2, 784, 768], P('section', 'dp')
- grad_enc_vec: float32 [6, 768], replicated
- grad_enc_qkv: float32 [768, 3, 768], P(None, None, 'tensor')
- grad_enc_qv_bias: float32 [2, 768], P(None, 'tensor')
- grad_enc_out_w: float32 [768, 768], P('tensor')
- grad_enc_fc1: float32 [768, 3072], P(None, 'tensor')
- grad_enc_fc1_bias: float32 [3072], P('tensor')
- grad_enc_fc2: float32 [3072, 768], P('tensor')
- grad_bridge_w: float32 [768, 512], replicated
- grad_dec_vec: float32 [8, 512], replicated
- grad_dec_pos: float32 [196, 512], replicated
- grad_dec_qkv: float32 [512, 3, 512], P(None, None, 'tensor')
- grad_dec_qv_bias: float32 [2, 512], P(None, 'tensor')
- grad_dec_out_w: float32 [512, 512], P('tensor')
- grad_dec_fc1: float32 [512, 2048], P(None, 'tensor')
- grad_dec_fc1_bias: float32 [2048], P('tensor')
- grad_dec_fc2: float32 [2048, 512], P('tensor')
Inputs may be any that keep to these rules, and one draw needn't show every extreme that they name: `keep_index`: within one image slot the 49 numbers are different.
All inputs are finite; a program needn't handle non-finite values.
Results may differ from a plain program's by a relative error of at most 0.025.
Values may be sent and summed in bfloat16 or wider, within the bound.
No kernel may reach another device: no remote copies, remote signals or barrier semaphores. Data moves between devices by JAX's collectives and lax.ppermute only.
A program may use at most 192 MiB of HBM per device.

v0:
```python
import functools
import math

import jax
import jax.numpy as jnp
from jax import lax
from jax.experimental import pallas as pl
from jax.experimental.pallas import tpu as pltpu
from jax.sharding import PartitionSpec as P

HE = 12
HD = 16
PATCHES = 196
VIS = 49
PAD_E = 64
PAD_D = 208
LANES = 128
EPSILON = 1e-06
LOW = jnp.bfloat16
FULL = jnp.float32
MIB = 2**20


def low(values):
    return values.astype(LOW)


def full(values):
    return values.astype(FULL)


def matmul(left, right):
    return jnp.dot(left, right, preferred_element_type=FULL)


def left_product(left, right):
    return lax.dot_general(left, right, (((0,), (0,)), ((), ())), preferred_element_type=FULL)


def right_product(left, right):
    return lax.dot_general(left, right, (((1,), (1,)), ((), ())), preferred_element_type=FULL)


def pair(first, second):
    return full(first) + full(second)


def swap(value, axis):
    return lax.ppermute(value, axis, [(i, i ^ 1) for i in range(lax.axis_size(axis))])


def normalize(values):
    center = values - jnp.mean(values, axis=-1, keepdims=True)
    scale = lax.rsqrt(jnp.mean(center * center, axis=-1, keepdims=True) + EPSILON)
    return center * scale, scale


def norm_back(grad, gain, xhat, scale):
    inner = grad * gain
    return scale * (
        inner
        - jnp.mean(inner, axis=-1, keepdims=True)
        - xhat * jnp.mean(inner * xhat, axis=-1, keepdims=True)
    )


def column_sum(values):
    return jnp.sum(full(values), axis=0, keepdims=True)


def one_hot_rows(padded, length, images, packed_first=False):
    shape = (images * length, images * padded) if packed_first else (images * padded, images * length)
    first = lax.broadcasted_iota(jnp.int32, shape, 0)
    second = lax.broadcasted_iota(jnp.int32, shape, 1)
    packed, wide = (first, second) if packed_first else (second, first)
    hit = None
    for image in range(images):
        here = (
            (packed >= image * length)
            & (packed < (image + 1) * length)
            & (wide - image * padded == packed - image * length)
        )
        hit = here if hit is None else hit | here
    return low(jnp.where(hit, 1.0, 0.0))


def head_masks(head_size):
    lane = lax.broadcasted_iota(jnp.int32, (1, LANES), 1)
    return [
        jnp.where((lane >= j * head_size) & (lane < (j + 1) * head_size), 1.0, 0.0)
        for j in range(LANES // head_size)
    ]


def spread_heads(values, masks):
    wide = full(values)
    return jnp.concatenate([low(wide * mask) for mask in masks], axis=0)


def gather_heads(stacked, masks):
    rows = stacked.shape[0] // len(masks)
    total = None
    for j, mask in enumerate(masks):
        term = stacked[j * rows : (j + 1) * rows] * mask
        total = term if total is None else total + term
    return total


def attend(queries, key_rows, value_rows, masks, allowed, factor):
    scores = right_product(spread_heads(queries, masks), key_rows) * factor
    scores = jnp.where(allowed, scores, -1e30)
    exponent = jnp.exp(scores - jnp.max(scores, axis=-1, keepdims=True))
    weights_low = low(exponent * (1.0 / jnp.sum(exponent, axis=-1, keepdims=True)))
    return weights_low, low(gather_heads(matmul(weights_low, value_rows), masks))


def attend_back(queries, key_rows, value_rows, weights_low, upstream, masks, factor):
    spread_up = spread_heads(upstream, masks)
    weight_grad = right_product(spread_up, value_rows)
    weights = full(weights_low)
    product = weights * weight_grad
    score_grad = low(product - weights * jnp.sum(product, axis=-1, keepdims=True))
    query_grad = gather_heads(matmul(score_grad, key_rows), masks) * factor
    key_grad = left_product(score_grad, spread_heads(queries, masks)) * factor
    value_grad = left_product(weights_low, spread_up)
    return low(query_grad), low(key_grad), low(value_grad)


def same_image(heads, images, padded, length):
    shape = (heads * images * padded, images * padded)
    row = lax.broadcasted_iota(jnp.int32, shape, 0)
    key = lax.broadcasted_iota(jnp.int32, shape, 1)
    hit = None
    for head in range(heads):
        for image in range(images):
            start = (head * images + image) * padded
            here = (
                (row >= start)
                & (row < start + padded)
                & (key >= image * padded)
                & (key < image * padded + length)
            )
            hit = here if hit is None else hit | here
    return hit


def live_rows(count, rows, padded):
    row = lax.broadcasted_iota(jnp.int32, (rows, 1), 0)
    return jnp.where(row < count * padded, 1.0, 0.0)


def kernel_call(order, kernel, outs, *arguments, scalars=0, scratch=(), name=None):
    count = len(arguments)
    before = order[-1:]

    def run(*refs):
        mark = count + len(before) + len(outs)
        refs[mark][...] = jnp.zeros((8, LANES), FULL)
        kernel(*refs[:count], *refs[count + len(before) : mark], *refs[mark + 1 :])

    specs = [pl.BlockSpec(memory_space=pltpu.SMEM)] * scalars
    specs += [pl.BlockSpec(memory_space=pltpu.VMEM)] * (count - scalars)
    specs += [pl.BlockSpec(memory_space=pl.ANY)] * len(before)
    results = pl.pallas_call(
        run,
        out_shape=[jax.ShapeDtypeStruct(x.shape, x.dtype) for x in outs] + [shaped((8, LANES), FULL)],
        in_specs=specs,
        out_specs=[pl.BlockSpec(memory_space=pltpu.VMEM)] * (len(outs) + 1),
        scratch_shapes=scratch,
        compiler_params=pltpu.CompilerParams(vmem_limit_bytes=24 * MIB),
        cost_estimate=pl.CostEstimate(flops=2 * 10**11, bytes_accessed=1, transcendentals=0),
        name=name,
    )(*arguments, *before)
    order.append(results[-1])
    return results[:-1]


def shaped(shape, dtype=LOW):
    return jax.ShapeDtypeStruct(shape, dtype)


def project_heads(normed, qkv_ref, bias, proj_ref, width):
    queries = low(matmul(normed, qkv_ref[0]) + bias[0:1])
    key_rows = low(matmul(normed, qkv_ref[1]))
    value_rows = low(matmul(normed, qkv_ref[2]) + bias[1:2])
    proj_ref[0] = queries
    proj_ref[1] = key_rows
    proj_ref[2] = value_rows


def enc_attend_kernel(
    images, head_size, place_ref, x_ref, vec_ref, qkv_ref, bias_ref, out_w_ref,
    part_ref, x_out_ref, normed_ref, proj_ref, weights_ref, mix_ref,
):
    width = qkv_ref.shape[2]
    if len(x_ref.shape) == 2:
        rows = x_ref[...]
    else:
        rows = low(jnp.where(place_ref[0] == 0, full(x_ref[:, 0, :]), full(x_ref[:, 1, :])))
    x = matmul(one_hot_rows(PAD_E, VIS, images), rows)
    x_out_ref[...] = low(x)
    vec = full(vec_ref[...])
    xhat, _ = normalize(x)
    normed = low(xhat * vec[0:1] + vec[1:2])
    normed_ref[...] = normed
    project_heads(normed, qkv_ref, full(bias_ref[...]), proj_ref, width)
    masks = head_masks(head_size)
    allowed = same_image(len(masks), images, PAD_E, VIS)
    for group in range(width // LANES):
        lanes = slice(group * LANES, (group + 1) * LANES)
        weights_low, mixture = attend(
            proj_ref[0, :, lanes],
            proj_ref[1, :, lanes],
            proj_ref[2, :, lanes],
            masks,
            allowed,
            1.0 / math.sqrt(head_size),
        )
        weights_ref[group] = weights_low
        mix_ref[:, lanes] = mixture
    part_ref[...] = low(matmul(mix_ref[...], out_w_ref[...]))


def mlp_forward(middle, gain, shift, fc1_ref, bias_ref, fc2_ref, normed_ref, hidden_ref, slope_ref):
    xhat, _ = normalize(middle)
    normed = low(xhat * gain + shift)
    normed_ref[...] = normed
    pre = matmul(normed, fc1_ref[...]) + full(bias_ref[...])
    share = 0.5 + 0.5 * lax.erf(pre * math.sqrt(0.5))
    hidden = low(pre * share)
    hidden_ref[...] = hidden
    slope = share + pre * jnp.exp(-0.5 * pre * pre) * (1.0 / math.sqrt(2.0 * math.pi))
    if slope_ref is not None:
        slope_ref[...] = low(slope)
    return None if fc2_ref is None else low(matmul(hidden, fc2_ref[...])), slope


def enc_hidden_kernel(
    x_ref, vec_ref, part_ref, other_ref, fc1_ref, bias_ref, fc2_ref,
    part_two_ref, middle_ref, normed_ref, hidden_ref, slope_ref,
):
    vec = full(vec_ref[...])
    middle = full(x_ref[...]) + pair(part_ref[...], other_ref[...]) + vec[2:3]
    middle_ref[...] = middle
    part, _ = mlp_forward(
        middle, vec[3:4], vec[4:5], fc1_ref, bias_ref, fc2_ref, normed_ref, hidden_ref, slope_ref
    )
    part_two_ref[...] = part


def enc_side_hidden_kernel(
    x_ref, vec_ref, part_ref, other_ref, fc1_ref, bias_ref,
    middle_ref, normed_ref, hidden_ref, slope_ref,
):
    vec = full(vec_ref[...])
    middle = full(x_ref[...]) + pair(part_ref[...], other_ref[...]) + vec[2:3]
    middle_ref[...] = middle
    mlp_forward(middle, vec[3:4], vec[4:5], fc1_ref, bias_ref, None, normed_ref, hidden_ref, slope_ref)


def both_cores_kernel(place_ref, own_ref, over_ref, both_ref):
    first = place_ref[0] == 0
    own, over = full(own_ref[...]), full(over_ref[...])
    both_ref[:, 0, :] = low(jnp.where(first, own, over))
    both_ref[:, 1, :] = low(jnp.where(first, over, own))


def selector(keep_ref, image):
    patch = lax.broadcasted_iota(jnp.int32, (PAD_D, PAD_E), 0)
    return jnp.where(patch == keep_ref[image : image + 1, :], 1.0, 0.0)


def dec_attend_kernel(
    images, head_size, count_ref, keep_ref, middle_ref, part_ref, other_ref, enc_vec_ref, bridge_ref,
    vec_ref, pos_ref, qkv_ref, bias_ref, out_w_ref,
    part_out_ref, enc_out_ref, enc_pad_ref, starting_ref, normed_ref, proj_ref, weights_ref, mix_ref,
):
    width = qkv_ref.shape[2]
    vec = full(vec_ref[...])
    encoded = middle_ref[...] + pair(part_ref[...], other_ref[...]) + full(enc_vec_ref[...])[5:6]
    enc_pad = low(encoded * live_rows(count_ref[0], images * PAD_E, PAD_E))
    enc_pad_ref[...] = enc_pad
    enc_out_ref[...] = low(matmul(one_hot_rows(PAD_E, VIS, images, True), enc_pad))
    lifted = matmul(enc_pad, bridge_ref[...]) + vec[0:1]
    lifted_high = low(lifted)
    lifted_rest = low(lifted - full(lifted_high))
    pos = matmul(one_hot_rows(PAD_D, PATCHES, 1), pos_ref[...])
    for image in range(images):
        chosen = selector(keep_ref, image)
        rows = slice(image * PAD_E, (image + 1) * PAD_E)
        placed = matmul(low(chosen), lifted_high[rows]) + matmul(low(chosen), lifted_rest[rows])
        hidden_patch = 1.0 - jnp.sum(chosen, axis=1, keepdims=True)
        starting_ref[image * PAD_D : (image + 1) * PAD_D, :] = placed + hidden_patch * vec[1:2] + pos
    xhat, _ = normalize(starting_ref[...])
    normed = low(xhat * vec[2:3] + vec[3:4])
    normed_ref[...] = normed
    project_heads(normed, qkv_ref, full(bias_ref[...]), proj_ref, width)
    masks = head_masks(head_size)
    allowed = lax.broadcasted_iota(jnp.int32, (1, PAD_D), 1) < PATCHES
    groups = width // LANES
    for image in range(images):
        rows = slice(image * PAD_D, (image + 1) * PAD_D)
        for group in range(groups):
            lanes = slice(group * LANES, (group + 1) * LANES)
            weights_low, mixture = attend(
                proj_ref[0, rows, lanes],
                proj_ref[1, rows, lanes],
                proj_ref[2, rows, lanes],
                masks,
                allowed,
                1.0 / math.sqrt(head_size),
            )
            weights_ref[image * groups + group] = weights_low
            mix_ref[rows, lanes] = mixture
    part_out_ref[...] = low(matmul(mix_ref[...], out_w_ref[...]))


def dec_hidden_kernel(
    images, count_ref, starting_ref, part_ref, other_ref, vec_ref, fc1_ref, bias_ref, fc2_ref, cot_ref,
    part_back_ref, part_two_ref, middle_ref, normed_ref, hidden_ref, out_low_ref, up_ref,
    up_sum_ref, out_sum_ref,
):
    vec = full(vec_ref[...])
    middle = starting_ref[...] + pair(part_ref[...], other_ref[...]) + vec[4:5]
    middle_ref[...] = middle
    part, slope = mlp_forward(
        middle, vec[5:6], vec[6:7], fc1_ref, bias_ref, fc2_ref, normed_ref, hidden_ref, None
    )
    part_two_ref[...] = part
    spread = matmul(one_hot_rows(PAD_D, PATCHES, images), cot_ref[...])
    out_low = low(spread * live_rows(count_ref[0], images * PAD_D, PAD_D))
    out_low_ref[...] = out_low
    up_grad = low(slope * right_product(out_low, fc2_ref[...]))
    up_ref[...] = up_grad
    part_back_ref[...] = low(right_product(up_grad, fc1_ref[...]))
    up_sum_ref[...] = column_sum(up_grad)
    out_sum_ref[...] = column_sum(out_low)


def dec_out_kernel(images, count_ref, middle_ref, part_ref, other_ref, vec_ref, out_ref):
    decoded = middle_ref[...] + pair(part_ref[...], other_ref[...]) + full(vec_ref[...])[7:8]
    decoded = low(decoded * live_rows(count_ref[0], images * PAD_D, PAD_D))
    out_ref[...] = low(matmul(one_hot_rows(PAD_D, PATCHES, images, True), decoded))


def attention_back(
    first_row, images, padded, together, head_size, mixture_grad, proj_ref, weights_ref, stacked_ref
):
    masks = head_masks(head_size)
    groups = proj_ref.shape[2] // LANES
    step = images if together else 1
    for first in range(0, images, step):
        rows = slice(first * padded, (first + step) * padded)
        out_rows = slice(first_row + first * padded, first_row + (first + step) * padded)
        for group in range(groups):
            lanes = slice(group * LANES, (group + 1) * LANES)
            grads = attend_back(
                proj_ref[0, rows, lanes],
                proj_ref[1, rows, lanes],
                proj_ref[2, rows, lanes],
                weights_ref[first // step * groups + group],
                mixture_grad[out_rows, lanes],
                masks,
                1.0 / math.sqrt(head_size),
            )
            for j in range(3):
                stacked_ref[j, out_rows, lanes] = grads[j]


def normed_back(stacked_ref, qkv_ref):
    total = right_product(stacked_ref[0], qkv_ref[0])
    for j in (1, 2):
        total = total + right_product(stacked_ref[j], qkv_ref[j])
    return low(total)


def dec_attend_back_kernel(
    images, head_size, middle_ref, out_low_ref, part_in_ref, other_ref, vec_ref, proj_ref, weights_ref,
    qkv_ref, out_w_ref,
    part_ref, middle_grad_ref, middle_low_ref, stacked_ref, sums_ref, bias_sum_ref,
):
    vec = full(vec_ref[...])
    two_grad = pair(part_in_ref[...], other_ref[...])
    xhat, scale = normalize(middle_ref[...])
    middle_grad = full(out_low_ref[...]) + norm_back(two_grad, vec[5:6], xhat, scale)
    middle_grad_ref[...] = middle_grad
    middle_low = low(middle_grad)
    middle_low_ref[...] = middle_low
    mixture_grad = low(right_product(middle_low, out_w_ref[...]))
    attention_back(0, images, PAD_D, False, head_size, mixture_grad, proj_ref, weights_ref, stacked_ref)
    part_ref[...] = normed_back(stacked_ref, qkv_ref)
    sums_ref[0:1] = column_sum(middle_grad)
    sums_ref[1:2] = column_sum(two_grad * xhat)
    sums_ref[2:3] = column_sum(two_grad)
    bias_sum_ref[0:1] = column_sum(stacked_ref[0])
    bias_sum_ref[1:2] = column_sum(stacked_ref[2])


def dec_start_back_kernel(
    images, count_ref, keep_ref, starting_ref, part_ref, other_ref, vec_ref, middle_grad_ref, bridge_ref,
    enc_cot_ref, lifted_ref, pos_ref, sums_ref,
):
    vec = full(vec_ref[...])
    one_grad = pair(part_ref[...], other_ref[...])
    xhat, scale = normalize(starting_ref[...])
    starting_grad = middle_grad_ref[...] + norm_back(one_grad, vec[2:3], xhat, scale)
    sums_ref[2:3] = column_sum(one_grad * xhat)
    sums_ref[3:4] = column_sum(one_grad)
    token = None
    total = None
    for image in range(images):
        grad = starting_grad[image * PAD_D : (image + 1) * PAD_D]
        chosen = selector(keep_ref, image)
        hidden_patch = 1.0 - jnp.sum(chosen, axis=1, keepdims=True)
        term = column_sum(hidden_patch * grad)
        token = term if token is None else token + term
        total = grad if total is None else total + grad
        lifted_ref[image * PAD_E : (image + 1) * PAD_E, :] = low(left_product(low(chosen), low(grad)))
    pos_ref[...] = total
    lifted_grad = lifted_ref[...]
    sums_ref[0:1] = column_sum(lifted_grad)
    sums_ref[1:2] = token
    handed = right_product(lifted_grad, bridge_ref[...])
    enc_cot_ref[...] = low(handed * live_rows(count_ref[0], images * PAD_E, PAD_E))


def enc_hidden_back_kernel(cot_a, cot_b, slope_a, slope_b, fc1_ref, fc2_ref, part_ref, up_ref):
    slope = jnp.concatenate([slope_a[...], slope_b[...]], axis=0)
    up_grad = low(full(slope) * right_product(stacked_rows(cot_a, cot_b), fc2_ref[...]))
    up_ref[...] = up_grad
    part_ref[...] = low(right_product(up_grad, fc1_ref[...]))


def enc_attend_back_kernel(
    images, head_size, middle_a, middle_b, cot_a, cot_b, part_in_ref, other_ref, vec_ref, proj_a, proj_b,
    weights_a, weights_b, qkv_ref, out_w_ref, up_ref,
    part_ref, middle_grad_ref, middle_low_ref, stacked_ref, sums_ref, bias_sum_ref, up_sum_ref,
):
    vec = full(vec_ref[...])
    own = middle_a.shape[0]
    cot = full(stacked_rows(cot_a, cot_b))
    two_grad = pair(part_in_ref[...], other_ref[...])
    xhat, scale = normalize(stacked_rows(middle_a, middle_b))
    middle_grad = cot + norm_back(two_grad, vec[3:4], xhat, scale)
    middle_grad_ref[...] = middle_grad
    middle_low = low(middle_grad)
    middle_low_ref[...] = middle_low
    mixture_grad = low(right_product(middle_low, out_w_ref[...]))
    attention_back(0, images, PAD_E, True, head_size, mixture_grad, proj_a, weights_a, stacked_ref)
    attention_back(own, images, PAD_E, True, head_size, mixture_grad, proj_b, weights_b, stacked_ref)
    part_ref[...] = normed_back(stacked_ref, qkv_ref)
    sums_ref[0:1] = column_sum(middle_grad)
    sums_ref[1:2] = column_sum(two_grad * xhat)
    sums_ref[2:3] = column_sum(two_grad)
    sums_ref[3:4] = column_sum(cot)
    bias_sum_ref[0:1] = column_sum(stacked_ref[0])
    bias_sum_ref[1:2] = column_sum(stacked_ref[2])
    up_sum_ref[...] = column_sum(up_ref[...])


def enc_start_back_kernel(
    images, x_a, x_b, part_ref, other_ref, vec_ref, middle_grad_ref, sums_ref, up_sum_ref, bias_sum_ref,
    grad_in_ref, small_ref, rows_ref,
):
    vec = full(vec_ref[...])
    own = x_a.shape[0]
    one_grad = pair(part_ref[...], other_ref[...])
    xhat, scale = normalize(full(stacked_rows(x_a, x_b)))
    grad = middle_grad_ref[:own] + norm_back(one_grad[:own], vec[0:1], xhat[:own], scale[:own])
    take = full(one_hot_rows(PAD_E, VIS, images, True))
    grad_in_ref[:, 0, :] = jnp.dot(
        take, grad, preferred_element_type=FULL, precision=lax.Precision.HIGHEST
    )
    rows_ref[...] = jnp.zeros_like(rows_ref)
    rows_ref[0:1] = column_sum(one_grad * xhat)
    rows_ref[1:2] = column_sum(one_grad)
    rows_ref[2:6] = sums_ref[...]
    put_rows(rows_ref, 6, up_sum_ref, bias_sum_ref)
    small_ref[...] = low(rows_ref[...])


def chunk(index, size):
    return pl.ds(pl.multiple_of(index * size, LANES), size)


def dec_hidden_weights_kernel(place_ref, hidden_ref, out_low_ref, normed_ref, up_ref, keep_ref, send_ref):
    core = place_ref[0]
    rows, cols = hidden_ref.shape[1] // 2, out_low_ref.shape[1]
    half = normed_ref.shape[1] // 2
    for ref, index in ((send_ref, 1 - core), (keep_ref, core)):
        down = low(left_product(hidden_ref[:, chunk(index, rows)], out_low_ref[...]))
        up = low(left_product(normed_ref[:, chunk(index, half)], up_ref[...]))
        for part in range(2):
            ref[0, part] = down[part * rows // 2 : (part + 1) * rows // 2]
            ref[1, part] = up[:, part * cols : (part + 1) * cols]


def head_blocks(normed, stacked_ref, mix, middle_low_ref, core, side):
    half = normed[0].shape[1] // 2
    wide = middle_low_ref.shape[1] // 2
    left = jnp.concatenate([ref[:, chunk(core, half)] for ref in normed], axis=0)
    if side == 0:
        return low(left_product(left, stacked_ref[0])), low(left_product(left, stacked_ref[1]))
    out = left_product(
        jnp.concatenate([ref[...] for ref in mix], axis=0), middle_low_ref[:, chunk(core, wide)]
    )
    return low(left_product(left, stacked_ref[2])), low(out)


def dec_head_weights_kernel(
    place_ref, normed_ref, stacked_ref, mix_ref, middle_low_ref, keep_ref, send_ref
):
    core = place_ref[0]
    width = mix_ref.shape[1]
    for ref, index in ((send_ref, 1 - core), (keep_ref, core)):
        for side in range(2):
            first, second = head_blocks(
                [normed_ref], stacked_ref, [mix_ref], middle_low_ref, index, side
            )
            rows = first.shape[0] // 2
            for part in range(2):
                ref[side, part, :, :width] = first[part * rows : (part + 1) * rows]
                ref[side, part, :, width:] = second[part * rows : (part + 1) * rows]


def put_rows(rows_ref, row, up_sum_ref, bias_sum_ref):
    cols = rows_ref.shape[1]
    for piece in range(up_sum_ref.shape[1] // cols):
        rows_ref[row : row + 1] = up_sum_ref[:, piece * cols : (piece + 1) * cols]
        row += 1
    width = bias_sum_ref.shape[1]
    for piece in range(2):
        here, lane = row + piece * width // cols, piece * width % cols
        rows_ref[here : here + 1, lane : lane + width] = bias_sum_ref[piece : piece + 1]


def take_rows(rows_ref, row, up_sum_ref, bias_sum_ref):
    cols = rows_ref.shape[1]
    for piece in range(up_sum_ref.shape[1] // cols):
        up_sum_ref[:, piece * cols : (piece + 1) * cols] = rows_ref[row : row + 1]
        row += 1
    width = bias_sum_ref.shape[1]
    for piece in range(2):
        here, lane = row + piece * width // cols, piece * width % cols
        bias_sum_ref[piece : piece + 1] = rows_ref[here : here + 1, lane : lane + width]


def dec_bridge_weights_kernel(
    place_ref, enc_pad_ref, lifted_ref, pos_ref, sums_ref, middle_sums_ref, out_sum_ref, up_sum_ref,
    bias_sum_ref, keep_ref, send_ref, small_ref,
):
    core = place_ref[0]
    cols = lifted_ref.shape[1]
    bridge = low(left_product(enc_pad_ref[...], lifted_ref[...]))
    quarter = bridge.shape[0] // 4
    small_ref[...] = jnp.zeros_like(small_ref)
    small_ref[0:PAD_D] = pos_ref[...]
    row = PAD_D
    for ref, count in ((sums_ref, 4), (middle_sums_ref, 3), (out_sum_ref, 1)):
        small_ref[row : row + count] = ref[...]
        row += count
    put_rows(small_ref, row, up_sum_ref, bias_sum_ref)
    few = small_ref.shape[0] // 4
    first = core == 0

    def block(index):
        return jnp.concatenate(
            [bridge[index * quarter : (index + 1) * quarter], low(small_ref[index * few : (index + 1) * few])],
            axis=0,
        )

    for side in range(2):
        zero, one = block(side), block(2 + side)
        half = zero.shape[0] // 2
        for part in range(2):
            rows = slice(part * half, (part + 1) * half)
            keep_ref[side, part] = jnp.where(first, zero[rows], one[rows])
            send_ref[side, part] = jnp.where(first, one[rows], zero[rows])


def stacked_rows(first, second, lanes=slice(None)):
    return jnp.concatenate([first[:, lanes], second[:, lanes]], axis=0)


def enc_down_weights_kernel(place_ref, hidden_a, hidden_b, cot_a, cot_b, keep_ref, send_ref):
    core, side = place_ref[0], place_ref[1]
    cot = stacked_rows(cot_a, cot_b)
    half = keep_ref.shape[1]
    for ref, index in ((send_ref, 1 - core), (keep_ref, core)):
        block = low(left_product(stacked_rows(hidden_a, hidden_b, chunk(2 * index + side, 2 * half)), cot))
        ref[0] = block[:half]
        ref[1] = block[half:]


def enc_up_weights_kernel(place_ref, normed_a, normed_b, up_ref, keep_ref, send_ref):
    core, side = place_ref[0], place_ref[1]
    normed = stacked_rows(normed_a, normed_b)
    half, cols = keep_ref.shape[1:]
    for ref, index in ((send_ref, 1 - core), (keep_ref, core)):
        block = low(left_product(normed, up_ref[:, chunk(2 * index + side, cols)]))
        ref[0] = block[:half]
        ref[1] = block[half:]


def enc_head_weights_kernel(
    place_ref, normed_a, normed_b, stacked_ref, mix_a, mix_b, middle_low_ref, small_ref, keep_ref, send_ref
):
    core = place_ref[0]
    width = mix_a.shape[1]
    for wanted in range(2):

        @pl.when(place_ref[1] == wanted)
        def _(wanted=wanted):
            for ref, index in ((send_ref, 1 - core), (keep_ref, core)):
                first, second = head_blocks(
                    [normed_a, normed_b], stacked_ref, [mix_a, mix_b], middle_low_ref, index, wanted
                )
                rows = first.shape[0] // 2
                few = small_ref.shape[0] // 2
                for part in range(2):
                    ref[part, :rows, :width] = first[part * rows : (part + 1) * rows]
                    ref[part, :rows, width:] = second[part * rows : (part + 1) * rows]
                    ref[part, rows:] = small_ref[part * few : (part + 1) * few]


def fold_kernel(axis, place_ref, *refs):
    index = place_ref[axis]
    mine_ref, theirs_ref = refs[-2:]
    rows = 0
    for keep_ref, other_ref in zip(refs[:-2:2], refs[1:-2:2]):
        here = (slice(None),) * (len(keep_ref.shape) - 3) + (slice(rows, rows + keep_ref.shape[-2]),)
        rows += keep_ref.shape[-2]
        mine_ref[here] = low(pair(keep_ref[index], other_ref[index]))
        theirs_ref[here] = low(pair(keep_ref[1 - index], other_ref[1 - index]))


def add_kernel(first_ref, second_ref, sum_ref):
    sum_ref[...] = low(pair(first_ref[...], second_ref[...]))


def fold(order, place, axis, *arrays):
    shape = arrays[0].shape[1:-2] + (sum(x.shape[-2] for x in arrays[::2]), arrays[0].shape[-1])
    return kernel_call(
        order, functools.partial(fold_kernel, axis), [shaped(shape)] * 2, place, *arrays, scalars=1, name="fold"
    )


def add(order, first, second):
    return kernel_call(order, add_kernel, [shaped(first.shape)], first, second, name="add")[0]


def flip(value, step):
    return lax.ppermute(value, "dp", [(i, i ^ step) for i in range(lax.axis_size("dp"))])


def cross_start(value):
    return flip(value, 4) if lax.axis_size("dp") > 4 else jnp.zeros_like(value)


def cross_end(order, value, arrived):
    value = add(order, value, arrived)
    step = 8
    while step < lax.axis_size("dp"):
        value = add(order, value, flip(value, step))
        step *= 2
    return value


def pack_kernel(place_ref, mine_ref, other_ref, across_ref, there_ref, packed_ref):
    side, half = place_ref[1], place_ref[2]
    packed_ref[side, half] = mine_ref[...]
    packed_ref[side, 1 - half] = other_ref[...]
    packed_ref[1 - side, half] = across_ref[...]
    packed_ref[1 - side, 1 - half] = there_ref[...]


def pieces_of(place_ref, own_ref, over_ref):
    core = place_ref[0]
    return [
        (ref.at[side, half], index, side, half)
        for ref, index in ((own_ref, core), (over_ref, 1 - core))
        for side in range(2)
        for half in range(2)
    ]


def aligned(index, size):
    return pl.ds(pl.multiple_of(index * size, size), size)


def dec_hidden_whole_kernel(place_ref, own_ref, over_ref, fc1_ref, fc2_ref):
    for ref, core, side, half in pieces_of(place_ref, own_ref, over_ref):
        rows, cols = ref.shape
        if side == 0:
            fc2_ref[aligned(2 * core + half, rows), :] = full(ref[...])
        else:
            fc1_ref[aligned(core, rows), half * cols : (half + 1) * cols] = full(ref[...])


def put_heads(ref, rows, core, side, half, qkv_ref, out_w_ref):
    width = qkv_ref.shape[2]
    here = aligned(2 * core + half, rows)
    if side == 0:
        qkv_ref[0, here, :] = full(ref[:rows, :width])
        qkv_ref[1, here, :] = full(ref[:rows, width:])
    else:
        qkv_ref[2, here, :] = full(ref[:rows, :width])
        out_w_ref[half * rows : (half + 1) * rows, aligned(core, width)] = full(ref[:rows, width:])


def enc_head_whole_kernel(
    place_ref, own_ref, over_ref, qkv_ref, out_w_ref, vec_ref, up_sum_ref, bias_sum_ref, rows_ref
):
    few = rows_ref.shape[0] // 2
    rows = own_ref.shape[2] - few
    for ref, core, side, half in pieces_of(place_ref, own_ref, over_ref):
        put_heads(ref, rows, core, side, half, qkv_ref, out_w_ref)
    for half in range(2):
        rows_ref[half * few : (half + 1) * few] = full(own_ref[0, half, rows:])
    vec_ref[...] = rows_ref[0:6]
    take_rows(rows_ref, 6, up_sum_ref, bias_sum_ref)


def dec_rest_whole_kernel(
    place_ref, own_ref, over_ref, qkv_ref, out_w_ref, bridge_ref, pos_ref, vec_ref, up_sum_ref, bias_sum_ref,
    small_ref,
):
    quarter, few = bridge_ref.shape[0] // 4, small_ref.shape[0] // 4
    rows = qkv_ref.shape[1] // 4
    more = own_ref.shape[2] - rows
    for ref, core, side, half in pieces_of(place_ref, own_ref, over_ref):
        put_heads(ref, rows, core, side, half, qkv_ref, out_w_ref)
        index = 2 * core + side
        start = pl.multiple_of(index * quarter, 8)
        if half == 0:
            bridge_ref[pl.ds(start, more), :] = full(ref[rows:])
        else:
            left = quarter - more
            bridge_ref[pl.ds(start + more, left), :] = full(ref[rows : rows + left])
            small_ref[aligned(index, few), :] = full(ref[rows + left :])
    pos_ref[...] = small_ref[0:PATCHES]
    vec_ref[...] = small_ref[PAD_D : PAD_D + 8]
    take_rows(small_ref, PAD_D + 8, up_sum_ref, bias_sum_ref)


def enc_down_whole_kernel(place_ref, own_ref, over_ref, fc2_ref):
    for ref, core, side, half in pieces_of(place_ref, own_ref, over_ref):
        fc2_ref[aligned(4 * core + 2 * side + half, ref.shape[0]), :] = full(ref[...])


def enc_up_whole_kernel(place_ref, own_ref, over_ref, fc1_ref):
    for ref, core, side, half in pieces_of(place_ref, own_ref, over_ref):
        rows, cols = ref.shape
        fc1_ref[half * rows : (half + 1) * rows, aligned(2 * core + side, cols)] = full(ref[...])


def spread(piece):
    other = flip(piece, 2)
    return piece, other, flip(piece, 1), flip(other, 1)


def pack(order, place, pieces):
    (packed,) = kernel_call(
        order, pack_kernel, [shaped((2, 2) + pieces[0].shape)], place, *pieces, scalars=1, name="pack"
    )
    return packed, swap(packed, "section")


def pick(stacked, index):
    return lax.dynamic_index_in_dim(stacked, index, 0, keepdims=False)


def body(
    enc_in, keep_index, image_count, enc_vec, enc_qkv, enc_qv_bias, enc_out_w, enc_fc1, enc_fc1_bias, enc_fc2,
    bridge_w, dec_vec, dec_pos, dec_qkv, dec_qv_bias, dec_out_w, dec_fc1, dec_fc1_bias, dec_fc2, dec_cot,
):
    core = lax.axis_index("section")
    group = lax.axis_index("dp")
    place = jnp.stack([core, group % 2, group // 2 % 2]).astype(jnp.int32)
    images = keep_index.shape[1]
    enc_width, dec_width = bridge_w.shape
    enc_local, dec_local = enc_qkv.shape[2], dec_qkv.shape[2]
    enc_size, dec_size = enc_width // HE, dec_width // HD
    enc_mlp, dec_mlp = enc_fc1.shape[1], dec_fc1.shape[1]
    rows_e, rows_d = images * PAD_E, images * PAD_D
    enc_groups, dec_groups = enc_local // LANES, dec_local // LANES
    enc_heads, dec_heads = LANES // enc_size, LANES // dec_size
    enc_qkv, dec_qkv = jnp.transpose(enc_qkv, (1, 0, 2)), jnp.transpose(dec_qkv, (1, 0, 2))
    enc_fc1_bias, dec_fc1_bias = enc_fc1_bias[None], dec_fc1_bias[None]
    own_in = pick(enc_in, core)
    enc_in = jnp.transpose(enc_in, (1, 0, 2))
    keep = jnp.pad(pick(keep_index, core), ((0, 0), (0, PAD_E - VIS)), constant_values=-1)
    cot = pick(dec_cot, core)
    count = pick(image_count, core)
    dec_rows = images * PATCHES

    order = []
    call = functools.partial(kernel_call, order)

    def enc_attend(rows):
        return call(
            functools.partial(enc_attend_kernel, images, enc_size),
            [
                shaped((rows_e, enc_width)),
                shaped((rows_e, enc_width)),
                shaped((rows_e, enc_width)),
                shaped((3, rows_e, enc_local)),
                shaped((enc_groups, enc_heads * rows_e, rows_e)),
                shaped((rows_e, enc_local)),
            ],
            place, rows, enc_vec, enc_qkv, enc_qv_bias, enc_out_w,
            scalars=1, name="enc_attend",
        )

    side_in = flip(own_in, 1)
    part, x, normed, proj, weights, mix = enc_attend(enc_in)
    part_other = swap(part, "tensor")
    side_part, side_x, side_normed, side_proj, side_weights, side_mix = enc_attend(side_in)
    part_two, middle, normed_two, hidden, slope = call(
        enc_hidden_kernel,
        [
            shaped((rows_e, enc_width)),
            shaped((rows_e, enc_width), FULL),
            shaped((rows_e, enc_width)),
            shaped((rows_e, enc_mlp)),
            shaped((rows_e, enc_mlp)),
        ],
        x, enc_vec, part, part_other, enc_fc1, enc_fc1_bias, enc_fc2,
        name="enc_hidden",
    )
    part_two_other = swap(part_two, "tensor")
    side_part_other = swap(side_part, "tensor")

    (
        dec_part, enc_out, enc_pad, starting, dec_normed, dec_proj, dec_weights, dec_mix,
    ) = call(
        functools.partial(dec_attend_kernel, images, dec_size),
        [
            shaped((rows_d, dec_width)),
            shaped((images * VIS, enc_width)),
            shaped((rows_e, enc_width)),
            shaped((rows_d, dec_width), FULL),
            shaped((rows_d, dec_width)),
            shaped((3, rows_d, dec_local)),
            shaped((images * dec_groups, dec_heads * PAD_D, PAD_D)),
            shaped((rows_d, dec_local)),
        ],
        count, keep, middle, part_two, part_two_other, enc_vec, bridge_w,
        dec_vec, dec_pos, dec_qkv, dec_qv_bias, dec_out_w,
        scalars=1, name="dec_attend",
    )
    dec_part_other = swap(dec_part, "tensor")
    (enc_out_both,) = call(
        both_cores_kernel, [shaped((images * VIS, 2, enc_width))],
        place, enc_out, swap(enc_out, "section"), scalars=1, name="enc_out_both",
    )
    side_middle, side_normed_two, side_hidden, side_slope = call(
        enc_side_hidden_kernel,
        [
            shaped((rows_e, enc_width), FULL),
            shaped((rows_e, enc_width)),
            shaped((rows_e, enc_mlp)),
            shaped((rows_e, enc_mlp)),
        ],
        side_x, enc_vec, side_part, side_part_other, enc_fc1, enc_fc1_bias,
        name="enc_side_hidden",
    )
    (
        dec_part_back, dec_part_two, dec_middle, dec_normed_two, dec_hid, out_low, dec_up, up_sum, out_sum,
    ) = call(
        functools.partial(dec_hidden_kernel, images),
        [
            shaped((rows_d, dec_width)),
            shaped((rows_d, dec_width)),
            shaped((rows_d, dec_width), FULL),
            shaped((rows_d, dec_width)),
            shaped((rows_d, dec_mlp)),
            shaped((rows_d, dec_width)),
            shaped((rows_d, dec_mlp)),
            shaped((1, dec_mlp), FULL),
            shaped((1, dec_width), FULL),
        ],
        count, starting, dec_part, dec_part_other, dec_vec, dec_fc1, dec_fc1_bias, dec_fc2, cot,
        scalars=1, name="dec_hidden",
    )

    dec_part_back_other = swap(dec_part_back, "tensor")
    d1_keep, d1_send = call(
        dec_hidden_weights_kernel,
        [shaped((2, 2, dec_mlp // 4, dec_width))] * 2,
        place, dec_hid, out_low, dec_normed_two, dec_up,
        scalars=1, name="dec_hidden_weights",
    )
    d1_mine, d1_theirs = fold(order, place, 1, d1_keep, swap(d1_send, "section"))
    d1_arrived = flip(d1_theirs, 1)
    dec_part_one, dec_middle_grad, dec_middle_low, dec_stacked, middle_sums, dec_bias_sum = call(
        functools.partial(dec_attend_back_kernel, images, dec_size),
        [
            shaped((rows_d, dec_width)),
            shaped((rows_d, dec_width), FULL),
            shaped((rows_d, dec_width)),
            shaped((3, rows_d, dec_local)),
            shaped((3, dec_width), FULL),
            shaped((2, dec_local), FULL),
        ],
        dec_middle, out_low, dec_part_back, dec_part_back_other, dec_vec, dec_proj, dec_weights, dec_qkv, dec_out_w,
        name="dec_attend_back",
    )
    dec_part_one_other = swap(dec_part_one, "tensor")
    d1_mine, d1_theirs = fold(order, place, 2, d1_mine, d1_arrived)
    d1_arrived = flip(d1_theirs, 2)
    d2_keep, d2_send = call(
        dec_head_weights_kernel,
        [shaped((2, 2, dec_width // 4, 2 * dec_local))] * 2,
        place, dec_normed, dec_stacked, dec_mix, dec_middle_low,
        scalars=1, name="dec_head_weights",
    )
    d2_other = swap(d2_send, "section")
    d1 = add(order, d1_mine, d1_arrived)
    d1_arrived = cross_start(d1)
    enc_cot, lifted_grad, pos_grad, start_sums = call(
        functools.partial(dec_start_back_kernel, images),
        [
            shaped((rows_e, enc_width)),
            shaped((rows_e, dec_width)),
            shaped((PAD_D, dec_width), FULL),
            shaped((4, dec_width), FULL),
        ],
        count, keep, starting, dec_part_one, dec_part_one_other, dec_vec, dec_middle_grad, bridge_w,
        scalars=1, name="dec_start_back",
    )
    side_cot = flip(enc_cot, 1)
    small_rows = 256
    d3_keep, d3_send = call(
        dec_bridge_weights_kernel,
        [shaped((2, 2, enc_width // 8 + small_rows // 8, dec_width))] * 2,
        place, enc_pad, lifted_grad, pos_grad, start_sums, middle_sums, out_sum, up_sum, dec_bias_sum,
        scalars=1, scratch=[pltpu.VMEM((small_rows, dec_width), FULL)], name="dec_bridge_weights",
    )
    d3_other = swap(d3_send, "section")

    e1_keep, e1_send = call(
        enc_down_weights_kernel,
        [shaped((2, enc_mlp // 8, enc_width))] * 2,
        place, hidden, side_hidden, enc_cot, side_cot,
        scalars=1, name="enc_down_weights",
    )
    e1_other = swap(e1_send, "section")
    part, up = call(
        enc_hidden_back_kernel,
        [shaped((2 * rows_e, enc_width)), shaped((2 * rows_e, enc_mlp))],
        enc_cot, side_cot, slope, side_slope, enc_fc1, enc_fc2,
        name="enc_hidden_back",
    )
    part_other = swap(part, "tensor")
    e1_mine, e1_theirs = fold(order, place, 2, e1_keep, e1_other)
    e1_arrived = flip(e1_theirs, 2)
    d1 = cross_end(order, d1, d1_arrived)
    d1_spread = spread(d1)
    d2_mine, d2_theirs = fold(order, place, 1, d2_keep, d2_other, d3_keep, d3_other)
    d2_arrived = flip(d2_theirs, 1)
    e1 = add(order, e1_mine, e1_arrived)
    e1_arrived = cross_start(e1)
    back_part, middle_grad, middle_low, stacked, middle_two_sums, bias_sum, enc_up_sum = call(
        functools.partial(enc_attend_back_kernel, images, enc_size),
        [
            shaped((2 * rows_e, enc_width)),
            shaped((2 * rows_e, enc_width), FULL),
            shaped((2 * rows_e, enc_width)),
            shaped((3, 2 * rows_e, enc_local)),
            shaped((4, enc_width), FULL),
            shaped((2, enc_local), FULL),
            shaped((1, enc_mlp), FULL),
        ],
        middle, side_middle, enc_cot, side_cot, part, part_other, enc_vec, proj, side_proj,
        weights, side_weights, enc_qkv, enc_out_w, up,
        name="enc_attend_back",
    )
    back_part_other = swap(back_part, "tensor")
    d1_packed = pack(order, place, d1_spread)
    e2_keep, e2_send = call(
        enc_up_weights_kernel,
        [shaped((2, enc_width // 2, enc_mlp // 4))] * 2,
        place, normed_two, side_normed_two, up,
        scalars=1, name="enc_up_weights",
    )
    e2_other = swap(e2_send, "section")
    d2_mine, d2_theirs = fold(order, place, 2, d2_mine, d2_arrived)
    d2_arrived = flip(d2_theirs, 2)
    e2_mine, e2_theirs = fold(order, place, 2, e2_keep, e2_other)
    e2_arrived = flip(e2_theirs, 2)
    few = 32
    grad_in, small = call(
        functools.partial(enc_start_back_kernel, images),
        [shaped((images * VIS, 1, enc_width), FULL), shaped((few, enc_width))],
        x, side_x, back_part, back_part_other, enc_vec, middle_grad, middle_two_sums, enc_up_sum, bias_sum,
        scratch=[pltpu.VMEM((few, enc_width), FULL)], name="enc_start_back",
    )
    e3_keep, e3_send = call(
        enc_head_weights_kernel,
        [shaped((2, enc_width // 4 + few // 2, 2 * enc_local))] * 2,
        place, normed, side_normed, stacked, mix, side_mix, middle_low, small,
        scalars=1, name="enc_head_weights",
    )
    e3_other = swap(e3_send, "section")
    e1 = cross_end(order, e1, e1_arrived)
    e1_spread = spread(e1)
    e2 = add(order, e2_mine, e2_arrived)
    e2_arrived = cross_start(e2)
    e3_mine, e3_theirs = fold(order, place, 2, e3_keep, e3_other)
    e3_arrived = flip(e3_theirs, 2)
    g_dec_fc1, g_dec_fc2 = call(
        dec_hidden_whole_kernel,
        [shaped(dec_fc1.shape, FULL), shaped(dec_fc2.shape, FULL)],
        place, *d1_packed, scalars=1, name="dec_hidden_whole",
    )
    d2 = add(order, d2_mine, d2_arrived)
    d2_arrived = cross_start(d2)
    e1_packed = pack(order, place, e1_spread)
    e2 = cross_end(order, e2, e2_arrived)
    e2_spread = spread(e2)
    (g_enc_fc2,) = call(
        enc_down_whole_kernel, [shaped(enc_fc2.shape, FULL)],
        place, *e1_packed, scalars=1, name="enc_down_whole",
    )
    e3 = add(order, e3_mine, e3_arrived)
    e3_arrived = cross_start(e3)
    d2 = cross_end(order, d2, d2_arrived)
    d2_spread = spread(d2)
    e2_packed = pack(order, place, e2_spread)
    dec_part_two, e2_own = lax.optimization_barrier((dec_part_two, e2_packed[0]))
    dec_part_two_other = swap(dec_part_two, "tensor")
    (g_enc_fc1,) = call(
        enc_up_whole_kernel, [shaped(enc_fc1.shape, FULL)],
        place, e2_own, e2_packed[1], scalars=1, name="enc_up_whole",
    )
    e3 = cross_end(order, e3, e3_arrived)
    e3_spread = spread(e3)
    d2_packed = pack(order, place, d2_spread)
    (dec_out,) = call(
        functools.partial(dec_out_kernel, images),
        [shaped((dec_rows, dec_width))],
        count, dec_middle, dec_part_two, dec_part_two_other, dec_vec,
        scalars=1, name="dec_out",
    )
    g_dec_qkv, g_dec_out_w, g_bridge, g_dec_pos, g_dec_vec, g_dec_fc1_bias, g_dec_qv_bias = call(
        dec_rest_whole_kernel,
        [
            shaped(x.shape, FULL)
            for x in (dec_qkv, dec_out_w, bridge_w, dec_pos, dec_vec, dec_fc1_bias, dec_qv_bias)
        ],
        place, *d2_packed, scalars=1, scratch=[pltpu.VMEM((small_rows, dec_width), FULL)], name="dec_rest_whole",
    )
    e3_packed = pack(order, place, e3_spread)
    g_enc_qkv, g_enc_out_w, g_enc_vec, g_enc_fc1_bias, g_enc_qv_bias = call(
        enc_head_whole_kernel,
        [shaped(x.shape, FULL) for x in (enc_qkv, enc_out_w, enc_vec, enc_fc1_bias, enc_qv_bias)],
        place, *e3_packed, scalars=1, scratch=[pltpu.VMEM((few, enc_width), FULL)], name="enc_head_whole",
    )

    return (
        jnp.transpose(enc_out_both, (1, 0, 2)),
        dec_out[None],
        jnp.transpose(grad_in, (1, 0, 2)),
        g_enc_vec,
        jnp.transpose(g_enc_qkv, (1, 0, 2)),
        g_enc_qv_bias,
        g_enc_out_w,
        g_enc_fc1,
        g_enc_fc1_bias.reshape(-1),
        g_enc_fc2,
        g_bridge,
        g_dec_vec,
        g_dec_pos,
        jnp.transpose(g_dec_qkv, (1, 0, 2)),
        g_dec_qv_bias,
        g_dec_out_w,
        g_dec_fc1,
        g_dec_fc1_bias.reshape(-1),
        g_dec_fc2,
    )


def solution(mesh):
    return jax.shard_map(
        body,
        mesh=mesh,
        in_specs=(
            P(None, "dp", None),
            P(None, "dp", None),
            P(None, "dp"),
            P(),
            P(None, None, "tensor"),
            P(None, "tensor"),
            P("tensor", None),
            P(None, "tensor"),
            P("tensor"),
            P("tensor", None),
            P(),
            P(),
            P(),
            P(None, None, "tensor"),
            P(None, "tensor"),
            P("tensor", None),
            P(None, "tensor"),
            P("tensor"),
            P("tensor", None),
            P(None, "dp", None),
        ),
        out_specs=(
            P(None, "dp", None),
            P("section", "dp", None),
            P("section", "dp", None),
            P(),
            P(None, None, "tensor"),
            P(None, "tensor"),
            P("tensor", None),
            P(None, "tensor"),
            P("tensor"),
            P("tensor", None),
            P(),
            P(),
            P(),
            P(None, None, "tensor"),
            P(None, "tensor"),
            P("tensor", None),
            P(None, "tensor"),
            P("tensor"),
            P("tensor", None),
        ),
        check_vma=False,
    )
```

profile of v0, /device:TPU:0, one launch (start us, length us, event | category | flops | bytes accessed | tf_op | source)
XLA Modules:
  0.0 254.7 jit_solution(9098670246654215646)
XLA Ops:
  2.7 3.0 %collective-permute-start.1 = (bf16[98,768]{1,0:T(8,128)(2,1)}, bf16[98,768]{1,0:T(8,128)(2,1)}, u32[]{:S(2)}, u32[]{:S(2)}) collective-permute-start(bf16[98,768]{1,0:T(8,128)(2,1)} %bitcast.19), channel_id=1, source_target_pairs={{0,1},{1,0},{2,3},{3,2},{4,5},{5,4},{6,7},{7,6},{8,9},{9,8},{10,11... | collective-permute-start | bytes 451592 | tf_op jit(solution)/shard_map/ppermute | solution.py:653
  10.7 3.2 %enc_attend.2 = (bf16[128,768]{1,0:T(8,128)(2,1)}, bf16[128,768]{1,0:T(8,128)(2,1)S(1)}, bf16[128,768]{1,0:T(8,128)(2,1)S(1)}, bf16[3,128,384]{2,1,0:T(8,128)(2,...) custom-call(s32[3]{0:T(128)S(1)} %pad_add_fusion.refs_0_, ...), custom_call_target="tpu_custom_call" | custom-call | flops 199999995904 | bytes 1 | tf_op jit(solution)/shard_map/enc_attend/pallas_call | solution.py:164
  15.4 3.3 %enc_attend.3 = (bf16[128,768]{1,0:T(8,128)(2,1)}, bf16[128,768]{1,0:T(8,128)(2,1)S(1)}, bf16[128,768]{1,0:T(8,128)(2,1)S(1)}, bf16[3,128,384]{2,1,0:T(8,128)(2,...) custom-call(s32[3]{0:T(128)S(1)} %pad_add_fusion.refs_0_, ...), custom_call_target="tpu_custom_call" | custom-call | flops 199999995904 | bytes 1 | tf_op jit(solution)/shard_map/enc_attend/pallas_call | solution.py:164
  18.7 1.8 collective-permute-done.refs_3_
  20.6 2.4 enc_hidden.1
  25.2 3.6 %collective-permute-done.2.refs_4_ = bf16[128,768]{1,0:T(8,128)(2,1)S(1)} collective-permute-done((bf16[128,768]{1,0:T(8,128)(2,1)S(1)}, bf16[128,768]{1,0:T(8,128)(2,1)S(1)}, u32[]{:S(2)}, u32[]{:S(2)}) %collective-permute-start.2) | collective-permute-done | bytes 196640 | tf_op jit(solution)/shard_map/ppermute | solution.py:49
  28.8 5.0 %dec_attend.1 = (bf16[416,512]{1,0:T(8,128)(2,1)}, bf16[98,768]{1,0:T(8,128)(2,1)S(1)}, bf16[128,768]{1,0:T(8,128)(2,1)S(1)}, f32[416,512]{1,0:T(8,128)S(1)}, bf...) custom-call(s32[1]{0:T(128)} %bitcast.3.refs_0_, ...), custom_call_target="tpu_custom_call" | custom-call | flops 199999995904 | bytes 1 | tf_op jit(solution)/shard_map/dec_attend/pallas_call | solution.py:164
  37.5 4.4 %collective-permute-done.5.refs_3_ = bf16[128,768]{1,0:T(8,128)(2,1)} collective-permute-done((bf16[128,768]{1,0:T(8,128)(2,1)}, bf16[128,768]{1,0:T(8,128)(2,1)}, u32[]{:S(2)}, u32[]{:S(2)}) %collective-permute-start.5) | collective-permute-done | bytes 196640 | tf_op jit(solution)/shard_map/ppermute | solution.py:49
  42.0 2.0 enc_side_hidden.1
  44.0 6.7 %collective-permute-done.4.refs_3_ = bf16[416,512]{1,0:T(8,128)(2,1)} collective-permute-done((bf16[416,512]{1,0:T(8,128)(2,1)}, bf16[416,512]{1,0:T(8,128)(2,1)}, u32[]{:S(2)}, u32[]{:S(2)}) %collective-permute-start.4) | collective-permute-done | bytes 426016 | tf_op jit(solution)/shard_map/ppermute | solution.py:49
  50.7 5.3 %dec_hidden.1 = (bf16[416,512]{1,0:T(8,128)(2,1)}, bf16[416,512]{1,0:T(8,128)(2,1)}, f32[416,512]{1,0:T(8,128)S(1)}, bf16[416,512]{1,0:T(8,128)(2,1)S(1)}, bf16[...) custom-call(s32[1]{0:T(128)} %bitcast.3.refs_0_, ...), custom_call_target="tpu_custom_call" | custom-call | flops 199999995904 | bytes 1 | tf_op jit(solution)/shard_map/dec_hidden/pallas_call | solution.py:164
  56.0 2.0 dec_hidden_weights.1
  62.6 8.1 %collective-permute-done.6.refs_3_ = bf16[416,512]{1,0:T(8,128)(2,1)} collective-permute-done((bf16[416,512]{1,0:T(8,128)(2,1)}, bf16[416,512]{1,0:T(8,128)(2,1)}, u32[]{:S(2)}, u32[]{:S(2)}) %collective-permute-start.6) | collective-permute-done | bytes 426016 | tf_op jit(solution)/shard_map/ppermute | solution.py:49
  70.7 5.8 %dec_attend_back.1 = (bf16[416,512]{1,0:T(8,128)(2,1)}, f32[416,512]{1,0:T(8,128)S(1)}, bf16[416,512]{1,0:T(8,128)(2,1)S(1)}, bf16[3,416,256]{2,1,0:T(8,128)(2,1...) custom-call(f32[416,512]{1,0:T(8,128)S(1)} %get-tuple-element.200.refs_0_.refs_1_, ...), custom_call_target="tpu_custom_call" | custom-call | flops 199999995904 | bytes 1 | tf_op jit(solution)/shard_map/dec_attend_back/pallas_call | solution.py:164
  78.0 1.8 fold.8
  81.4 1.8 dec_head_weights.1
  83.2 4.5 %collective-permute-done.10.refs_1_ = bf16[256,512]{1,0:T(8,128)(2,1)} collective-permute-done((bf16[256,512]{1,0:T(8,128)(2,1)}, bf16[256,512]{1,0:T(8,128)(2,1)}, u32[]{:S(2)}, u32[]{:S(2)}) %collective-permute-start.10) | collective-permute-done | bytes 262176 | tf_op jit(solution)/shard_map/ppermute | solution.py:653
  87.8 1.8 add.38
  89.6 3.7 %dec_start_back.1 = (bf16[128,768]{1,0:T(8,128)(2,1)}, bf16[128,512]{1,0:T(8,128)(2,1)S(1)}, f32[208,512]{1,0:T(8,128)S(1)}, f32[4,512]{1,0:T(4,128)S(1)}, f32[8,128]{1,0:T(8,128)S(1)}) custom-call(s32[1]{0:T(128)} %bitcast.3.refs_0_, s32[2,64]{1,0:T(2,128)S(1)} %copy-done.6, f32[416,512]{1,0:T(8,128)S(1)} %get-tuple-element.194.refs_1_.refs_2_, ...), custom_call_target="tpu_custom_call" | custom-call | flops 199999995904 | bytes 1 | tf_op jit(solution)/shard_map/dec_start_back/pallas_call | solution.py:164
  93.7 2.6 %collective-permute-start.12 = (bf16[256,512]{1,0:T(8,128)(2,1)}, bf16[256,512]{1,0:T(8,128)(2,1)}, u32[]{:S(2)}, u32[]{:S(2)}) collective-permute-start(bf16[256,512]{1,0:T(8,128)(2,1)} %get-tuple-element.247.refs_0_), channel_id=1, source_target_pairs={{0,4},{1,5},{2,6},{3,7},{4,0},{5,1},{6,2},{7,3},{8,12},{9,13},{10,... | collective-permute-start | bytes 786440 | tf_op jit(solution)/shard_map/ppermute | solution.py:653
  96.3 1.7 dec_bridge_weights.1
  99.2 2.4 enc_down_weights.1
  101.8 3.3 %enc_hidden_back.1 = (bf16[256,768]{1,0:T(8,128)(2,1)}, bf16[256,1536]{1,0:T(8,128)(2,1)S(1)}, f32[8,128]{1,0:T(8,128)S(1)}) custom-call(bf16[128,768]{1,0:T(8,128)(2,1)} %get-tuple-element.230.refs_3_.refs_0_.refs_2_, bf16[128,768]{1,0:T(8,128)(2,1)} %collective-permute-done.11.refs_4_.refs_1_.refs_3_, bf16[128,1536]{1,0:T(8,128)(2,1)S(1)} %get-tuple-element.231.refs_2_, ...), custom_call_target="tpu_custom_call" | custom-call | flops 199999995904 | bytes 1 | tf_op jit(solution)/shard_map/enc_hidden_back/pallas_call | solution.py:164
  105.6 1.9 fold.9
  107.5 1.8 add.39
  112.3 2.1 fold.10
  115.5 4.3 %collective-permute-done.14.refs_2_ = bf16[256,512]{1,0:T(8,128)(2,1)} collective-permute-done((bf16[256,512]{1,0:T(8,128)(2,1)}, bf16[256,512]{1,0:T(8,128)(2,1)}, u32[]{:S(2)}, u32[]{:S(2)}) %collective-permute-start.14) | collective-permute-done | bytes 262176 | tf_op jit(solution)/shard_map/ppermute | solution.py:653
  120.8 3.6 %collective-permute-done.18.refs_1_ = bf16[192,768]{1,0:T(8,128)(2,1)} collective-permute-done((bf16[192,768]{1,0:T(8,128)(2,1)}, bf16[192,768]{1,0:T(8,128)(2,1)}, u32[]{:S(2)}, u32[]{:S(2)}) %collective-permute-start.18) | collective-permute-done | bytes 294944 | tf_op jit(solution)/shard_map/ppermute | solution.py:653
  124.5 1.9 add.40
  126.4 2.7 %collective-permute-start.24 = (bf16[192,768]{1,0:T(8,128)(2,1)}, bf16[192,768]{1,0:T(8,128)(2,1)}, u32[]{:S(2)}, u32[]{:S(2)}) collective-permute-start(bf16[192,768]{1,0:T(8,128)(2,1)} %get-tuple-element.278.refs_0_), channel_id=1, source_target_pairs={{0,4},{1,5},{2,6},{3,7},{4,0},{5,1},{6,2},{7,3},{8,12},{9,13},{10,... | collective-permute-start | bytes 884744 | tf_op jit(solution)/shard_map/ppermute | solution.py:653
  129.1 6.2 %enc_attend_back.1 = (bf16[256,768]{1,0:T(8,128)(2,1)}, f32[256,768]{1,0:T(8,128)S(1)}, bf16[256,768]{1,0:T(8,128)(2,1)S(1)}, bf16[3,256,384]{2,1,0:T(8,128)(2,1...) custom-call(f32[128,768]{1,0:T(8,128)S(1)} %copy-done.46, ...), custom_call_target="tpu_custom_call" | custom-call | flops 199999995904 | bytes 1 | tf_op jit(solution)/shard_map/enc_attend_back/pallas_call | solution.py:164
  136.6 2.2 pack.5
  138.9 1.7 enc_up_weights.1
  140.6 1.8 fold.11
  144.3 1.9 fold.12
  146.7 2.9 %enc_start_back.1 = (f32[98,1,768]{2,1,0:T(1,128)}, bf16[32,768]{1,0:T(8,128)(2,1)S(1)}, f32[8,128]{1,0:T(8,128)S(1)}) custom-call(bf16[128,768]{1,0:T(8,128)(2,1)S(1)} %copy-done.48, bf16[128,768]{1,0:T(8,128)(2,1)S(1)} %copy-done.50, bf16[256,768]{1,0:T(8,128)(2,1)} %get-tuple-element.285.refs_2_, bf16[256,768]{1,0:T(8,128)(2,1)} %collective-permute-done.25.refs_3_, ...), custom_call_target="tpu_custom_call" | custom-call | flops 199999995904 | bytes 1 | tf_op jit(solution)/shard_map/enc_start_back/pallas_call | solution.py:164
  149.5 2.0 enc_head_weights.1
  151.5 1.8 add.41
  158.0 1.8 add.42
  159.8 4.3 %collective-permute-done.27.refs_2_ = bf16[192,768]{1,0:T(8,128)(2,1)} collective-permute-done((bf16[192,768]{1,0:T(8,128)(2,1)}, bf16[192,768]{1,0:T(8,128)(2,1)}, u32[]{:S(2)}, u32[]{:S(2)}) %collective-permute-start.27) | collective-permute-done | bytes 294944 | tf_op jit(solution)/shard_map/ppermute | solution.py:653
  166.0 1.9 fold.13
  167.9 3.8 %dec_hidden_whole.1 = (f32[512,1024]{1,0:T(8,128)}, f32[1024,512]{1,0:T(8,128)}, f32[8,128]{1,0:T(8,128)S(1)}) custom-call(s32[3]{0:T(128)S(1)} %copy-done.9, bf16[2,2,256,512]{3,2,1,0:T(8,128)(2,1)} %get-tuple-element.299.refs_1_, bf16[2,2,256,512]{3,2,1,0:T(8,128)(2,1)} %collective-permute-done.31.refs_2_, f32[8,128]{1,0:T(8,128)S(1)} %get-tuple-element.303.refs_3_), custom_call_target="tpu_custom_call" | custom-call | flops 199999995904 | bytes 1 | tf_op jit(solution)/shard_map/dec_hidden_whole/pallas_call | solution.py:164
  171.7 1.7 add.43
  173.4 2.3 pack.6
  175.7 4.0 %collective-permute-done.26.refs_1_ = bf16[384,384]{1,0:T(8,128)(2,1)} collective-permute-done((bf16[384,384]{1,0:T(8,128)(2,1)}, bf16[384,384]{1,0:T(8,128)(2,1)}, u32[]{:S(2)}, u32[]{:S(2)}) %collective-permute-start.26) | collective-permute-done | bytes 294944 | tf_op jit(solution)/shard_map/ppermute | solution.py:653
  179.7 1.8 add.44
  181.5 2.1 collective-permute-start.34
  183.7 2.0 collective-permute-start.37
  185.7 11.7 %collective-permute-done.33.refs_2_ = bf16[384,384]{1,0:T(8,128)(2,1)} collective-permute-done((bf16[384,384]{1,0:T(8,128)(2,1)}, bf16[384,384]{1,0:T(8,128)(2,1)}, u32[]{:S(2)}, u32[]{:S(2)}) %collective-permute-start.33) | collective-permute-done | bytes 294944 | tf_op jit(solution)/shard_map/ppermute | solution.py:653
  197.4 2.1 collective-permute-start.35
  199.5 4.1 %enc_down_whole.1 = (f32[1536,768]{1,0:T(8,128)}, f32[8,128]{1,0:T(8,128)S(1)}) custom-call(s32[3]{0:T(128)S(1)} %copy-done.9, bf16[2,2,192,768]{3,2,1,0:T(8,128)(2,1)} %get-tuple-element.311.refs_1_, bf16[2,2,192,768]{3,2,1,0:T(8,128)(2,1)} %collective-permute-done.38.refs_2_, f32[8,128]{1,0:T(8,128)S(1)} %get-tuple-element.312.refs_3_), custom_call_target="tpu_custom_call" | custom-call | flops 199999995904 | bytes 1 | tf_op jit(solution)/shard_map/enc_down_whole/pallas_call | solution.py:164
  203.7 1.8 add.45
  205.5 1.8 add.46
  209.5 2.8 %collective-permute-start.43 = (bf16[208,768]{1,0:T(8,128)(2,1)}, bf16[208,768]{1,0:T(8,128)(2,1)}, u32[]{:S(2)}, u32[]{:S(2)}) collective-permute-start(bf16[208,768]{1,0:T(8,128)(2,1)} %get-tuple-element.319.refs_0_), channel_id=1, source_target_pairs={{0,4},{1,5},{2,6},{3,7},{4,0},{5,1},{6,2},{7,3},{8,12},{9,13},{10,... | collective-permute-start | bytes 958472 | tf_op jit(solution)/shard_map/ppermute | solution.py:653
  212.8 9.0 %collective-permute-done.40.refs_2_ = bf16[256,512]{1,0:T(8,128)(2,1)} collective-permute-done((bf16[256,512]{1,0:T(8,128)(2,1)}, bf16[256,512]{1,0:T(8,128)(2,1)}, u32[]{:S(2)}, u32[]{:S(2)}) %collective-permute-start.40) | collective-permute-done | bytes 262176 | tf_op jit(solution)/shard_map/ppermute | solution.py:653
  222.6 3.0 %enc_up_whole.1 = (f32[768,1536]{1,0:T(8,128)}, f32[8,128]{1,0:T(8,128)S(1)}) custom-call(s32[3]{0:T(128)S(1)} %copy-done.9, bf16[2,2,384,384]{3,2,1,0:T(8,128)(2,1)S(1)} %get-tuple-element.320.refs_1_, bf16[2,2,384,384]{3,2,1,0:T(8,128)(2,1)S(1)} %collective-permute-done.44.refs_2_, f32[8,128]{1,0:T(8,128)S(1)} %get-tuple-element.321.refs_3_), custom_call_target="tpu_custom_call" | custom-call | flops 199999995904 | bytes 1 | tf_op jit(solution)/shard_map/enc_up_whole/pallas_call | solution.py:164
  227.1 1.9 add.47
  230.4 2.3 pack.8
  232.7 3.0 %dec_out.1 = (bf16[392,512]{1,0:T(8,128)(2,1)}, f32[8,128]{1,0:T(8,128)S(1)}) custom-call(s32[1]{0:T(128)} %bitcast.3.refs_0_, f32[416,512]{1,0:T(8,128)S(1)} %copy-done.42, bf16[416,512]{1,0:T(8,128)(2,1)} %get-tuple-element.317.refs_2_, bf16[416,512]{1,0:T(8,128)(2,1)} %collective-permute-done.39.refs_3_, bf16[8,512]{1,0:T(8,128)(2,1)S(1)} %copy-done.38, ...), custom_call_target="tpu_custom_call" | custom-call | flops 199999995904 | bytes 1 | tf_op jit(solution)/shard_map/dec_out/pallas_call | solution.py:164
  235.8 3.3 %collective-permute-done.45.refs_2_ = bf16[208,768]{1,0:T(8,128)(2,1)} collective-permute-done((bf16[208,768]{1,0:T(8,128)(2,1)}, bf16[208,768]{1,0:T(8,128)(2,1)}, u32[]{:S(2)}, u32[]{:S(2)}) %collective-permute-start.45) | collective-permute-done | bytes 319520 | tf_op jit(solution)/shard_map/ppermute | solution.py:653
  239.7 3.6 %dec_rest_whole.1 = (f32[3,512,256]{2,1,0:T(8,128)}, f32[256,512]{1,0:T(8,128)}, f32[768,512]{1,0:T(8,128)}, f32[196,512]{1,0:T(8,128)}, f32[8,512]{1,0:T(8,128)...) custom-call(s32[3]{0:T(128)S(1)} %copy-done.9, bf16[2,2,256,512]{3,2,1,0:T(8,128)(2,1)} %get-tuple-element.328.refs_1_, ...), custom_call_target="tpu_custom_call" | custom-call | flops 199999995904 | bytes 1 | tf_op jit(solution)/shard_map/dec_rest_whole/pallas_call | solution.py:164
  243.3 3.6 %collective-permute-done.47.refs_4_ = bf16[208,768]{1,0:T(8,128)(2,1)} collective-permute-done((bf16[208,768]{1,0:T(8,128)(2,1)}, bf16[208,768]{1,0:T(8,128)(2,1)}, u32[]{:S(2)}, u32[]{:S(2)}) %collective-permute-start.47) | collective-permute-done | bytes 319520 | tf_op jit(solution)/shard_map/ppermute | solution.py:653
  248.3 3.0 %collective-permute-done.49.refs_2_ = bf16[2,2,208,768]{3,2,1,0:T(8,128)(2,1)S(1)} collective-permute-done((bf16[2,2,208,768]{3,2,1,0:T(8,128)(2,1)S(1)}, bf16[2,2,208,768]{3,2,1,0:T(8,128)(2,1)S(1)}, u32[]{:S(2)}, u32[]{:S(2)}) %collective-permute-start.49) | collective-permute-done | bytes 1277984 | tf_op jit(solution)/shard_map/ppermute | solution.py:49
  251.3 2.8 %enc_head_whole.1 = (f32[3,768,384]{2,1,0:T(8,128)}, f32[384,768]{1,0:T(8,128)}, f32[6,768]{1,0:T(8,128)}, f32[1,1536]{1,0:T(1,128)S(1)}, f32[2,384]{1,0:T(2,128)}, /*index=5*/f32[8,128]{1,0:T(8,128)}) custom-call(s32[3]{0:T(128)S(1)} %copy-done.9, bf16[2,2,208,768]{3,2,1,0:T(8,128)(2,1)S(1)} %get-tuple-element.331.refs_1_, ...), custom_call_target="tpu_custom_call" | custom-call | flops 199999995904 | bytes 1 | tf_op jit(solution)/shard_map/enc_head_whole/pallas_call | solution.py:164
  (202 shorter events, 48.8 us)
Async XLA Ops:
  0.7 33.2 %copy-start = (bf16[2,392,512]{2,1,0:T(8,128)(2,1)S(1)}, bf16[2,392,512]{2,1,0:T(8,128)(2,1)}, u32[]{:S(2)}) copy-start(bf16[2,392,512]{2,1,0:T(8,128)(2,1)} %param.39) | copy-start | bytes 2408452
  2.7 12.6 %collective-permute-start.1 = (bf16[98,768]{1,0:T(8,128)(2,1)}, bf16[98,768]{1,0:T(8,128)(2,1)}, u32[]{:S(2)}, u32[]{:S(2)}) collective-permute-start(bf16[98,768]{1,0:T(8,128)(2,1)} %bitcast.19), channel_id=1, source_target_pairs={{0,1},{1,0},{2,3},{3,2},{4,5},{5,4},{6,7},{7,6},{8,9},{9,8},{10,11... | collective-permute-start | bytes 451592 | tf_op jit(solution)/shard_map/ppermute | solution.py:653
  5.8 9.6 %copy-start.7 = (s32[3]{0:T(128)}, s32[3]{0:T(128)S(1)}, u32[]{:S(2)}) copy-start(s32[3]{0:T(128)S(1)} %pad_add_fusion.refs_0_) | copy-start | bytes 40
  13.8 6.7 %collective-permute-start = (bf16[128,768]{1,0:T(8,128)(2,1)}, bf16[128,768]{1,0:T(8,128)(2,1)}, u32[]{:S(2)}, u32[]{:S(2)}) collective-permute-start(bf16[128,768]{1,0:T(8,128)(2,1)} %get-tuple-element.185.refs_2_), channel_id=1, source_target_pairs={{0,8},{8,0},{1,9},{9,1},{2,10},{10,2},{3,11},{11,3},{4,12},{12,4},... | collective-permute-start | bytes 589832 | tf_op jit(solution)/shard_map/ppermute | solution.py:49
  18.7 23.3 %copy-start.49 = (bf16[128,768]{1,0:T(8,128)(2,1)}, bf16[128,768]{1,0:T(8,128)(2,1)S(1)}, u32[]{:S(2)}) copy-start(bf16[128,768]{1,0:T(8,128)(2,1)S(1)} %get-tuple-element.196.refs_0_.refs_1_) | copy-start | bytes 589828
  20.6 8.2 %copy-start.20 = (bf16[512,3,256]{2,0,1:T(8,128)(2,1)S(1)}, bf16[512,3,256]{2,0,1:T(8,128)(2,1)}, u32[]{:S(2)}) copy-start(bf16[512,3,256]{2,0,1:T(8,128)(2,1)} %param.33) | copy-start | bytes 2359300
  23.0 10.8 %copy-start.45 = (f32[128,768]{1,0:T(8,128)}, f32[128,768]{1,0:T(8,128)S(1)}, u32[]{:S(2)}) copy-start(f32[128,768]{1,0:T(8,128)S(1)} %get-tuple-element.188.refs_2_.refs_0_) | copy-start | bytes 1179652
  23.0 5.7 %collective-permute-start.2 = (bf16[128,768]{1,0:T(8,128)(2,1)S(1)}, bf16[128,768]{1,0:T(8,128)(2,1)S(1)}, u32[]{:S(2)}, u32[]{:S(2)}) collective-permute-start(bf16[128,768]{1,0:T(8,128)(2,1)S(1)} %get-tuple-element.189.refs_3_), channel_id=1, source_target_pairs={{0,8},{8,0},{1,9},{9,1},{2,10},{10,2},{3,11},{11,3},{4,12},{12,4},... | collective-permute-start | bytes 589832 | tf_op jit(solution)/shard_map/ppermute | solution.py:49
  25.2 8.6 %copy-start.5 = (s32[2,64]{1,0:T(2,128)}, s32[2,64]{1,0:T(2,128)S(1)}, u32[]{:S(2)}) copy-start(s32[2,64]{1,0:T(2,128)S(1)} %pad.4.refs_1_) | copy-start | bytes 1540
  33.8 2.2 collective-permute-start.3
  33.9 8.1 %collective-permute-start.5 = (bf16[128,768]{1,0:T(8,128)(2,1)}, bf16[128,768]{1,0:T(8,128)(2,1)}, u32[]{:S(2)}, u32[]{:S(2)}) collective-permute-start(bf16[128,768]{1,0:T(8,128)(2,1)} %get-tuple-element.197.refs_2_), channel_id=1, source_target_pairs={{0,8},{8,0},{1,9},{9,1},{2,10},{10,2},{3,11},{11,3},{4,12},{12,4},... | collective-permute-start | bytes 589832 | tf_op jit(solution)/shard_map/ppermute | solution.py:49
  35.4 15.2 %collective-permute-start.4 = (bf16[416,512]{1,0:T(8,128)(2,1)}, bf16[416,512]{1,0:T(8,128)(2,1)}, u32[]{:S(2)}, u32[]{:S(2)}) collective-permute-start(bf16[416,512]{1,0:T(8,128)(2,1)} %get-tuple-element.195.refs_2_), channel_id=1, source_target_pairs={{0,8},{8,0},{1,9},{9,1},{2,10},{10,2},{3,11},{11,3},{4,12},{12,4},... | collective-permute-start | bytes 1277960 | tf_op jit(solution)/shard_map/ppermute | solution.py:49
  42.0 8.7 %copy-start.18 = (bf16[512,1024]{1,0:T(8,128)(2,1)S(1)}, bf16[512,1024]{1,0:T(8,128)(2,1)}, u32[]{:S(2)}) copy-start(bf16[512,1024]{1,0:T(8,128)(2,1)} %refs_5_.9) | copy-start | bytes 3145732
  42.0 8.7 %copy-start.19 = (bf16[1024,512]{1,0:T(8,128)(2,1)S(1)}, bf16[1024,512]{1,0:T(8,128)(2,1)}, u32[]{:S(2)}) copy-start(bf16[1024,512]{1,0:T(8,128)(2,1)} %refs_7_.4) | copy-start | bytes 3145732
  42.0 8.7 %copy-start.36 = (bf16[8,512]{1,0:T(8,128)(2,1)S(1)}, bf16[8,512]{1,0:T(8,128)(2,1)}, u32[]{:S(2)}) copy-start(bf16[8,512]{1,0:T(8,128)(2,1)} %refs_4_.17) | copy-start | bytes 24580
  56.0 14.7 %copy-start.41 = (f32[416,512]{1,0:T(8,128)}, f32[416,512]{1,0:T(8,128)S(1)}, u32[]{:S(2)}) copy-start(f32[416,512]{1,0:T(8,128)S(1)} %get-tuple-element.200.refs_0_.refs_1_) | copy-start | bytes 2555908
  58.0 2.7 %collective-permute-start.7 = (bf16[2,2,256,512]{3,2,1,0:T(8,128)(2,1)S(1)}, bf16[2,2,256,512]{3,2,1,0:T(8,128)(2,1)S(1)}, u32[]{:S(2)}, u32[]{:S(2)}) collective-permute-start(bf16[2,2,256,512]{3,2,1,0:T(8,128)(2,1)S(1)} %get-tuple-element.213), channel_id=1, source_target_pairs={{0,16},{16,0},{1,17},{17,1},{2,18},{18,2},{3,19},{19,3},{4,20},{20... | collective-permute-start | bytes 3145736 | tf_op jit(solution)/shard_map/ppermute | solution.py:49
  58.1 12.5 %collective-permute-start.6 = (bf16[416,512]{1,0:T(8,128)(2,1)}, bf16[416,512]{1,0:T(8,128)(2,1)}, u32[]{:S(2)}, u32[]{:S(2)}) collective-permute-start(bf16[416,512]{1,0:T(8,128)(2,1)} %get-tuple-element.205.refs_2_), channel_id=1, source_target_pairs={{0,8},{8,0},{1,9},{9,1},{2,10},{10,2},{3,11},{11,3},{4,12},{12,4},... | collective-permute-start | bytes 1277960 | tf_op jit(solution)/shard_map/ppermute | solution.py:49
  60.8 9.9 %copy-start.21 = (bf16[512,3,256]{2,0,1:T(8,128)(2,1)S(1)}, bf16[512,3,256]{2,0,1:T(8,128)(2,1)}, u32[]{:S(2)}) copy-start(bf16[512,3,256]{2,0,1:T(8,128)(2,1)} %param.33) | copy-start | bytes 2359300
  60.8 9.9 %copy-start.28 = (bf16[256,512]{1,0:T(8,128)(2,1)S(1)}, bf16[256,512]{1,0:T(8,128)(2,1)}, u32[]{:S(2)}) copy-start(bf16[256,512]{1,0:T(8,128)(2,1)} %refs_8_.3) | copy-start | bytes 786436
  60.8 9.9 %copy-start.37 = (bf16[8,512]{1,0:T(8,128)(2,1)S(1)}, bf16[8,512]{1,0:T(8,128)(2,1)}, u32[]{:S(2)}) copy-start(bf16[8,512]{1,0:T(8,128)(2,1)} %refs_4_.17) | copy-start | bytes 24580
  60.8 9.9 %copy-start.44 = (bf16[416,512]{1,0:T(8,128)(2,1)S(1)}, bf16[416,512]{1,0:T(8,128)(2,1)}, u32[]{:S(2)}) copy-start(bf16[416,512]{1,0:T(8,128)(2,1)} %copy-done.43) | copy-start | bytes 1277956
  62.2 15.8 %collective-permute-start.9 = (bf16[2,256,512]{2,1,0:T(8,128)(2,1)}, bf16[2,256,512]{2,1,0:T(8,128)(2,1)}, u32[]{:S(2)}, u32[]{:S(2)}) collective-permute-start(bf16[2,256,512]{2,1,0:T(8,128)(2,1)} %get-tuple-element.219), channel_id=1, source_target_pairs={{0,1},{1,0},{2,3},{3,2},{4,5},{5,4},{6,7},{7,6},{8,9},{9,8},{10,11... | collective-permute-start | bytes 1572872 | tf_op jit(solution)/shard_map/ppermute | solution.py:653
  76.5 13.0 %collective-permute-start.8 = (bf16[416,512]{1,0:T(8,128)(2,1)}, bf16[416,512]{1,0:T(8,128)(2,1)}, u32[]{:S(2)}, u32[]{:S(2)}) collective-permute-start(bf16[416,512]{1,0:T(8,128)(2,1)} %get-tuple-element.216.refs_3_), channel_id=1, source_target_pairs={{0,8},{8,0},{1,9},{9,1},{2,10},{10,2},{3,11},{11,3},{4,12},{12,4},... | collective-permute-start | bytes 1277960 | tf_op jit(solution)/shard_map/ppermute | solution.py:49
  79.8 7.9 %collective-permute-start.10 = (bf16[256,512]{1,0:T(8,128)(2,1)}, bf16[256,512]{1,0:T(8,128)(2,1)}, u32[]{:S(2)}, u32[]{:S(2)}) collective-permute-start(bf16[256,512]{1,0:T(8,128)(2,1)} %get-tuple-element.222), channel_id=1, source_target_pairs={{0,2},{1,3},{2,0},{3,1},{4,6},{5,7},{6,4},{7,5},{8,10},{9,11},{10,... | collective-permute-start | bytes 786440 | tf_op jit(solution)/shard_map/ppermute | solution.py:653
  83.2 28.4 %collective-permute-start.19 = (bf16[2,2,128,512]{3,2,1,0:T(8,128)(2,1)}, bf16[2,2,128,512]{3,2,1,0:T(8,128)(2,1)}, u32[]{:S(2)}, u32[]{:S(2)}) collective-permute-start(bf16[2,2,128,512]{3,2,1,0:T(8,128)(2,1)} %get-tuple-element.262), channel_id=1, source_target_pairs={{0,16},{16,0},{1,17},{17,1},{2,18},{18,2},{3,19},{19,3},{4,20},{20... | collective-permute-start | bytes 1572872 | tf_op jit(solution)/shard_map/ppermute | solution.py:49
  93.2 6.0 %collective-permute-start.11 = (bf16[128,768]{1,0:T(8,128)(2,1)}, bf16[128,768]{1,0:T(8,128)(2,1)}, u32[]{:S(2)}, u32[]{:S(2)}) collective-permute-start(bf16[128,768]{1,0:T(8,128)(2,1)} %get-tuple-element.230.refs_3_.refs_0_.refs_2_), channel_id=1, source_target_pairs={{0,1},{1,0},{2,3},{3,2},{4,5},{5,4},{6,7},{7,6},{8,9},{9,8},{10,11... | collective-permute-start | bytes 589832 | tf_op jit(solution)/shard_map/ppermute | solution.py:653
  93.7 13.8 %collective-permute-start.12 = (bf16[256,512]{1,0:T(8,128)(2,1)}, bf16[256,512]{1,0:T(8,128)(2,1)}, u32[]{:S(2)}, u32[]{:S(2)}) collective-permute-start(bf16[256,512]{1,0:T(8,128)(2,1)} %get-tuple-element.247.refs_0_), channel_id=1, source_target_pairs={{0,4},{1,5},{2,6},{3,7},{4,0},{5,1},{6,2},{7,3},{8,12},{9,13},{10,... | collective-permute-start | bytes 786440 | tf_op jit(solution)/shard_map/ppermute | solution.py:653
  98.1 14.3 %collective-permute-start.20 = (bf16[2,2,128,512]{3,2,1,0:T(8,128)(2,1)}, bf16[2,2,128,512]{3,2,1,0:T(8,128)(2,1)}, u32[]{:S(2)}, u32[]{:S(2)}) collective-permute-start(bf16[2,2,128,512]{3,2,1,0:T(8,128)(2,1)} %get-tuple-element.264), channel_id=1, source_target_pairs={{0,16},{16,0},{1,17},{17,1},{2,18},{18,2},{3,19},{19,3},{4,20},{20... | collective-permute-start | bytes 1572872 | tf_op jit(solution)/shard_map/ppermute | solution.py:49
  101.6 4.0 %collective-permute-start.13 = (bf16[2,192,768]{2,1,0:T(8,128)(2,1)}, bf16[2,192,768]{2,1,0:T(8,128)(2,1)}, u32[]{:S(2)}, u32[]{:S(2)}) collective-permute-start(bf16[2,192,768]{2,1,0:T(8,128)(2,1)} %get-tuple-element.249), channel_id=1, source_target_pairs={{0,16},{16,0},{1,17},{17,1},{2,18},{18,2},{3,19},{19,3},{4,20},{20... | collective-permute-start | bytes 1769480 | tf_op jit(solution)/shard_map/ppermute | solution.py:49
  105.1 24.0 %collective-permute-start.17 = (bf16[256,768]{1,0:T(8,128)(2,1)}, bf16[256,768]{1,0:T(8,128)(2,1)}, u32[]{:S(2)}, u32[]{:S(2)}) collective-permute-start(bf16[256,768]{1,0:T(8,128)(2,1)} %get-tuple-element.254.refs_4_), channel_id=1, source_target_pairs={{0,8},{8,0},{1,9},{9,1},{2,10},{10,2},{3,11},{11,3},{4,12},{12,4},... | collective-permute-start | bytes 1179656 | tf_op jit(solution)/shard_map/ppermute | solution.py:49
  109.3 27.3 %collective-permute-start.15 = (bf16[256,512]{1,0:T(8,128)(2,1)}, bf16[256,512]{1,0:T(8,128)(2,1)}, u32[]{:S(2)}, u32[]{:S(2)}) collective-permute-start(bf16[256,512]{1,0:T(8,128)(2,1)} %get-tuple-element.252.refs_1_), channel_id=1, source_target_pairs={{0,1},{1,0},{2,3},{3,2},{4,5},{5,4},{6,7},{7,6},{8,9},{9,8},{10,11... | collective-permute-start | bytes 786440 | tf_op jit(solution)/shard_map/ppermute | solution.py:653
  110.3 9.6 %collective-permute-start.14 = (bf16[256,512]{1,0:T(8,128)(2,1)}, bf16[256,512]{1,0:T(8,128)(2,1)}, u32[]{:S(2)}, u32[]{:S(2)}) collective-permute-start(bf16[256,512]{1,0:T(8,128)(2,1)} %get-tuple-element.252.refs_1_), channel_id=1, source_target_pairs={{0,2},{1,3},{2,0},{3,1},{4,6},{5,7},{6,4},{7,5},{8,10},{9,11},{10,... | collective-permute-start | bytes 786440 | tf_op jit(solution)/shard_map/ppermute | solution.py:653
  111.6 12.9 %collective-permute-start.18 = (bf16[192,768]{1,0:T(8,128)(2,1)}, bf16[192,768]{1,0:T(8,128)(2,1)}, u32[]{:S(2)}, u32[]{:S(2)}) collective-permute-start(bf16[192,768]{1,0:T(8,128)(2,1)} %get-tuple-element.260), channel_id=1, source_target_pairs={{0,2},{1,3},{2,0},{3,1},{4,6},{5,7},{6,4},{7,5},{8,10},{9,11},{10,... | collective-permute-start | bytes 884744 | tf_op jit(solution)/shard_map/ppermute | solution.py:653
  114.4 26.2 %collective-permute-start.22 = (bf16[2,256,512]{2,1,0:T(8,128)(2,1)}, bf16[2,256,512]{2,1,0:T(8,128)(2,1)}, u32[]{:S(2)}, u32[]{:S(2)}) collective-permute-start(bf16[2,256,512]{2,1,0:T(8,128)(2,1)} %get-tuple-element.273), channel_id=1, source_target_pairs={{0,1},{1,0},{2,3},{3,2},{4,5},{5,4},{6,7},{7,6},{8,9},{9,8},{10,11... | collective-permute-start | bytes 1572872 | tf_op jit(solution)/shard_map/ppermute | solution.py:653
  119.8 16.8 %collective-permute-start.16 = (bf16[256,512]{1,0:T(8,128)(2,1)}, bf16[256,512]{1,0:T(8,128)(2,1)}, u32[]{:S(2)}, u32[]{:S(2)}) collective-permute-start(bf16[256,512]{1,0:T(8,128)(2,1)} %collective-permute-done.14.refs_2_), channel_id=1, source_target_pairs={{0,1},{1,0},{2,3},{3,2},{4,5},{5,4},{6,7},{7,6},{8,9},{9,8},{10,11... | collective-permute-start | bytes 786440 | tf_op jit(solution)/shard_map/ppermute | solution.py:653
  126.4 25.2 %collective-permute-start.24 = (bf16[192,768]{1,0:T(8,128)(2,1)}, bf16[192,768]{1,0:T(8,128)(2,1)}, u32[]{:S(2)}, u32[]{:S(2)}) collective-permute-start(bf16[192,768]{1,0:T(8,128)(2,1)} %get-tuple-element.278.refs_0_), channel_id=1, source_target_pairs={{0,4},{1,5},{2,6},{3,7},{4,0},{5,1},{6,2},{7,3},{8,12},{9,13},{10,... | collective-permute-start | bytes 884744 | tf_op jit(solution)/shard_map/ppermute | solution.py:653
  135.3 11.4 %collective-permute-start.25 = (bf16[256,768]{1,0:T(8,128)(2,1)}, bf16[256,768]{1,0:T(8,128)(2,1)}, u32[]{:S(2)}, u32[]{:S(2)}) collective-permute-start(bf16[256,768]{1,0:T(8,128)(2,1)} %get-tuple-element.285.refs_2_), channel_id=1, source_target_pairs={{0,8},{8,0},{1,9},{9,1},{2,10},{10,2},{3,11},{11,3},{4,12},{12,4},... | collective-permute-start | bytes 1179656 | tf_op jit(solution)/shard_map/ppermute | solution.py:49
  140.6 3.6 %collective-permute-start.21 = (bf16[2,384,384]{2,1,0:T(8,128)(2,1)}, bf16[2,384,384]{2,1,0:T(8,128)(2,1)}, u32[]{:S(2)}, u32[]{:S(2)}) collective-permute-start(bf16[2,384,384]{2,1,0:T(8,128)(2,1)} %get-tuple-element.271), channel_id=1, source_target_pairs={{0,16},{16,0},{1,17},{17,1},{2,18},{18,2},{3,19},{19,3},{4,20},{20... | collective-permute-start | bytes 1769480 | tf_op jit(solution)/shard_map/ppermute | solution.py:49
  142.5 29.2 %collective-permute-start.30 = (bf16[256,512]{1,0:T(8,128)(2,1)}, bf16[256,512]{1,0:T(8,128)(2,1)}, u32[]{:S(2)}, u32[]{:S(2)}) collective-permute-start(bf16[256,512]{1,0:T(8,128)(2,1)} %get-tuple-element.298), channel_id=1, source_target_pairs={{0,2},{1,3},{2,0},{3,1},{4,6},{5,7},{6,4},{7,5},{8,10},{9,11},{10,... | collective-permute-start | bytes 786440 | tf_op jit(solution)/shard_map/ppermute | solution.py:653
  144.0 23.9 %collective-permute-start.31 = (bf16[2,2,256,512]{3,2,1,0:T(8,128)(2,1)}, bf16[2,2,256,512]{3,2,1,0:T(8,128)(2,1)}, u32[]{:S(2)}, u32[]{:S(2)}) collective-permute-start(bf16[2,2,256,512]{3,2,1,0:T(8,128)(2,1)} %get-tuple-element.299.refs_1_), channel_id=1, source_target_pairs={{0,16},{16,0},{1,17},{17,1},{2,18},{18,2},{3,19},{19,3},{4,20},{20... | collective-permute-start | bytes 3145736 | tf_op jit(solution)/shard_map/ppermute | solution.py:49
  146.2 11.8 %collective-permute-start.23 = (bf16[384,384]{1,0:T(8,128)(2,1)}, bf16[384,384]{1,0:T(8,128)(2,1)}, u32[]{:S(2)}, u32[]{:S(2)}) collective-permute-start(bf16[384,384]{1,0:T(8,128)(2,1)} %get-tuple-element.277), channel_id=1, source_target_pairs={{0,2},{1,3},{2,0},{3,1},{4,6},{5,7},{6,4},{7,5},{8,10},{9,11},{10,... | collective-permute-start | bytes 884744 | tf_op jit(solution)/shard_map/ppermute | solution.py:653
  153.4 20.0 %collective-permute-start.28 = (bf16[192,768]{1,0:T(8,128)(2,1)}, bf16[192,768]{1,0:T(8,128)(2,1)}, u32[]{:S(2)}, u32[]{:S(2)}) collective-permute-start(bf16[192,768]{1,0:T(8,128)(2,1)} %get-tuple-element.296.refs_1_), channel_id=1, source_target_pairs={{0,1},{1,0},{2,3},{3,2},{4,5},{5,4},{6,7},{7,6},{8,9},{9,8},{10,11... | collective-permute-start | bytes 884744 | tf_op jit(solution)/shard_map/ppermute | solution.py:653
  154.9 9.2 %collective-permute-start.27 = (bf16[192,768]{1,0:T(8,128)(2,1)}, bf16[192,768]{1,0:T(8,128)(2,1)}, u32[]{:S(2)}, u32[]{:S(2)}) collective-permute-start(bf16[192,768]{1,0:T(8,128)(2,1)} %get-tuple-element.296.refs_1_), channel_id=1, source_target_pairs={{0,2},{1,3},{2,0},{3,1},{4,6},{5,7},{6,4},{7,5},{8,10},{9,11},{10,... | collective-permute-start | bytes 884744 | tf_op jit(solution)/shard_map/ppermute | solution.py:653
  158.0 6.8 %collective-permute-start.32 = (bf16[2,208,768]{2,1,0:T(8,128)(2,1)}, bf16[2,208,768]{2,1,0:T(8,128)(2,1)}, u32[]{:S(2)}, u32[]{:S(2)}) collective-permute-start(bf16[2,208,768]{2,1,0:T(8,128)(2,1)} %get-tuple-element.301), channel_id=1, source_target_pairs={{0,16},{16,0},{1,17},{17,1},{2,18},{18,2},{3,19},{19,3},{4,20},{20... | collective-permute-start | bytes 1916936 | tf_op jit(solution)/shard_map/ppermute | solution.py:49
  164.1 15.6 %collective-permute-start.26 = (bf16[384,384]{1,0:T(8,128)(2,1)}, bf16[384,384]{1,0:T(8,128)(2,1)}, u32[]{:S(2)}, u32[]{:S(2)}) collective-permute-start(bf16[384,384]{1,0:T(8,128)(2,1)} %get-tuple-element.295.refs_0_), channel_id=1, source_target_pairs={{0,4},{1,5},{2,6},{3,7},{4,0},{5,1},{6,2},{7,3},{8,12},{9,13},{10,... | collective-permute-start | bytes 884744 | tf_op jit(solution)/shard_map/ppermute | solution.py:653
  164.8 8.6 %collective-permute-start.29 = (bf16[192,768]{1,0:T(8,128)(2,1)}, bf16[192,768]{1,0:T(8,128)(2,1)}, u32[]{:S(2)}, u32[]{:S(2)}) collective-permute-start(bf16[192,768]{1,0:T(8,128)(2,1)} %collective-permute-done.27.refs_2_), channel_id=1, source_target_pairs={{0,1},{1,0},{2,3},{3,2},{4,5},{5,4},{6,7},{7,6},{8,9},{9,8},{10,11... | collective-permute-start | bytes 884744 | tf_op jit(solution)/shard_map/ppermute | solution.py:653
  175.7 23.8 %collective-permute-start.38 = (bf16[2,2,192,768]{3,2,1,0:T(8,128)(2,1)}, bf16[2,2,192,768]{3,2,1,0:T(8,128)(2,1)}, u32[]{:S(2)}, u32[]{:S(2)}) collective-permute-start(bf16[2,2,192,768]{3,2,1,0:T(8,128)(2,1)} %get-tuple-element.311.refs_1_), channel_id=1, source_target_pairs={{0,16},{16,0},{1,17},{17,1},{2,18},{18,2},{3,19},{19,3},{4,20},{20... | collective-permute-start | bytes 3538952 | tf_op jit(solution)/shard_map/ppermute | solution.py:49
  181.5 15.9 %collective-permute-start.33 = (bf16[384,384]{1,0:T(8,128)(2,1)}, bf16[384,384]{1,0:T(8,128)(2,1)}, u32[]{:S(2)}, u32[]{:S(2)}) collective-permute-start(bf16[384,384]{1,0:T(8,128)(2,1)} %get-tuple-element.307.refs_1_), channel_id=1, source_target_pairs={{0,2},{1,3},{2,0},{3,1},{4,6},{5,7},{6,4},{7,5},{8,10},{9,11},{10,... | collective-permute-start | bytes 884744 | tf_op jit(solution)/shard_map/ppermute | solution.py:653
  181.5 25.7 %collective-permute-start.34 = (bf16[384,384]{1,0:T(8,128)(2,1)}, bf16[384,384]{1,0:T(8,128)(2,1)}, u32[]{:S(2)}, u32[]{:S(2)}) collective-permute-start(bf16[384,384]{1,0:T(8,128)(2,1)} %get-tuple-element.307.refs_1_), channel_id=1, source_target_pairs={{0,1},{1,0},{2,3},{3,2},{4,5},{5,4},{6,7},{7,6},{8,9},{9,8},{10,11... | collective-permute-start | bytes 884744 | tf_op jit(solution)/shard_map/ppermute | solution.py:653
  183.7 20.0 %collective-permute-start.37 = (bf16[208,768]{1,0:T(8,128)(2,1)}, bf16[208,768]{1,0:T(8,128)(2,1)}, u32[]{:S(2)}, u32[]{:S(2)}) collective-permute-start(bf16[208,768]{1,0:T(8,128)(2,1)} %get-tuple-element.310), channel_id=1, source_target_pairs={{0,2},{1,3},{2,0},{3,1},{4,6},{5,7},{6,4},{7,5},{8,10},{9,11},{10,... | collective-permute-start | bytes 958472 | tf_op jit(solution)/shard_map/ppermute | solution.py:653
  185.7 19.8 %collective-permute-start.36 = (bf16[256,512]{1,0:T(8,128)(2,1)}, bf16[256,512]{1,0:T(8,128)(2,1)}, u32[]{:S(2)}, u32[]{:S(2)}) collective-permute-start(bf16[256,512]{1,0:T(8,128)(2,1)} %get-tuple-element.308.refs_0_), channel_id=1, source_target_pairs={{0,4},{1,5},{2,6},{3,7},{4,0},{5,1},{6,2},{7,3},{8,12},{9,13},{10,... | collective-permute-start | bytes 786440 | tf_op jit(solution)/shard_map/ppermute | solution.py:653
  197.4 9.8 %collective-permute-start.35 = (bf16[384,384]{1,0:T(8,128)(2,1)}, bf16[384,384]{1,0:T(8,128)(2,1)}, u32[]{:S(2)}, u32[]{:S(2)}) collective-permute-start(bf16[384,384]{1,0:T(8,128)(2,1)} %collective-permute-done.33.refs_2_), channel_id=1, source_target_pairs={{0,1},{1,0},{2,3},{3,2},{4,5},{5,4},{6,7},{7,6},{8,9},{9,8},{10,11... | collective-permute-start | bytes 884744 | tf_op jit(solution)/shard_map/ppermute | solution.py:653
  208.6 14.0 %collective-permute-start.44 = (bf16[2,2,384,384]{3,2,1,0:T(8,128)(2,1)S(1)}, bf16[2,2,384,384]{3,2,1,0:T(8,128)(2,1)S(1)}, u32[]{:S(2)}, u32[]{:S(2)}) collective-permute-start(bf16[2,2,384,384]{3,2,1,0:T(8,128)(2,1)S(1)} %get-tuple-element.320.refs_1_), channel_id=1, source_target_pairs={{0,16},{16,0},{1,17},{17,1},{2,18},{18,2},{3,19},{19,3},{4,20},{20... | collective-permute-start | bytes 3538952 | tf_op jit(solution)/shard_map/ppermute | solution.py:49
  208.7 13.2 %collective-permute-start.40 = (bf16[256,512]{1,0:T(8,128)(2,1)}, bf16[256,512]{1,0:T(8,128)(2,1)}, u32[]{:S(2)}, u32[]{:S(2)}) collective-permute-start(bf16[256,512]{1,0:T(8,128)(2,1)} %get-tuple-element.318.refs_1_), channel_id=1, source_target_pairs={{0,2},{1,3},{2,0},{3,1},{4,6},{5,7},{6,4},{7,5},{8,10},{9,11},{10,... | collective-permute-start | bytes 786440 | tf_op jit(solution)/shard_map/ppermute | solution.py:653
  208.8 21.6 %collective-permute-start.41 = (bf16[256,512]{1,0:T(8,128)(2,1)}, bf16[256,512]{1,0:T(8,128)(2,1)}, u32[]{:S(2)}, u32[]{:S(2)}) collective-permute-start(bf16[256,512]{1,0:T(8,128)(2,1)} %get-tuple-element.318.refs_1_), channel_id=1, source_target_pairs={{0,1},{1,0},{2,3},{3,2},{4,5},{5,4},{6,7},{7,6},{8,9},{9,8},{10,11... | collective-permute-start | bytes 786440 | tf_op jit(solution)/shard_map/ppermute | solution.py:653
  209.5 17.6 %collective-permute-start.43 = (bf16[208,768]{1,0:T(8,128)(2,1)}, bf16[208,768]{1,0:T(8,128)(2,1)}, u32[]{:S(2)}, u32[]{:S(2)}) collective-permute-start(bf16[208,768]{1,0:T(8,128)(2,1)} %get-tuple-element.319.refs_0_), channel_id=1, source_target_pairs={{0,4},{1,5},{2,6},{3,7},{4,0},{5,1},{6,2},{7,3},{8,12},{9,13},{10,... | collective-permute-start | bytes 958472 | tf_op jit(solution)/shard_map/ppermute | solution.py:653
  212.3 20.5 %collective-permute-start.39 = (bf16[416,512]{1,0:T(8,128)(2,1)}, bf16[416,512]{1,0:T(8,128)(2,1)}, u32[]{:S(2)}, u32[]{:S(2)}) collective-permute-start(bf16[416,512]{1,0:T(8,128)(2,1)} %get-tuple-element.317.refs_2_), channel_id=1, source_target_pairs={{0,8},{8,0},{1,9},{9,1},{2,10},{10,2},{3,11},{11,3},{4,12},{12,4},... | collective-permute-start | bytes 1277960 | tf_op jit(solution)/shard_map/ppermute | solution.py:49
  221.9 8.5 %collective-permute-start.42 = (bf16[256,512]{1,0:T(8,128)(2,1)}, bf16[256,512]{1,0:T(8,128)(2,1)}, u32[]{:S(2)}, u32[]{:S(2)}) collective-permute-start(bf16[256,512]{1,0:T(8,128)(2,1)} %collective-permute-done.40.refs_2_), channel_id=1, source_target_pairs={{0,1},{1,0},{2,3},{3,2},{4,5},{5,4},{6,7},{7,6},{8,9},{9,8},{10,11... | collective-permute-start | bytes 786440 | tf_op jit(solution)/shard_map/ppermute | solution.py:653
  229.0 14.3 %collective-permute-start.46 = (bf16[208,768]{1,0:T(8,128)(2,1)}, bf16[208,768]{1,0:T(8,128)(2,1)}, u32[]{:S(2)}, u32[]{:S(2)}) collective-permute-start(bf16[208,768]{1,0:T(8,128)(2,1)} %get-tuple-element.327.refs_1_), channel_id=1, source_target_pairs={{0,1},{1,0},{2,3},{3,2},{4,5},{5,4},{6,7},{7,6},{8,9},{9,8},{10,11... | collective-permute-start | bytes 958472 | tf_op jit(solution)/shard_map/ppermute | solution.py:653
  230.4 8.7 %collective-permute-start.45 = (bf16[208,768]{1,0:T(8,128)(2,1)}, bf16[208,768]{1,0:T(8,128)(2,1)}, u32[]{:S(2)}, u32[]{:S(2)}) collective-permute-start(bf16[208,768]{1,0:T(8,128)(2,1)} %get-tuple-element.327.refs_1_), channel_id=1, source_target_pairs={{0,2},{1,3},{2,0},{3,1},{4,6},{5,7},{6,4},{7,5},{8,10},{9,11},{10,... | collective-permute-start | bytes 958472 | tf_op jit(solution)/shard_map/ppermute | solution.py:653
  232.7 7.0 %collective-permute-start.48 = (bf16[2,2,256,512]{3,2,1,0:T(8,128)(2,1)}, bf16[2,2,256,512]{3,2,1,0:T(8,128)(2,1)}, u32[]{:S(2)}, u32[]{:S(2)}) collective-permute-start(bf16[2,2,256,512]{3,2,1,0:T(8,128)(2,1)} %get-tuple-element.328.refs_1_), channel_id=1, source_target_pairs={{0,16},{16,0},{1,17},{17,1},{2,18},{18,2},{3,19},{19,3},{4,20},{20... | collective-permute-start | bytes 3145736 | tf_op jit(solution)/shard_map/ppermute | solution.py:49
  239.1 7.8 %collective-permute-start.47 = (bf16[208,768]{1,0:T(8,128)(2,1)}, bf16[208,768]{1,0:T(8,128)(2,1)}, u32[]{:S(2)}, u32[]{:S(2)}) collective-permute-start(bf16[208,768]{1,0:T(8,128)(2,1)} %collective-permute-done.45.refs_2_), channel_id=1, source_target_pairs={{0,1},{1,0},{2,3},{3,2},{4,5},{5,4},{6,7},{7,6},{8,9},{9,8},{10,11... | collective-permute-start | bytes 958472 | tf_op jit(solution)/shard_map/ppermute | solution.py:653
  248.2 3.1 %collective-permute-start.49 = (bf16[2,2,208,768]{3,2,1,0:T(8,128)(2,1)S(1)}, bf16[2,2,208,768]{3,2,1,0:T(8,128)(2,1)S(1)}, u32[]{:S(2)}, u32[]{:S(2)}) collective-permute-start(bf16[2,2,208,768]{3,2,1,0:T(8,128)(2,1)S(1)} %get-tuple-element.331.refs_1_), channel_id=1, source_target_pairs={{0,16},{16,0},{1,17},{17,1},{2,18},{18,2},{3,19},{19,3},{4,20},{20... | collective-permute-start | bytes 3833864 | tf_op jit(solution)/shard_map/ppermute | solution.py:49
  (41 other events, 175.7 us)
where the time goes:
time: 256 us; the launch traced here: 255 us
  Pallas kernels  117 us (46%)
  waiting for transfers between devices  81.3 us (32%)
  starting transfers between devices  46.5 us (18%)
  local copies, waits for them, and re-layouts  7.97 us (3%)
    pallas_call x46, Pallas kernels, kernel_call(): pl.pallas_call(run, out_shape=[jax.ShapeDtypeStruct(x.shape, x.dtype) for...  117 us
    ppermute x29, waiting for transfers between devices, flip(): lax.ppermute(value, 'dp', [(i, i ^ step) for i in range(lax.axis_size('dp...  52.6 us
    ppermute x29, starting transfers between devices, flip(): lax.ppermute(value, 'dp', [(i, i ^ step) for i in range(lax.axis_size('dp...  35.3 us
    ppermute x21, waiting for transfers between devices, swap(): lax.ppermute(value, axis, [(i, i ^ 1) for i in range(lax.axis_size(axis))])  28.6 us
    ppermute x21, starting transfers between devices, swap(): lax.ppermute(value, axis, [(i, i ^ 1) for i in range(lax.axis_size(axis))])  11.1 us
    unnamed x111, local copies, waits for them, and re-layouts  5.98 us
  transfers between devices with their start and end apart: 50, of which 19 were waited for; matrix products, arithmetic and copies ran while one was open for 0% of the time, Pallas kernels for 38%

commit v1 on v0

--- a/solution.py
+++ b/solution.py
@@ -149,9 +149,9 @@
     return jnp.where(row < count * padded, 1.0, 0.0)
 
 
-def kernel_call(order, kernel, outs, *arguments, scalars=0, scratch=(), name=None):
+def kernel_call(order, kernel, outs, *arguments, scalars=0, scratch=(), after=(), memory=24, name=None):
     count = len(arguments)
-    before = order[-1:]
+    before = order[-1:] + list(after)
 
     def run(*refs):
         mark = count + len(before) + len(outs)
@@ -167,12 +167,16 @@
         in_specs=specs,
         out_specs=[pl.BlockSpec(memory_space=pltpu.VMEM)] * (len(outs) + 1),
         scratch_shapes=scratch,
-        compiler_params=pltpu.CompilerParams(vmem_limit_bytes=24 * MIB),
+        compiler_params=pltpu.CompilerParams(vmem_limit_bytes=memory * MIB),
         cost_estimate=pl.CostEstimate(flops=2 * 10**11, bytes_accessed=1, transcendentals=0),
         name=name,
     )(*arguments, *before)
     order.append(results[-1])
     return results[:-1]
+
+
+def chunk(index, size):
+    return pl.ds(pl.multiple_of(index * size, LANES), size)
 
 
 def shaped(shape, dtype=LOW):
@@ -235,9 +239,19 @@
     return None if fc2_ref is None else low(matmul(hidden, fc2_ref[...])), slope
 
 
+def enc_forward_send(place_ref, first_normed_ref, mix_ref, normed_ref, hidden_ref, send_ref):
+    core, side = 1 - place_ref[0], place_ref[1]
+    width, wide = normed_ref.shape[1], hidden_ref.shape[1] // 4
+    half = width // 2
+    send_ref[:, :wide] = hidden_ref[:, chunk(2 * core + side, wide)]
+    send_ref[:, wide : wide + width] = normed_ref[...]
+    send_ref[:, wide + width : wide + width + half] = first_normed_ref[:, chunk(core, half)]
+    send_ref[:, wide + width + half :] = mix_ref[...]
+
+
 def enc_hidden_kernel(
-    x_ref, vec_ref, part_ref, other_ref, fc1_ref, bias_ref, fc2_ref,
-    part_two_ref, middle_ref, normed_ref, hidden_ref, slope_ref,
+    place_ref, x_ref, vec_ref, part_ref, other_ref, fc1_ref, bias_ref, first_normed_ref, mix_ref, fc2_ref,
+    part_two_ref, middle_ref, normed_ref, hidden_ref, slope_ref, send_ref,
 ):
     vec = full(vec_ref[...])
     middle = full(x_ref[...]) + pair(part_ref[...], other_ref[...]) + vec[2:3]
@@ -246,16 +260,18 @@
         middle, vec[3:4], vec[4:5], fc1_ref, bias_ref, fc2_ref, normed_ref, hidden_ref, slope_ref
     )
     part_two_ref[...] = part
+    enc_forward_send(place_ref, first_normed_ref, mix_ref, normed_ref, hidden_ref, send_ref)
 
 
 def enc_side_hidden_kernel(
-    x_ref, vec_ref, part_ref, other_ref, fc1_ref, bias_ref,
-    middle_ref, normed_ref, hidden_ref, slope_ref,
+    place_ref, x_ref, vec_ref, part_ref, other_ref, fc1_ref, bias_ref, first_normed_ref, mix_ref,
+    middle_ref, normed_ref, hidden_ref, slope_ref, send_ref,
 ):
     vec = full(vec_ref[...])
     middle = full(x_ref[...]) + pair(part_ref[...], other_ref[...]) + vec[2:3]
     middle_ref[...] = middle
     mlp_forward(middle, vec[3:4], vec[4:5], fc1_ref, bias_ref, None, normed_ref, hidden_ref, slope_ref)
+    enc_forward_send(place_ref, first_normed_ref, mix_ref, normed_ref, hidden_ref, send_ref)
 
 
 def both_cores_kernel(place_ref, own_ref, over_ref, both_ref):
@@ -316,9 +332,9 @@
 
 
 def dec_hidden_kernel(
-    images, count_ref, starting_ref, part_ref, other_ref, vec_ref, fc1_ref, bias_ref, fc2_ref, cot_ref,
+    images, count_ref, place_ref, starting_ref, part_ref, other_ref, vec_ref, fc1_ref, bias_ref, fc2_ref, cot_ref,
     part_back_ref, part_two_ref, middle_ref, normed_ref, hidden_ref, out_low_ref, up_ref,
-    up_sum_ref, out_sum_ref,
+    up_sum_ref, out_sum_ref, send_ref,
 ):
     vec = full(vec_ref[...])
     middle = starting_ref[...] + pair(part_ref[...], other_ref[...]) + vec[4:5]
@@ -335,6 +351,13 @@
     part_back_ref[...] = low(right_product(up_grad, fc1_ref[...]))
     up_sum_ref[...] = column_sum(up_grad)
     out_sum_ref[...] = column_sum(out_low)
+    core = 1 - place_ref[0]
+    width, wide = out_low.shape[1], up_grad.shape[1]
+    half = width // 2
+    send_ref[:, : wide // 2] = hidden_ref[:, chunk(core, wide // 2)]
+    send_ref[:, wide // 2 : wide // 2 + half] = normed_ref[:, chunk(core, half)]
+    send_ref[:, wide // 2 + half : wide // 2 + half + wide] = up_grad
+    send_ref[:, wide // 2 + half + wide :] = out_low
 
 
 def dec_out_kernel(images, count_ref, middle_ref, part_ref, other_ref, vec_ref, out_ref):
@@ -375,9 +398,9 @@
 
 
 def dec_attend_back_kernel(
-    images, head_size, middle_ref, out_low_ref, part_in_ref, other_ref, vec_ref, proj_ref, weights_ref,
-    qkv_ref, out_w_ref,
-    part_ref, middle_grad_ref, middle_low_ref, stacked_ref, sums_ref, bias_sum_ref,
+    images, head_size, place_ref, middle_ref, out_low_ref, part_in_ref, other_ref, vec_ref, proj_ref, weights_ref,
+    qkv_ref, out_w_ref, normed_ref, mix_ref,
+    part_ref, middle_grad_ref, middle_low_ref, stacked_ref, sums_ref, bias_sum_ref, send_ref,
 ):
     vec = full(vec_ref[...])
     two_grad = pair(part_in_ref[...], other_ref[...])
@@ -389,6 +412,14 @@
     mixture_grad = low(right_product(middle_low, out_w_ref[...]))
     attention_back(0, images, PAD_D, False, head_size, mixture_grad, proj_ref, weights_ref, stacked_ref)
     part_ref[...] = normed_back(stacked_ref, qkv_ref)
+    core = 1 - place_ref[0]
+    width = mix_ref.shape[1]
+    half = middle_low.shape[1] // 2
+    for j in range(3):
+        send_ref[:, j * width : (j + 1) * width] = stacked_ref[j]
+    send_ref[:, 3 * width : 4 * width] = mix_ref[...]
+    send_ref[:, 4 * width : 4 * width + half] = normed_ref[:, chunk(core, half)]
+    send_ref[:, 4 * width + half :] = middle_low_ref[:, chunk(core, half)]
     sums_ref[0:1] = column_sum(middle_grad)
     sums_ref[1:2] = column_sum(two_grad * xhat)
     sums_ref[2:3] = column_sum(two_grad)
@@ -424,17 +455,20 @@
     enc_cot_ref[...] = low(handed * live_rows(count_ref[0], images * PAD_E, PAD_E))
 
 
-def enc_hidden_back_kernel(cot_a, cot_b, slope_a, slope_b, fc1_ref, fc2_ref, part_ref, up_ref):
+def enc_hidden_back_kernel(
+    place_ref, cot_a, cot_b, slope_a, slope_b, fc1_ref, fc2_ref, part_ref, up_ref, send_ref
+):
     slope = jnp.concatenate([slope_a[...], slope_b[...]], axis=0)
     up_grad = low(full(slope) * right_product(stacked_rows(cot_a, cot_b), fc2_ref[...]))
     up_ref[...] = up_grad
     part_ref[...] = low(right_product(up_grad, fc1_ref[...]))
+    send_ref[...] = up_ref[:, chunk(2 * (1 - place_ref[0]) + place_ref[1], send_ref.shape[1])]
 
 
 def enc_attend_back_kernel(
-    images, head_size, middle_a, middle_b, cot_a, cot_b, part_in_ref, other_ref, vec_ref, proj_a, proj_b,
+    images, head_size, place_ref, middle_a, middle_b, cot_a, cot_b, part_in_ref, other_ref, vec_ref, proj_a, proj_b,
     weights_a, weights_b, qkv_ref, out_w_ref, up_ref,
-    part_ref, middle_grad_ref, middle_low_ref, stacked_ref, sums_ref, bias_sum_ref, up_sum_ref,
+    part_ref, middle_grad_ref, middle_low_ref, stacked_ref, sums_ref, bias_sum_ref, up_sum_ref, send_ref,
 ):
     vec = full(vec_ref[...])
     own = middle_a.shape[0]
@@ -449,6 +483,18 @@
     attention_back(0, images, PAD_E, True, head_size, mixture_grad, proj_a, weights_a, stacked_ref)
     attention_back(own, images, PAD_E, True, head_size, mixture_grad, proj_b, weights_b, stacked_ref)
     part_ref[...] = normed_back(stacked_ref, qkv_ref)
+    width = qkv_ref.shape[2]
+
+    @pl.when(place_ref[1] == 0)
+    def _():
+        send_ref[:, :width] = stacked_ref[0]
+        send_ref[:, width:] = stacked_ref[1]
+
+    @pl.when(place_ref[1] == 1)
+    def _():
+        send_ref[:, :width] = stacked_ref[2]
+        send_ref[:, width:] = middle_low_ref[:, chunk(1 - place_ref[0], width)]
+
     sums_ref[0:1] = column_sum(middle_grad)
     sums_ref[1:2] = column_sum(two_grad * xhat)
     sums_ref[2:3] = column_sum(two_grad)
@@ -479,48 +525,55 @@
     small_ref[...] = low(rows_ref[...])
 
 
-def chunk(index, size):
-    return pl.ds(pl.multiple_of(index * size, LANES), size)
-
-
-def dec_hidden_weights_kernel(place_ref, hidden_ref, out_low_ref, normed_ref, up_ref, keep_ref, send_ref):
+def tall(*parts):
+    return jnp.concatenate(parts, axis=0)
+
+
+def by_side(place_ref, mine_ref, theirs_ref, blocks):
+    first = place_ref[1] == 0
+    rows = mine_ref.shape[1]
+    for part in range(2):
+        zero, one = (low(block[part * rows : (part + 1) * rows]) for block in blocks)
+        mine_ref[part] = jnp.where(first, zero, one)
+        theirs_ref[part] = jnp.where(first, one, zero)
+
+
+def dec_hidden_weights_kernel(
+    place_ref, hidden_ref, out_low_ref, normed_ref, up_ref, over_ref, mine_ref, theirs_ref
+):
     core = place_ref[0]
-    rows, cols = hidden_ref.shape[1] // 2, out_low_ref.shape[1]
-    half = normed_ref.shape[1] // 2
-    for ref, index in ((send_ref, 1 - core), (keep_ref, core)):
-        down = low(left_product(hidden_ref[:, chunk(index, rows)], out_low_ref[...]))
-        up = low(left_product(normed_ref[:, chunk(index, half)], up_ref[...]))
-        for part in range(2):
-            ref[0, part] = down[part * rows // 2 : (part + 1) * rows // 2]
-            ref[1, part] = up[:, part * cols : (part + 1) * cols]
-
-
-def head_blocks(normed, stacked_ref, mix, middle_low_ref, core, side):
-    half = normed[0].shape[1] // 2
-    wide = middle_low_ref.shape[1] // 2
-    left = jnp.concatenate([ref[:, chunk(core, half)] for ref in normed], axis=0)
-    if side == 0:
-        return low(left_product(left, stacked_ref[0])), low(left_product(left, stacked_ref[1]))
-    out = left_product(
-        jnp.concatenate([ref[...] for ref in mix], axis=0), middle_low_ref[:, chunk(core, wide)]
-    )
-    return low(left_product(left, stacked_ref[2])), low(out)
+    width, wide = out_low_ref.shape[1], up_ref.shape[1]
+    half = width // 2
+    over_up = over_ref[:, wide // 2 + half : wide // 2 + half + wide]
+    over_out = over_ref[:, wide // 2 + half + wide :]
+    down = left_product(
+        tall(hidden_ref[:, chunk(core, wide // 2)], over_ref[:, : wide // 2]), tall(out_low_ref[...], over_out)
+    )
+    up = left_product(
+        tall(normed_ref[:, chunk(core, half)], over_ref[:, wide // 2 : wide // 2 + half]),
+        tall(up_ref[...], over_up),
+    )
+    by_side(place_ref, mine_ref, theirs_ref, (down, tall(up[:, :width], up[:, width:])))
 
 
 def dec_head_weights_kernel(
-    place_ref, normed_ref, stacked_ref, mix_ref, middle_low_ref, keep_ref, send_ref
+    place_ref, normed_ref, stacked_ref, mix_ref, middle_low_ref, over_ref, mine_ref, theirs_ref
 ):
     core = place_ref[0]
     width = mix_ref.shape[1]
-    for ref, index in ((send_ref, 1 - core), (keep_ref, core)):
-        for side in range(2):
-            first, second = head_blocks(
-                [normed_ref], stacked_ref, [mix_ref], middle_low_ref, index, side
-            )
-            rows = first.shape[0] // 2
-            for part in range(2):
-                ref[side, part, :, :width] = first[part * rows : (part + 1) * rows]
-                ref[side, part, :, width:] = second[part * rows : (part + 1) * rows]
+    half = normed_ref.shape[1] // 2
+    left = tall(normed_ref[:, chunk(core, half)], over_ref[:, 4 * width : 4 * width + half])
+    grads = [
+        left_product(left, tall(stacked_ref[j], over_ref[:, j * width : (j + 1) * width])) for j in range(3)
+    ]
+    out = left_product(
+        tall(mix_ref[...], over_ref[:, 3 * width : 4 * width]),
+        tall(middle_low_ref[:, chunk(core, half)], over_ref[:, 4 * width + half :]),
+    )
+    by_side(
+        place_ref, mine_ref, theirs_ref,
+        (jnp.concatenate(grads[:2], axis=1), jnp.concatenate([grads[2], out], axis=1)),
+    )
 
 
 def put_rows(rows_ref, row, up_sum_ref, bias_sum_ref):
@@ -582,45 +635,97 @@
     return jnp.concatenate([first[:, lanes], second[:, lanes]], axis=0)
 
 
-def enc_down_weights_kernel(place_ref, hidden_a, hidden_b, cot_a, cot_b, keep_ref, send_ref):
-    core, side = place_ref[0], place_ref[1]
-    cot = stacked_rows(cot_a, cot_b)
-    half = keep_ref.shape[1]
-    for ref, index in ((send_ref, 1 - core), (keep_ref, core)):
-        block = low(left_product(stacked_rows(hidden_a, hidden_b, chunk(2 * index + side, 2 * half)), cot))
-        ref[0] = block[:half]
-        ref[1] = block[half:]
-
-
-def enc_up_weights_kernel(place_ref, normed_a, normed_b, up_ref, keep_ref, send_ref):
-    core, side = place_ref[0], place_ref[1]
-    normed = stacked_rows(normed_a, normed_b)
-    half, cols = keep_ref.shape[1:]
-    for ref, index in ((send_ref, 1 - core), (keep_ref, core)):
-        block = low(left_product(normed, up_ref[:, chunk(2 * index + side, cols)]))
-        ref[0] = block[:half]
-        ref[1] = block[half:]
-
-
-def enc_head_weights_kernel(
-    place_ref, normed_a, normed_b, stacked_ref, mix_a, mix_b, middle_low_ref, small_ref, keep_ref, send_ref
-):
-    core = place_ref[0]
+def enc_hidden_weights_kernel(
+    place_ref, hidden_a, hidden_b, cot_a, cot_b, normed_a, normed_b, up_ref,
+    forward_a, forward_b, over_cot_a, over_cot_b, over_up, mine_ref, theirs_ref,
+):
+    core, side, half = place_ref[0], place_ref[1], place_ref[2]
+    rows = mine_ref.shape[0] // 2
+    width = 2 * rows
+    features = cot_a.shape[1]
+    lanes = chunk(2 * core + side, width)
+    down = low(
+        left_product(
+            tall(hidden_a[:, lanes], hidden_b[:, lanes], forward_a[:, :width], forward_b[:, :width]),
+            tall(cot_a[...], cot_b[...], over_cot_a[...], over_cot_b[...]),
+        )
+    )
+    here = slice(width, width + features)
+    up = low(
+        left_product(
+            tall(normed_a[...], normed_b[...], forward_a[:, here], forward_b[:, here]),
+            tall(up_ref[:, lanes], over_up[...]),
+        )
+    )
+    for part in range(2):
+        block = (
+            down[part * rows : (part + 1) * rows],
+            up[2 * part * rows : (2 * part + 1) * rows],
+            up[(2 * part + 1) * rows : (2 * part + 2) * rows],
+        )
+        for ref, index in ((mine_ref, half), (theirs_ref, 1 - half)):
+
+            @pl.when(index == part)
+            def _(ref=ref, block=block):
+                ref[:rows] = block[0]
+                ref[rows:, :width] = block[1]
+                ref[rows:, width:] = block[2]
+
+
+def last_weights_kernel(
+    place_ref, normed_a, normed_b, stacked_ref, mix_a, mix_b, middle_low_ref, forward_a, forward_b, over_ref,
+    small_ref, rest_mine, rest_other, mine_ref, theirs_ref,
+):
+    core, half = place_ref[0], place_ref[2]
     width = mix_a.shape[1]
-    for wanted in range(2):
-
-        @pl.when(place_ref[1] == wanted)
-        def _(wanted=wanted):
-            for ref, index in ((send_ref, 1 - core), (keep_ref, core)):
-                first, second = head_blocks(
-                    [normed_a, normed_b], stacked_ref, [mix_a, mix_b], middle_low_ref, index, wanted
-                )
-                rows = first.shape[0] // 2
-                few = small_ref.shape[0] // 2
-                for part in range(2):
-                    ref[part, :rows, :width] = first[part * rows : (part + 1) * rows]
-                    ref[part, :rows, width:] = second[part * rows : (part + 1) * rows]
-                    ref[part, rows:] = small_ref[part * few : (part + 1) * few]
+    half_width = normed_a.shape[1] // 2
+    lanes = chunk(core, half_width)
+    start = forward_a.shape[1] - half_width - width
+    left = tall(
+        normed_a[:, lanes], normed_b[:, lanes],
+        forward_a[:, start : start + half_width], forward_b[:, start : start + half_width],
+    )
+    few = small_ref.shape[0] // 2
+    columns = mine_ref.shape[1]
+
+    def put(first, second):
+        rows = first.shape[0] // 2
+        for part in range(2):
+            here = slice(part * rows, (part + 1) * rows)
+            block = jnp.concatenate([first[here], second[here]], axis=1)
+            block = tall(low(block), small_ref[part * few : (part + 1) * few])
+            for ref, index in ((mine_ref, half), (theirs_ref, 1 - half)):
+
+                @pl.when(index == part)
+                def _(ref=ref, block=block):
+                    for i in range(block.shape[1] // columns):
+                        ref[i * block.shape[0] : (i + 1) * block.shape[0]] = block[
+                            :, i * columns : (i + 1) * columns
+                        ]
+
+    @pl.when(place_ref[1] == 0)
+    def _():
+        put(
+            left_product(left, tall(stacked_ref[0], over_ref[:, :width])),
+            left_product(left, tall(stacked_ref[1], over_ref[:, width:])),
+        )
+
+    @pl.when(place_ref[1] == 1)
+    def _():
+        put(
+            left_product(left, tall(stacked_ref[2], over_ref[:, :width])),
+            left_product(
+                tall(mix_a[...], mix_b[...], forward_a[:, start + half_width :], forward_b[:, start + half_width :]),
+                tall(middle_low_ref[:, lanes], over_ref[:, width:]),
+            ),
+        )
+
+    for ref, index in ((mine_ref, half), (theirs_ref, 1 - half)):
+        total = low(pair(rest_mine[index], rest_other[index]))
+        count = total.shape[0]
+        row = ref.shape[0] - count * (total.shape[1] // columns)
+        for i in range(total.shape[1] // columns):
+            ref[row + i * count : row + (i + 1) * count] = total[:, i * columns : (i + 1) * columns]
 
 
 def fold_kernel(axis, place_ref, *refs):
@@ -634,19 +739,37 @@
         theirs_ref[here] = low(pair(keep_ref[1 - index], other_ref[1 - index]))
 
 
+def fold_more_kernel(place_ref, keep_ref, other_ref, before_mine, before_theirs, mine_ref, theirs_ref):
+    index = place_ref[2]
+    rows = before_mine.shape[0]
+    mine_ref[:rows] = before_mine[...]
+    theirs_ref[:rows] = before_theirs[...]
+    mine_ref[rows:] = low(pair(keep_ref[index], other_ref[index]))
+    theirs_ref[rows:] = low(pair(keep_ref[1 - index], other_ref[1 - index]))
+
+
 def add_kernel(first_ref, second_ref, sum_ref):
     sum_ref[...] = low(pair(first_ref[...], second_ref[...]))
 
 
-def fold(order, place, axis, *arrays):
+def fold(order, place, axis, *arrays, after=()):
     shape = arrays[0].shape[1:-2] + (sum(x.shape[-2] for x in arrays[::2]), arrays[0].shape[-1])
     return kernel_call(
-        order, functools.partial(fold_kernel, axis), [shaped(shape)] * 2, place, *arrays, scalars=1, name="fold"
-    )
-
-
-def add(order, first, second):
-    return kernel_call(order, add_kernel, [shaped(first.shape)], first, second, name="add")[0]
+        order, functools.partial(fold_kernel, axis), [shaped(shape)] * 2, place, *arrays,
+        scalars=1, after=after, name="fold",
+    )
+
+
+def add(order, first, second, after=()):
+    return kernel_call(order, add_kernel, [shaped(first.shape)], first, second, after=after, name="add")[0]
+
+
+def mark_kernel(out_ref):
+    out_ref[...] = jnp.zeros_like(out_ref)
+
+
+def mark(order, *values):
+    kernel_call(order, mark_kernel, [shaped((8, LANES), FULL)], after=values, name="mark")
 
 
 def flip(value, step):
@@ -657,8 +780,8 @@
     return flip(value, 4) if lax.axis_size("dp") > 4 else jnp.zeros_like(value)
 
 
-def cross_end(order, value, arrived):
-    value = add(order, value, arrived)
+def cross_end(order, value, arrived, after=()):
+    value = add(order, value, arrived, after)
     step = 8
     while step < lax.axis_size("dp"):
         value = add(order, value, flip(value, step))
@@ -688,70 +811,77 @@
     return pl.ds(pl.multiple_of(index * size, size), size)
 
 
-def dec_hidden_whole_kernel(place_ref, own_ref, over_ref, fc1_ref, fc2_ref):
-    for ref, core, side, half in pieces_of(place_ref, own_ref, over_ref):
-        rows, cols = ref.shape
-        if side == 0:
-            fc2_ref[aligned(2 * core + half, rows), :] = full(ref[...])
-        else:
-            fc1_ref[aligned(core, rows), half * cols : (half + 1) * cols] = full(ref[...])
-
-
-def put_heads(ref, rows, core, side, half, qkv_ref, out_w_ref):
-    width = qkv_ref.shape[2]
+def put_heads(block, core, side, half, qkv_ref, out_w_ref):
+    rows, width = block.shape[0], qkv_ref.shape[2]
     here = aligned(2 * core + half, rows)
     if side == 0:
-        qkv_ref[0, here, :] = full(ref[:rows, :width])
-        qkv_ref[1, here, :] = full(ref[:rows, width:])
+        qkv_ref[0, here, :] = full(block[:, :width])
+        qkv_ref[1, here, :] = full(block[:, width:])
     else:
-        qkv_ref[2, here, :] = full(ref[:rows, :width])
-        out_w_ref[half * rows : (half + 1) * rows, aligned(core, width)] = full(ref[:rows, width:])
-
-
-def enc_head_whole_kernel(
-    place_ref, own_ref, over_ref, qkv_ref, out_w_ref, vec_ref, up_sum_ref, bias_sum_ref, rows_ref
+        qkv_ref[2, here, :] = full(block[:, :width])
+        out_w_ref[half * rows : (half + 1) * rows, aligned(core, width)] = full(block[:, width:])
+
+
+def dec_whole_kernel(place_ref, own_ref, over_ref, fc1_ref, fc2_ref, qkv_ref, out_w_ref):
+    rows, cols = fc1_ref.shape[0] // 2, fc1_ref.shape[1] // 2
+    for ref, core, side, half in pieces_of(place_ref, own_ref, over_ref):
+        if side == 0:
+            fc2_ref[aligned(2 * core + half, rows), :] = full(ref[:rows])
+        else:
+            fc1_ref[aligned(core, rows), half * cols : (half + 1) * cols] = full(ref[:rows])
+        put_heads(ref[rows:], core, side, half, qkv_ref, out_w_ref)
+
+
+def last_whole_kernel(
+    place_ref, own_ref, over_ref, qkv_ref, out_w_ref, vec_ref, up_sum_ref, bias_sum_ref,
+    bridge_ref, pos_ref, dec_vec_ref, dec_up_sum_ref, dec_bias_sum_ref, rows_ref, small_ref,
 ):
     few = rows_ref.shape[0] // 2
-    rows = own_ref.shape[2] - few
+    rows = qkv_ref.shape[1] // 4 + few
+    width = own_ref.shape[3]
+    wide, cols = 2 * qkv_ref.shape[2], bridge_ref.shape[1]
+    rest = (own_ref.shape[2] - rows * (wide // width)) * width // cols
+    quarter, part = bridge_ref.shape[0] // 4, small_ref.shape[0] // 4
+
+    def take(ref, row, count, lanes):
+        return jnp.concatenate(
+            [ref[row + i * count : row + (i + 1) * count] for i in range(lanes // width)], axis=1
+        )
+
     for ref, core, side, half in pieces_of(place_ref, own_ref, over_ref):
-        put_heads(ref, rows, core, side, half, qkv_ref, out_w_ref)
-    for half in range(2):
-        rows_ref[half * few : (half + 1) * few] = full(own_ref[0, half, rows:])
-    vec_ref[...] = rows_ref[0:6]
-    take_rows(rows_ref, 6, up_sum_ref, bias_sum_ref)
-
-
-def dec_rest_whole_kernel(
-    place_ref, own_ref, over_ref, qkv_ref, out_w_ref, bridge_ref, pos_ref, vec_ref, up_sum_ref, bias_sum_ref,
-    small_ref,
-):
-    quarter, few = bridge_ref.shape[0] // 4, small_ref.shape[0] // 4
-    rows = qkv_ref.shape[1] // 4
-    more = own_ref.shape[2] - rows
-    for ref, core, side, half in pieces_of(place_ref, own_ref, over_ref):
-        put_heads(ref, rows, core, side, half, qkv_ref, out_w_ref)
+        heads = take(ref, 0, rows, wide)
+        put_heads(heads[: rows - few], core, side, half, qkv_ref, out_w_ref)
+        block = take(ref, rows * (wide // width), rest, cols)
         index = 2 * core + side
         start = pl.multiple_of(index * quarter, 8)
         if half == 0:
-            bridge_ref[pl.ds(start, more), :] = full(ref[rows:])
+            bridge_ref[pl.ds(start, rest), :] = full(block)
         else:
-            left = quarter - more
-            bridge_ref[pl.ds(start + more, left), :] = full(ref[rows : rows + left])
-            small_ref[aligned(index, few), :] = full(ref[rows + left :])
+            left = quarter - rest
+            bridge_ref[pl.ds(start + rest, left), :] = full(block[:left])
+            small_ref[aligned(index, part), :] = full(block[left:])
+    for half in range(2):
+        rows_ref[half * few : (half + 1) * few] = pair(
+            take(own_ref.at[0, half], 0, rows, wide)[rows - few :],
+            take(over_ref.at[0, half], 0, rows, wide)[rows - few :],
+        )
+    vec_ref[...] = rows_ref[0:6]
+    take_rows(rows_ref, 6, up_sum_ref, bias_sum_ref)
     pos_ref[...] = small_ref[0:PATCHES]
-    vec_ref[...] = small_ref[PAD_D : PAD_D + 8]
-    take_rows(small_ref, PAD_D + 8, up_sum_ref, bias_sum_ref)
-
-
-def enc_down_whole_kernel(place_ref, own_ref, over_ref, fc2_ref):
+    dec_vec_ref[...] = small_ref[PAD_D : PAD_D + 8]
+    take_rows(small_ref, PAD_D + 8, dec_up_sum_ref, dec_bias_sum_ref)
+
+
+def enc_hidden_whole_kernel(place_ref, own_ref, over_ref, fc1_ref, fc2_ref):
     for ref, core, side, half in pieces_of(place_ref, own_ref, over_ref):
-        fc2_ref[aligned(4 * core + 2 * side + half, ref.shape[0]), :] = full(ref[...])
-
-
-def enc_up_whole_kernel(place_ref, own_ref, over_ref, fc1_ref):
-    for ref, core, side, half in pieces_of(place_ref, own_ref, over_ref):
-        rows, cols = ref.shape
-        fc1_ref[half * rows : (half + 1) * rows, aligned(2 * core + side, cols)] = full(ref[...])
+        rows = ref.shape[0] // 2
+        width = 2 * rows
+        fc2_ref[aligned(4 * core + 2 * side + half, rows), :] = full(ref[:rows])
+        lanes = aligned(2 * core + side, width)
+        for part in range(2):
+            fc1_ref[(2 * half + part) * rows : (2 * half + part + 1) * rows, lanes] = full(
+                ref[rows:, part * width : (part + 1) * width]
+            )
 
 
 def spread(piece):
@@ -759,9 +889,9 @@
     return piece, other, flip(piece, 1), flip(other, 1)
 
 
-def pack(order, place, pieces):
+def pack(order, place, pieces, after=()):
     (packed,) = kernel_call(
-        order, pack_kernel, [shaped((2, 2) + pieces[0].shape)], place, *pieces, scalars=1, name="pack"
+        order, pack_kernel, [shaped((2, 2) + pieces[0].shape)], place, *pieces, scalars=1, after=after, name="pack"
     )
     return packed, swap(packed, "section")
 
@@ -797,7 +927,7 @@
     order = []
     call = functools.partial(kernel_call, order)
 
-    def enc_attend(rows):
+    def enc_attend(rows, memory=24):
         return call(
             functools.partial(enc_attend_kernel, images, enc_size),
             [
@@ -809,14 +939,15 @@
                 shaped((rows_e, enc_local)),
             ],
             place, rows, enc_vec, enc_qkv, enc_qv_bias, enc_out_w,
-            scalars=1, name="enc_attend",
+            scalars=1, memory=memory, name="enc_attend",
         )
 
+    part, x, normed, proj, weights, mix = enc_attend(enc_in, 60)
+    part_other = swap(part, "tensor")
+    own_in, x = lax.optimization_barrier((own_in, x))
     side_in = flip(own_in, 1)
-    part, x, normed, proj, weights, mix = enc_attend(enc_in)
-    part_other = swap(part, "tensor")
     side_part, side_x, side_normed, side_proj, side_weights, side_mix = enc_attend(side_in)
-    part_two, middle, normed_two, hidden, slope = call(
+    part_two, middle, normed_two, hidden, slope, forward_send = call(
         enc_hidden_kernel,
         [
             shaped((rows_e, enc_width)),
@@ -824,9 +955,10 @@
             shaped((rows_e, enc_width)),
             shaped((rows_e, enc_mlp)),
             shaped((rows_e, enc_mlp)),
+            shaped((rows_e, enc_mlp // 4 + enc_width + enc_width // 2 + enc_local)),
         ],
-        x, enc_vec, part, part_other, enc_fc1, enc_fc1_bias, enc_fc2,
-        name="enc_hidden",
+        place, x, enc_vec, part, part_other, enc_fc1, enc_fc1_bias, normed, mix, enc_fc2,
+        scalars=1, name="enc_hidden",
     )
     part_two_other = swap(part_two, "tensor")
     side_part_other = swap(side_part, "tensor")
@@ -850,23 +982,22 @@
         scalars=1, name="dec_attend",
     )
     dec_part_other = swap(dec_part, "tensor")
-    (enc_out_both,) = call(
-        both_cores_kernel, [shaped((images * VIS, 2, enc_width))],
-        place, enc_out, swap(enc_out, "section"), scalars=1, name="enc_out_both",
-    )
-    side_middle, side_normed_two, side_hidden, side_slope = call(
+    enc_out_over = swap(enc_out, "section")
+    forward_over = swap(forward_send, "section")
+    side_middle, side_normed_two, side_hidden, side_slope, side_forward_send = call(
         enc_side_hidden_kernel,
         [
             shaped((rows_e, enc_width), FULL),
             shaped((rows_e, enc_width)),
             shaped((rows_e, enc_mlp)),
             shaped((rows_e, enc_mlp)),
+            shaped((rows_e, enc_mlp // 4 + enc_width + enc_width // 2 + enc_local)),
         ],
-        side_x, enc_vec, side_part, side_part_other, enc_fc1, enc_fc1_bias,
-        name="enc_side_hidden",
+        place, side_x, enc_vec, side_part, side_part_other, enc_fc1, enc_fc1_bias, side_normed, side_mix,
+        scalars=1, name="enc_side_hidden",
     )
     (
-        dec_part_back, dec_part_two, dec_middle, dec_normed_two, dec_hid, out_low, dec_up, up_sum, out_sum,
+        dec_part_back, dec_part_two, dec_middle, dec_normed_two, dec_hid, out_low, dec_up, up_sum, out_sum, d1_send,
     ) = call(
         functools.partial(dec_hidden_kernel, images),
         [
@@ -879,21 +1010,27 @@
             shaped((rows_d, dec_mlp)),
             shaped((1, dec_mlp), FULL),
             shaped((1, dec_width), FULL),
+            shaped((rows_d, dec_mlp // 2 + dec_width // 2 + dec_mlp + dec_width)),
         ],
-        count, starting, dec_part, dec_part_other, dec_vec, dec_fc1, dec_fc1_bias, dec_fc2, cot,
-        scalars=1, name="dec_hidden",
-    )
-
+        count, place, starting, dec_part, dec_part_other, dec_vec, dec_fc1, dec_fc1_bias, dec_fc2, cot,
+        scalars=2, after=[forward_over], name="dec_hidden",
+    )
+
+    side_forward_over = swap(side_forward_send, "section")
+    d1_over = swap(d1_send, "section")
     dec_part_back_other = swap(dec_part_back, "tensor")
-    d1_keep, d1_send = call(
+    (enc_out_both,) = call(
+        both_cores_kernel, [shaped((images * VIS, 2, enc_width))],
+        place, enc_out, enc_out_over, scalars=1, name="enc_out_both",
+    )
+    d1_mine, d1_theirs = call(
         dec_hidden_weights_kernel,
-        [shaped((2, 2, dec_mlp // 4, dec_width))] * 2,
-        place, dec_hid, out_low, dec_normed_two, dec_up,
-        scalars=1, name="dec_hidden_weights",
-    )
-    d1_mine, d1_theirs = fold(order, place, 1, d1_keep, swap(d1_send, "section"))
+        [shaped((2, dec_mlp // 4, dec_width))] * 2,
+        place, dec_hid, out_low, dec_normed_two, dec_up, d1_over,
+        scalars=1, after=[side_forward_over], name="dec_hidden_weights",
+    )
     d1_arrived = flip(d1_theirs, 1)
-    dec_part_one, dec_middle_grad, dec_middle_low, dec_stacked, middle_sums, dec_bias_sum = call(
+    dec_part_one, dec_middle_grad, dec_middle_low, dec_stacked, middle_sums, dec_bias_sum, d2_send = call(
         functools.partial(dec_attend_back_kernel, images, dec_size),
         [
             shaped((rows_d, dec_width)),
@@ -902,22 +1039,22 @@
             shaped((3, rows_d, dec_local)),
             shaped((3, dec_width), FULL),
             shaped((2, dec_local), FULL),
+            shaped((rows_d, 4 * dec_local + dec_width)),
         ],
-        dec_middle, out_low, dec_part_back, dec_part_back_other, dec_vec, dec_proj, dec_weights, dec_qkv, dec_out_w,
-        name="dec_attend_back",
-    )
+        place, dec_middle, out_low, dec_part_back, dec_part_back_other, dec_vec, dec_proj, dec_weights, dec_qkv, dec_out_w,
+        dec_normed, dec_mix,
+        scalars=1, name="dec_attend_back",
+    )
+    d2_over = swap(d2_send, "section")
     dec_part_one_other = swap(dec_part_one, "tensor")
     d1_mine, d1_theirs = fold(order, place, 2, d1_mine, d1_arrived)
-    d1_arrived = flip(d1_theirs, 2)
-    d2_keep, d2_send = call(
+    d2_mine, d2_theirs = call(
         dec_head_weights_kernel,
-        [shaped((2, 2, dec_width // 4, 2 * dec_local))] * 2,
-        place, dec_normed, dec_stacked, dec_mix, dec_middle_low,
+        [shaped((2, dec_width // 4, 2 * dec_local))] * 2,
+        place, dec_normed, dec_stacked, dec_mix, dec_middle_low, d2_over,
         scalars=1, name="dec_head_weights",
     )
-    d2_other = swap(d2_send, "section")
-    d1 = add(order, d1_mine, d1_arrived)
-    d1_arrived = cross_start(d1)
+    d2_arrived = flip(d2_theirs, 1)
     enc_cot, lifted_grad, pos_grad, start_sums = call(
         functools.partial(dec_start_back_kernel, images),
         [
@@ -930,6 +1067,14 @@
         scalars=1, name="dec_start_back",
     )
     side_cot = flip(enc_cot, 1)
+    over_cot = swap(enc_cot, "section")
+    d1_mine, d1_theirs = call(
+        fold_more_kernel,
+        [shaped((dec_mlp // 4 + dec_width // 4, dec_width))] * 2,
+        place, d2_mine, d2_arrived, d1_mine, d1_theirs,
+        scalars=1, name="fold_more",
+    )
+    d1_arrived = flip(d1_theirs, 2)
     small_rows = 256
     d3_keep, d3_send = call(
         dec_bridge_weights_kernel,
@@ -938,30 +1083,34 @@
         scalars=1, scratch=[pltpu.VMEM((small_rows, dec_width), FULL)], name="dec_bridge_weights",
     )
     d3_other = swap(d3_send, "section")
-
-    e1_keep, e1_send = call(
-        enc_down_weights_kernel,
-        [shaped((2, enc_mlp // 8, enc_width))] * 2,
-        place, hidden, side_hidden, enc_cot, side_cot,
-        scalars=1, name="enc_down_weights",
-    )
-    e1_other = swap(e1_send, "section")
-    part, up = call(
+    side_cot, d3_keep = lax.optimization_barrier((side_cot, d3_keep))
+    side_over_cot = swap(side_cot, "section")
+
+    part, up, up_send = call(
         enc_hidden_back_kernel,
-        [shaped((2 * rows_e, enc_width)), shaped((2 * rows_e, enc_mlp))],
-        enc_cot, side_cot, slope, side_slope, enc_fc1, enc_fc2,
-        name="enc_hidden_back",
-    )
+        [
+            shaped((2 * rows_e, enc_width)),
+            shaped((2 * rows_e, enc_mlp)),
+            shaped((2 * rows_e, enc_mlp // 4)),
+        ],
+        place, enc_cot, side_cot, slope, side_slope, enc_fc1, enc_fc2,
+        scalars=1, after=[over_cot], name="enc_hidden_back",
+    )
+    up_over = swap(up_send, "section")
     part_other = swap(part, "tensor")
-    e1_mine, e1_theirs = fold(order, place, 2, e1_keep, e1_other)
+    d3_mine, d3_theirs = fold(order, place, 1, d3_keep, d3_other, after=[side_over_cot])
+    d3_arrived = flip(d3_theirs, 1)
+    e1_mine, e1_theirs = call(
+        enc_hidden_weights_kernel,
+        [shaped((enc_mlp // 4, enc_width))] * 2,
+        place, hidden, side_hidden, enc_cot, side_cot, normed_two, side_normed_two, up,
+        forward_over, side_forward_over, over_cot, side_over_cot, up_over,
+        scalars=1, name="enc_hidden_weights",
+    )
     e1_arrived = flip(e1_theirs, 2)
-    d1 = cross_end(order, d1, d1_arrived)
-    d1_spread = spread(d1)
-    d2_mine, d2_theirs = fold(order, place, 1, d2_keep, d2_other, d3_keep, d3_other)
-    d2_arrived = flip(d2_theirs, 1)
-    e1 = add(order, e1_mine, e1_arrived)
-    e1_arrived = cross_start(e1)
-    back_part, middle_grad, middle_low, stacked, middle_two_sums, bias_sum, enc_up_sum = call(
+    d1 = add(order, d1_mine, d1_arrived)
+    d1_arrived = cross_start(d1)
+    back_part, middle_grad, middle_low, stacked, middle_two_sums, bias_sum, enc_up_sum, e3_send = call(
         functools.partial(enc_attend_back_kernel, images, enc_size),
         [
             shaped((2 * rows_e, enc_width)),
@@ -971,24 +1120,20 @@
             shaped((4, enc_width), FULL),
             shaped((2, enc_local), FULL),
             shaped((1, enc_mlp), FULL),
+            shaped((2 * rows_e, 2 * enc_local)),
         ],
-        middle, side_middle, enc_cot, side_cot, part, part_other, enc_vec, proj, side_proj,
+        place, middle, side_middle, enc_cot, side_cot, part, part_other, enc_vec, proj, side_proj,
         weights, side_weights, enc_qkv, enc_out_w, up,
-        name="enc_attend_back",
-    )
+        scalars=1, after=[d3_arrived], name="enc_attend_back",
+    )
+    e3_over = swap(e3_send, "section")
     back_part_other = swap(back_part, "tensor")
-    d1_packed = pack(order, place, d1_spread)
-    e2_keep, e2_send = call(
-        enc_up_weights_kernel,
-        [shaped((2, enc_width // 2, enc_mlp // 4))] * 2,
-        place, normed_two, side_normed_two, up,
-        scalars=1, name="enc_up_weights",
-    )
-    e2_other = swap(e2_send, "section")
-    d2_mine, d2_theirs = fold(order, place, 2, d2_mine, d2_arrived)
-    d2_arrived = flip(d2_theirs, 2)
-    e2_mine, e2_theirs = fold(order, place, 2, e2_keep, e2_other)
-    e2_arrived = flip(e2_theirs, 2)
+    d1 = cross_end(order, d1, d1_arrived)
+    d1_spread = spread(d1)
+    e1 = add(order, e1_mine, e1_arrived, [e3_over])
+    dec_part_two, e1 = lax.optimization_barrier((dec_part_two, e1))
+    dec_part_two_other = swap(dec_part_two, "tensor")
+    e1_arrived = cross_start(e1)
     few = 32
     grad_in, small = call(
         functools.partial(enc_start_back_kernel, images),
@@ -996,66 +1141,64 @@
         x, side_x, back_part, back_part_other, enc_vec, middle_grad, middle_two_sums, enc_up_sum, bias_sum,
         scratch=[pltpu.VMEM((few, enc_width), FULL)], name="enc_start_back",
     )
-    e3_keep, e3_send = call(
-        enc_head_weights_kernel,
-        [shaped((2, enc_width // 4 + few // 2, 2 * enc_local))] * 2,
-        place, normed, side_normed, stacked, mix, side_mix, middle_low, small,
-        scalars=1, name="enc_head_weights",
-    )
-    e3_other = swap(e3_send, "section")
-    e1 = cross_end(order, e1, e1_arrived)
-    e1_spread = spread(e1)
-    e2 = add(order, e2_mine, e2_arrived)
-    e2_arrived = cross_start(e2)
-    e3_mine, e3_theirs = fold(order, place, 2, e3_keep, e3_other)
+    e3_mine, e3_theirs = call(
+        last_weights_kernel,
+        [
+            shaped(
+                (
+                    ((enc_width // 4 + few // 2) * 2 * enc_local + (enc_width + small_rows) // 8 * dec_width)
+                    // (dec_width // 2),
+                    dec_width // 2,
+                )
+            )
+        ] * 2,
+        place, normed, side_normed, stacked, mix, side_mix, middle_low, forward_over, side_forward_over, e3_over,
+        small, d3_mine, d3_arrived,
+        scalars=1, after=[d1_spread[1]], name="last_weights",
+    )
     e3_arrived = flip(e3_theirs, 2)
-    g_dec_fc1, g_dec_fc2 = call(
-        dec_hidden_whole_kernel,
-        [shaped(dec_fc1.shape, FULL), shaped(dec_fc2.shape, FULL)],
-        place, *d1_packed, scalars=1, name="dec_hidden_whole",
-    )
-    d2 = add(order, d2_mine, d2_arrived)
-    d2_arrived = cross_start(d2)
-    e1_packed = pack(order, place, e1_spread)
-    e2 = cross_end(order, e2, e2_arrived)
-    e2_spread = spread(e2)
-    (g_enc_fc2,) = call(
-        enc_down_whole_kernel, [shaped(enc_fc2.shape, FULL)],
-        place, *e1_packed, scalars=1, name="enc_down_whole",
-    )
-    e3 = add(order, e3_mine, e3_arrived)
-    e3_arrived = cross_start(e3)
-    d2 = cross_end(order, d2, d2_arrived)
-    d2_spread = spread(d2)
-    e2_packed = pack(order, place, e2_spread)
-    dec_part_two, e2_own = lax.optimization_barrier((dec_part_two, e2_packed[0]))
-    dec_part_two_other = swap(dec_part_two, "tensor")
-    (g_enc_fc1,) = call(
-        enc_up_whole_kernel, [shaped(enc_fc1.shape, FULL)],
-        place, e2_own, e2_packed[1], scalars=1, name="enc_up_whole",
-    )
-    e3 = cross_end(order, e3, e3_arrived)
-    e3_spread = spread(e3)
-    d2_packed = pack(order, place, d2_spread)
+    d1_packed = pack(order, place, d1_spread)
     (dec_out,) = call(
         functools.partial(dec_out_kernel, images),
         [shaped((dec_rows, dec_width))],
         count, dec_middle, dec_part_two, dec_part_two_other, dec_vec,
         scalars=1, name="dec_out",
     )
-    g_dec_qkv, g_dec_out_w, g_bridge, g_dec_pos, g_dec_vec, g_dec_fc1_bias, g_dec_qv_bias = call(
-        dec_rest_whole_kernel,
+    e1 = cross_end(order, e1, e1_arrived)
+    e1_spread = spread(e1)
+    e3 = add(order, e3_mine, e3_arrived)
+    e3_arrived = cross_start(e3)
+    g_dec_fc1, g_dec_fc2, g_dec_qkv, g_dec_out_w = call(
+        dec_whole_kernel,
+        [shaped(x.shape, FULL) for x in (dec_fc1, dec_fc2, dec_qkv, dec_out_w)],
+        place, *d1_packed, scalars=1, name="dec_whole",
+    )
+    mark(order, e1_spread[1])
+    e3 = cross_end(order, e3, e3_arrived)
+    e3_spread = spread(e3)
+    e1_packed = pack(order, place, e1_spread)
+    mark(order, e3_spread[1])
+    g_enc_fc1, g_enc_fc2 = call(
+        enc_hidden_whole_kernel,
+        [shaped(enc_fc1.shape, FULL), shaped(enc_fc2.shape, FULL)],
+        place, *e1_packed, scalars=1, name="enc_hidden_whole",
+    )
+    e3_packed = pack(order, place, e3_spread)
+    (
+        g_enc_qkv, g_enc_out_w, g_enc_vec, g_enc_fc1_bias, g_enc_qv_bias,
+        g_bridge, g_dec_pos, g_dec_vec, g_dec_fc1_bias, g_dec_qv_bias,
+    ) = call(
+        last_whole_kernel,
         [
             shaped(x.shape, FULL)
-            for x in (dec_qkv, dec_out_w, bridge_w, dec_pos, dec_vec, dec_fc1_bias, dec_qv_bias)
+            for x in (
+                enc_qkv, enc_out_w, enc_vec, enc_fc1_bias, enc_qv_bias,
+                bridge_w, dec_pos, dec_vec, dec_fc1_bias, dec_qv_bias,
+            )
         ],
-        place, *d2_packed, scalars=1, scratch=[pltpu.VMEM((small_rows, dec_width), FULL)], name="dec_rest_whole",
-    )
-    e3_packed = pack(order, place, e3_spread)
-    g_enc_qkv, g_enc_out_w, g_enc_vec, g_enc_fc1_bias, g_enc_qv_bias = call(
-        enc_head_whole_kernel,
-        [shaped(x.shape, FULL) for x in (enc_qkv, enc_out_w, enc_vec, enc_fc1_bias, enc_qv_bias)],
-        place, *e3_packed, scalars=1, scratch=[pltpu.VMEM((few, enc_width), FULL)], name="enc_head_whole",
+        place, *e3_packed, scalars=1,
+        scratch=[pltpu.VMEM((few, enc_width), FULL), pltpu.VMEM((small_rows, dec_width), FULL)],
+        name="last_whole",
     )
 
     return (

time: 256 us -> 234 us (0.914)
  starting transfers between devices: 46.5 us -> 32.2 us
  Pallas kernels: 117 us -> 106 us
  waiting for transfers between devices: 81.3 us -> 88.2 us
  local copies, waits for them, and re-layouts: 7.97 us -> 3.62 us
    ppermute x29 -> x20, starting transfers between devices: 35.3 us -> 20.7 us  [flip(): lax.ppermute(value, 'dp', [(i, i ^ step) for i in range(lax.axis_size('dp...]
    ppermute x29 -> x20, waiting for transfers between devices: 52.6 us -> 65.9 us  [flip(): lax.ppermute(value, 'dp', [(i, i ^ step) for i in range(lax.axis_size('dp...]
    pallas_call x46 -> x35, Pallas kernels: 117 us -> 106 us  [kernel_call(): pl.pallas_call(run, out_shape=[jax.ShapeDtypeStruct(x.shape, x.dtype) for...]
    ppermute x21 -> x22, waiting for transfers between devices: 28.6 us -> 22.3 us  [swap(): lax.ppermute(value, axis, [(i, i ^ 1) for i in range(lax.axis_size(axis))])]
    unnamed x111 -> x113, local copies, waits for them, and re-layouts: 5.98 us -> 1.64 us
    ppermute x21 -> x22, starting transfers between devices: 11.1 us -> 11.5 us  [swap(): lax.ppermute(value, axis, [(i, i ^ 1) for i in range(lax.axis_size(axis))])]
  transfers between devices with their start and end apart: 50 -> 42, of which waited for: 19 -> 19; matrix products, arithmetic and copies ran while one was open for 0% -> 0% of each run, Pallas kernels for 38% -> 40%
where the time goes in v1:
time: 234 us; the launch traced here: 233 us
  Pallas kernels  106 us (45%)
  waiting for transfers between devices  88.2 us (38%)
  starting transfers between devices  32.2 us (14%)
  local copies, waits for them, and re-layouts  3.62 us (2%)
    pallas_call x35, Pallas kernels, kernel_call(): pl.pallas_call(run, out_shape=[jax.ShapeDtypeStruct(x.shape, x.dtype) for...  106 us
    ppermute x20, waiting for transfers between devices, flip(): lax.ppermute(value, 'dp', [(i, i ^ step) for i in range(lax.axis_size('dp...  65.9 us
    ppermute x22, waiting for transfers between devices, swap(): lax.ppermute(value, axis, [(i, i ^ 1) for i in range(lax.axis_size(axis))])  22.3 us
    ppermute x20, starting transfers between devices, flip(): lax.ppermute(value, 'dp', [(i, i ^ step) for i in range(lax.axis_size('dp...  20.7 us
    ppermute x22, starting transfers between devices, swap(): lax.ppermute(value, axis, [(i, i ^ 1) for i in range(lax.axis_size(axis))])  11.5 us
  transfers between devices with their start and end apart: 42, of which 19 were waited for; matrix products, arithmetic and copies ran while one was open for 0% of the time, Pallas kernels for 40%

profile of v1, /device:TPU:0, one launch (start us, length us, event | category | flops | bytes accessed | tf_op | source)
XLA Modules:
  0.0 232.9 jit_solution(15044000783715221931)
XLA Ops:
  0.7 1.3 constant_dynamic-slice_fusion
  3.4 4.5 %enc_attend.2 = (bf16[128,768]{1,0:T(8,128)(2,1)}, bf16[128,768]{1,0:T(8,128)(2,1)}, bf16[128,768]{1,0:T(8,128)(2,1)}, bf16[3,128,384]{2,1,0:T(8,128)(2,1)}, bf1...) custom-call(s32[3]{0:T(128)} %pad_add_fusion.refs_0_.refs_1_, bf16[98,2,768]{2,1,0:T(2,128)(2,1)} %bitcast.25, ...), custom_call_target="tpu_custom_call" | custom-call | flops 199999995904 | bytes 1 | tf_op jit(solution)/shard_map/enc_attend/pallas_call | solution.py:164
  7.9 3.0 %collective-permute-start.1 = (bf16[98,768]{1,0:T(8,128)(2,1)S(1)}, bf16[98,768]{1,0:T(8,128)(2,1)S(1)}, u32[]{:S(2)}, u32[]{:S(2)}) collective-permute-start(bf16[98,768]{1,0:T(8,128)(2,1)S(1)} %bitcast.26), channel_id=1, source_target_pairs={{0,1},{1,0},{2,3},{3,2},{4,5},{5,4},{6,7},{7,6},{8,9},{9,8},{10,11... | collective-permute-start | bytes 451592 | tf_op jit(solution)/shard_map/ppermute | solution.py:776
  10.9 1.5 collective-permute-start
  13.0 2.0 collective-permute-done.1.refs_1_
  15.8 2.7 %enc_attend.3 = (bf16[128,768]{1,0:T(8,128)(2,1)}, bf16[128,768]{1,0:T(8,128)(2,1)S(1)}, bf16[128,768]{1,0:T(8,128)(2,1)S(1)}, bf16[3,128,384]{2,1,0:T(8,128)(2,...) custom-call(s32[3]{0:T(128)S(1)} %copy-done.4, ...), custom_call_target="tpu_custom_call" | custom-call | flops 199999995904 | bytes 1 | tf_op jit(solution)/shard_map/enc_attend/pallas_call | solution.py:164
  18.7 3.0 %enc_hidden.1 = (bf16[128,768]{1,0:T(8,128)(2,1)S(1)}, f32[128,768]{1,0:T(8,128)S(1)}, bf16[128,768]{1,0:T(8,128)(2,1)S(1)}, bf16[128,1536]{1,0:T(8,128)(2,1)S(1...) custom-call(s32[3]{0:T(128)S(1)} %copy-done.4, ...), custom_call_target="tpu_custom_call" | custom-call | flops 199999995904 | bytes 1 | tf_op jit(solution)/shard_map/enc_hidden/pallas_call | solution.py:164
  21.7 1.7 collective-permute-start.2
  23.9 5.6 %collective-permute-done.2.refs_4_ = bf16[128,768]{1,0:T(8,128)(2,1)S(1)} collective-permute-done((bf16[128,768]{1,0:T(8,128)(2,1)S(1)}, bf16[128,768]{1,0:T(8,128)(2,1)S(1)}, u32[]{:S(2)}, u32[]{:S(2)}) %collective-permute-start.2) | collective-permute-done | bytes 196640 | tf_op jit(solution)/shard_map/ppermute | solution.py:49
  29.6 5.0 %dec_attend.1 = (bf16[416,512]{1,0:T(8,128)(2,1)}, bf16[98,768]{1,0:T(8,128)(2,1)}, bf16[128,768]{1,0:T(8,128)(2,1)S(1)}, f32[416,512]{1,0:T(8,128)S(1)}, bf16[4...) custom-call(s32[1]{0:T(128)} %bitcast.3.refs_0_, ...), custom_call_target="tpu_custom_call" | custom-call | flops 199999995904 | bytes 1 | tf_op jit(solution)/shard_map/dec_attend/pallas_call | solution.py:164
  34.6 1.8 collective-permute-start.4
  36.5 2.8 %enc_side_hidden.1 = (f32[128,768]{1,0:T(8,128)S(1)}, bf16[128,768]{1,0:T(8,128)(2,1)S(1)}, bf16[128,1536]{1,0:T(8,128)(2,1)S(1)}, bf16[128,1536]{1,0:T(8,128)(2...) custom-call(s32[3]{0:T(128)S(1)} %copy-done.4, bf16[128,768]{1,0:T(8,128)(2,1)S(1)} %get-tuple-element.181.refs_1_, ...), custom_call_target="tpu_custom_call" | custom-call | flops 199999995904 | bytes 1 | tf_op jit(solution)/shard_map/enc_side_hidden/pallas_call | solution.py:164
  39.4 7.7 %collective-permute-done.4.refs_4_ = bf16[416,512]{1,0:T(8,128)(2,1)} collective-permute-done((bf16[416,512]{1,0:T(8,128)(2,1)}, bf16[416,512]{1,0:T(8,128)(2,1)}, u32[]{:S(2)}, u32[]{:S(2)}) %collective-permute-start.4) | collective-permute-done | bytes 426016 | tf_op jit(solution)/shard_map/ppermute | solution.py:49
  47.2 5.9 %dec_hidden.1 = (bf16[416,512]{1,0:T(8,128)(2,1)}, bf16[416,512]{1,0:T(8,128)(2,1)}, f32[416,512]{1,0:T(8,128)S(1)}, bf16[416,512]{1,0:T(8,128)(2,1)S(1)}, bf16[...) custom-call(s32[1]{0:T(128)} %bitcast.3.refs_0_, ...), custom_call_target="tpu_custom_call" | custom-call | flops 199999995904 | bytes 1 | tf_op jit(solution)/shard_map/dec_hidden/pallas_call | solution.py:164
  53.1 1.7 collective-permute-start.7
  54.8 2.2 enc_out_both.1
  57.0 2.1 collective-permute-done.8.refs_5_
  59.1 3.7 %dec_hidden_weights.1 = (bf16[2,256,512]{2,1,0:T(8,128)(2,1)S(1)}, bf16[2,256,512]{2,1,0:T(8,128)(2,1)}, f32[8,128]{1,0:T(8,128)S(1)}) custom-call(s32[3]{0:T(128)S(1)} %copy-done.4, bf16[416,1024]{1,0:T(8,128)(2,1)S(1)} %get-tuple-element.200.refs_1_, bf16[416,512]{1,0:T(8,128)(2,1)S(1)} %get-tuple-element.194.refs_2_, ...), custom_call_target="tpu_custom_call" | custom-call | flops 199999995904 | bytes 1 | tf_op jit(solution)/shard_map/dec_hidden_weights/pallas_call | solution.py:164
  62.8 1.5 collective-permute-start.12
  64.8 6.4 %dec_attend_back.1 = (bf16[416,512]{1,0:T(8,128)(2,1)}, f32[416,512]{1,0:T(8,128)S(1)}, bf16[416,512]{1,0:T(8,128)(2,1)S(1)}, bf16[3,416,256]{2,1,0:T(8,128)(2,1...) custom-call(s32[3]{0:T(128)S(1)} %copy-done.4, ...), custom_call_target="tpu_custom_call" | custom-call | flops 199999995904 | bytes 1 | tf_op jit(solution)/shard_map/dec_attend_back/pallas_call | solution.py:164
  71.2 1.7 collective-permute-start.10
  72.9 4.2 %collective-permute-done.12.refs_2_ = bf16[2,256,512]{2,1,0:T(8,128)(2,1)} collective-permute-done((bf16[2,256,512]{2,1,0:T(8,128)(2,1)}, bf16[2,256,512]{2,1,0:T(8,128)(2,1)}, u32[]{:S(2)}, u32[]{:S(2)}) %collective-permute-start.12) | collective-permute-done | bytes 524320 | tf_op jit(solution)/shard_map/ppermute | solution.py:776
  78.4 2.8 %dec_head_weights.1 = (bf16[2,128,512]{2,1,0:T(8,128)(2,1)S(1)}, bf16[2,128,512]{2,1,0:T(8,128)(2,1)}, f32[8,128]{1,0:T(8,128)S(1)}) custom-call(s32[3]{0:T(128)S(1)} %copy-done.4, bf16[416,512]{1,0:T(8,128)(2,1)S(1)} %copy-done.31, bf16[3,416,256]{2,1,0:T(8,128)(2,1)S(1)} %get-tuple-element.209.refs_2_, bf16[416,256]{1,0:T(8,128)(2,1)S(1)} %copy-done.36, ...), custom_call_target="tpu_custom_call" | custom-call | flops 199999995904 | bytes 1 | tf_op jit(solution)/shard_map/dec_head_weights/pallas_call | solution.py:164
  81.2 1.5 collective-permute-start.14
  82.7 3.7 %dec_start_back.1 = (bf16[128,768]{1,0:T(8,128)(2,1)}, bf16[128,512]{1,0:T(8,128)(2,1)S(1)}, f32[208,512]{1,0:T(8,128)S(1)}, f32[4,512]{1,0:T(4,128)S(1)}, f32[8,128]{1,0:T(8,128)S(1)}) custom-call(s32[1]{0:T(128)} %bitcast.3.refs_0_, s32[2,64]{1,0:T(2,128)S(1)} %copy-done.3, f32[416,512]{1,0:T(8,128)S(1)} %copy-done.27, ...), custom_call_target="tpu_custom_call" | custom-call | flops 199999995904 | bytes 1 | tf_op jit(solution)/shard_map/dec_start_back/pallas_call | solution.py:164
  87.3 1.7 collective-permute-done.14.refs_2_
  89.0 1.8 fold_more.1
  90.8 1.7 dec_bridge_weights.1
  92.5 1.5 collective-permute-done.13.refs_2_.refs_4_
  94.0 1.6 collective-permute-start.20
  95.9 3.3 %enc_hidden_back.1 = (bf16[256,768]{1,0:T(8,128)(2,1)}, bf16[256,1536]{1,0:T(8,128)(2,1)S(1)}, bf16[256,384]{1,0:T(8,128)(2,1)}, f32[8,128]{1,0:T(8,128)S(1)}) custom-call(s32[3]{0:T(128)S(1)} %copy-done.4, bf16[128,768]{1,0:T(8,128)(2,1)} %get-tuple-element.217.refs_1_.refs_3_, bf16[128,768]{1,0:T(8,128)(2,1)} %collective-permute-done.13.refs_2_.refs_4_, ...), custom_call_target="tpu_custom_call" | custom-call | flops 199999995904 | bytes 1 | tf_op jit(solution)/shard_map/enc_hidden_back/pallas_call | solution.py:164
  100.4 1.8 fold.3
  102.2 1.6 collective-permute-start.23
  103.8 3.6 %enc_hidden_weights.1 = (bf16[384,768]{1,0:T(8,128)(2,1)S(1)}, bf16[384,768]{1,0:T(8,128)(2,1)}, f32[8,128]{1,0:T(8,128)S(1)}) custom-call(s32[3]{0:T(128)S(1)} %copy-done.4, bf16[128,1536]{1,0:T(8,128)(2,1)S(1)} %get-tuple-element.192.refs_1_, bf16[128,1536]{1,0:T(8,128)(2,1)S(1)} %get-tuple-element.193.refs_2_, ...), custom_call_target="tpu_custom_call" | custom-call | flops 199999995904 | bytes 1 | tf_op jit(solution)/shard_map/enc_hidden_weights/pallas_call | solution.py:164
  107.4 2.0 add.34
  109.4 2.6 %collective-permute-start.21 = (bf16[384,512]{1,0:T(8,128)(2,1)}, bf16[384,512]{1,0:T(8,128)(2,1)}, u32[]{:S(2)}, u32[]{:S(2)}) collective-permute-start(bf16[384,512]{1,0:T(8,128)(2,1)} %get-tuple-element.250.refs_0_), channel_id=1, source_target_pairs={{0,4},{1,5},{2,6},{3,7},{4,0},{5,1},{6,2},{7,3},{8,12},{9,13},{10,... | collective-permute-start | bytes 1179656 | tf_op jit(solution)/shard_map/ppermute | solution.py:776
  112.4 5.8 %enc_attend_back.1 = (bf16[256,768]{1,0:T(8,128)(2,1)}, f32[256,768]{1,0:T(8,128)S(1)}, bf16[256,768]{1,0:T(8,128)(2,1)S(1)}, bf16[3,256,384]{2,1,0:T(8,128)(2,1...) custom-call(s32[3]{0:T(128)S(1)} %copy-done.4, ...), custom_call_target="tpu_custom_call" | custom-call | flops 199999995904 | bytes 1 | tf_op jit(solution)/shard_map/enc_attend_back/pallas_call | solution.py:164
  118.8 10.8 %collective-permute-done.21.refs_1_ = bf16[384,512]{1,0:T(8,128)(2,1)} collective-permute-done((bf16[384,512]{1,0:T(8,128)(2,1)}, bf16[384,512]{1,0:T(8,128)(2,1)}, u32[]{:S(2)}, u32[]{:S(2)}) %collective-permute-start.21) | collective-permute-done | bytes 393248 | tf_op jit(solution)/shard_map/ppermute | solution.py:776
  129.6 2.0 add.35
  132.3 3.3 %collective-permute-done.19.refs_1_ = bf16[384,768]{1,0:T(8,128)(2,1)} collective-permute-done((bf16[384,768]{1,0:T(8,128)(2,1)}, bf16[384,768]{1,0:T(8,128)(2,1)}, u32[]{:S(2)}, u32[]{:S(2)}) %collective-permute-start.19) | collective-permute-done | bytes 589856 | tf_op jit(solution)/shard_map/ppermute | solution.py:776
  135.6 2.1 add.36
  139.1 2.9 %enc_start_back.1 = (f32[98,1,768]{2,1,0:T(1,128)}, bf16[32,768]{1,0:T(8,128)(2,1)S(1)}, f32[8,128]{1,0:T(8,128)S(1)}) custom-call(bf16[128,768]{1,0:T(8,128)(2,1)S(1)} %copy-done.41, bf16[128,768]{1,0:T(8,128)(2,1)S(1)} %copy-done.45, bf16[256,768]{1,0:T(8,128)(2,1)} %get-tuple-element.267.refs_2_, bf16[256,768]{1,0:T(8,128)(2,1)} %collective-permute-done.29.refs_3_, ...), custom_call_target="tpu_custom_call" | custom-call | flops 199999995904 | bytes 1 | tf_op jit(solution)/shard_map/enc_start_back/pallas_call | solution.py:164
  142.0 5.1 %collective-permute-done.26.refs_14_.refs_2_ = bf16[384,512]{1,0:T(8,128)(2,1)} collective-permute-done((bf16[384,512]{1,0:T(8,128)(2,1)}, bf16[384,512]{1,0:T(8,128)(2,1)}, u32[]{:S(2)}, u32[]{:S(2)}) %collective-permute-start.26) | collective-permute-done | bytes 393248 | tf_op jit(solution)/shard_map/ppermute | solution.py:776
  147.1 1.5 collective-permute-start.28
  148.7 2.9 %last_weights.1 = (bf16[880,256]{1,0:T(8,128)(2,1)S(1)}, bf16[880,256]{1,0:T(8,128)(2,1)}, f32[8,128]{1,0:T(8,128)S(1)}) custom-call(s32[3]{0:T(128)S(1)} %copy-done.4, bf16[128,768]{1,0:T(8,128)(2,1)S(1)} %copy-done.39, bf16[128,768]{1,0:T(8,128)(2,1)S(1)} %copy-done.43, bf16[3,256,384]{2,1,0:T(8,128)(2,1)S(1)} %get-tuple-element.265.refs_3_, ...), custom_call_target="tpu_custom_call" | custom-call | flops 199999995904 | bytes 1 | tf_op jit(solution)/shard_map/last_weights/pallas_call | solution.py:164
  151.6 6.1 %collective-permute-done.28.refs_4_ = bf16[384,512]{1,0:T(8,128)(2,1)} collective-permute-done((bf16[384,512]{1,0:T(8,128)(2,1)}, bf16[384,512]{1,0:T(8,128)(2,1)}, u32[]{:S(2)}, u32[]{:S(2)}) %collective-permute-start.28) | collective-permute-done | bytes 393248 | tf_op jit(solution)/shard_map/ppermute | solution.py:776
  157.7 2.6 %pack.3 = (bf16[2,2,384,512]{3,2,1,0:T(8,128)(2,1)}, f32[8,128]{1,0:T(8,128)S(1)}) custom-call(s32[3]{0:T(128)S(1)} %copy-done.4, bf16[384,512]{1,0:T(8,128)(2,1)} %get-tuple-element.264.refs_1_, bf16[384,512]{1,0:T(8,128)(2,1)} %collective-permute-done.26.refs_14_.refs_2_, bf16[384,512]{1,0:T(8,128)(2,1)} %collective-permute-done.27.refs_3_, ...), custom_call_target="tpu_custom_call" | custom-call | flops 199999995904 | bytes 1 | tf_op jit(solution)/shard_map/pack/pallas_call | solution.py:164
  160.3 3.0 %dec_out.1 = (bf16[392,512]{1,0:T(8,128)(2,1)}, f32[8,128]{1,0:T(8,128)S(1)}) custom-call(s32[1]{0:T(128)} %bitcast.3.refs_0_, f32[416,512]{1,0:T(8,128)S(1)} %get-tuple-element.190.refs_1_, bf16[416,512]{1,0:T(8,128)(2,1)} %get-tuple-element.263.refs_2_, bf16[416,512]{1,0:T(8,128)(2,1)} %collective-permute-done.25.refs_3_, bf16[8,512]{1,0:T(8,128)(2,1)S(1)} %copy-done.23, ...), custom_call_target="tpu_custom_call" | custom-call | flops 199999995904 | bytes 1 | tf_op jit(solution)/shard_map/dec_out/pallas_call | solution.py:164
  163.3 2.0 collective-permute-done.31.refs_1_
  165.3 2.2 add.37
  168.1 5.5 %collective-permute-done.30.refs_1_ = bf16[880,256]{1,0:T(8,128)(2,1)} collective-permute-done((bf16[880,256]{1,0:T(8,128)(2,1)}, bf16[880,256]{1,0:T(8,128)(2,1)}, u32[]{:S(2)}, u32[]{:S(2)}) %collective-permute-start.30) | collective-permute-done | bytes 450592 | tf_op jit(solution)/shard_map/ppermute | solution.py:776
  173.6 1.9 add.38
  175.5 14.8 %collective-permute-done.34.refs_1_.refs_2_ = bf16[384,768]{1,0:T(8,128)(2,1)} collective-permute-done((bf16[384,768]{1,0:T(8,128)(2,1)}, bf16[384,768]{1,0:T(8,128)(2,1)}, u32[]{:S(2)}, u32[]{:S(2)}) %collective-permute-start.34) | collective-permute-done | bytes 589856 | tf_op jit(solution)/shard_map/ppermute | solution.py:776
  191.5 4.8 %dec_whole.1 = (f32[512,1024]{1,0:T(8,128)}, f32[1024,512]{1,0:T(8,128)}, f32[3,512,256]{2,1,0:T(8,128)}, f32[256,512]{1,0:T(8,128)}, f32[8,128]{1,0:T(8,128)S(1)}) custom-call(s32[3]{0:T(128)S(1)} %copy-done.4, bf16[2,2,384,512]{3,2,1,0:T(8,128)(2,1)} %get-tuple-element.286.refs_1_, bf16[2,2,384,512]{3,2,1,0:T(8,128)(2,1)} %collective-permute-done.33.refs_2_, ...), custom_call_target="tpu_custom_call" | custom-call | flops 199999995904 | bytes 1 | tf_op jit(solution)/shard_map/dec_whole/pallas_call | solution.py:164
  197.0 2.0 add.39
  199.8 7.1 %collective-permute-done.39.refs_4_ = bf16[384,768]{1,0:T(8,128)(2,1)} collective-permute-done((bf16[384,768]{1,0:T(8,128)(2,1)}, bf16[384,768]{1,0:T(8,128)(2,1)}, u32[]{:S(2)}, u32[]{:S(2)}) %collective-permute-start.39) | collective-permute-done | bytes 589856 | tf_op jit(solution)/shard_map/ppermute | solution.py:776
  206.9 3.2 %pack.4 = (bf16[2,2,384,768]{3,2,1,0:T(8,128)(2,1)}, f32[8,128]{1,0:T(8,128)S(1)}) custom-call(s32[3]{0:T(128)S(1)} %copy-done.4, bf16[384,768]{1,0:T(8,128)(2,1)} %get-tuple-element.289.refs_1_, bf16[384,768]{1,0:T(8,128)(2,1)} %collective-permute-done.34.refs_1_.refs_2_, bf16[384,768]{1,0:T(8,128)(2,1)} %collective-permute-done.38.refs_3_, ...), custom_call_target="tpu_custom_call" | custom-call | flops 199999995904 | bytes 1 | tf_op jit(solution)/shard_map/pack/pallas_call | solution.py:164
  210.1 1.7 collective-permute-start.37
  212.3 2.6 %collective-permute-done.40.refs_2_ = bf16[2,2,384,768]{3,2,1,0:T(8,128)(2,1)} collective-permute-done((bf16[2,2,384,768]{3,2,1,0:T(8,128)(2,1)}, bf16[2,2,384,768]{3,2,1,0:T(8,128)(2,1)}, u32[]{:S(2)}, u32[]{:S(2)}) %collective-permute-start.40) | collective-permute-done | bytes 2359328 | tf_op jit(solution)/shard_map/ppermute | solution.py:49
  214.9 6.7 %enc_hidden_whole.1 = (f32[768,1536]{1,0:T(8,128)}, f32[1536,768]{1,0:T(8,128)}, f32[8,128]{1,0:T(8,128)S(1)}) custom-call(s32[3]{0:T(128)S(1)} %copy-done.4, bf16[2,2,384,768]{3,2,1,0:T(8,128)(2,1)} %get-tuple-element.293.refs_1_, bf16[2,2,384,768]{3,2,1,0:T(8,128)(2,1)} %collective-permute-done.40.refs_2_, f32[8,128]{1,0:T(8,128)S(1)} %get-tuple-element.295.refs_3_), custom_call_target="tpu_custom_call" | custom-call | flops 199999995904 | bytes 1 | tf_op jit(solution)/shard_map/enc_hidden_whole/pallas_call | solution.py:164
  221.6 1.8 collective-permute-done.37.refs_4_
  223.4 1.6 pack.5
  225.1 3.7 %collective-permute-done.41.refs_2_ = bf16[2,2,880,256]{3,2,1,0:T(8,128)(2,1)S(1)} collective-permute-done((bf16[2,2,880,256]{3,2,1,0:T(8,128)(2,1)S(1)}, bf16[2,2,880,256]{3,2,1,0:T(8,128)(2,1)S(1)}, u32[]{:S(2)}, u32[]{:S(2)}) %collective-permute-start.41) | collective-permute-done | bytes 1802272 | tf_op jit(solution)/shard_map/ppermute | solution.py:49
  228.8 3.5 %last_whole.1 = (f32[3,768,384]{2,1,0:T(8,128)}, f32[384,768]{1,0:T(8,128)}, f32[6,768]{1,0:T(8,128)}, f32[1,1536]{1,0:T(1,128)S(1)}, f32[2,384]{1,0:T(2,128)}, ...) custom-call(s32[3]{0:T(128)S(1)} %copy-done.4, ...), custom_call_target="tpu_custom_call" | custom-call | flops 199999995904 | bytes 1 | tf_op jit(solution)/shard_map/last_whole/pallas_call | solution.py:164
  (177 shorter events, 15.2 us)
Async XLA Ops:
  0.7 22.8 %copy-start = (bf16[2,392,512]{2,1,0:T(8,128)(2,1)S(1)}, bf16[2,392,512]{2,1,0:T(8,128)(2,1)}, u32[]{:S(2)}) copy-start(bf16[2,392,512]{2,1,0:T(8,128)(2,1)} %param.39) | copy-start | bytes 2408452
  3.3 11.7 %copy-start.4 = (s32[3]{0:T(128)S(1)}, s32[3]{0:T(128)}, u32[]{:S(2)}) copy-start(s32[3]{0:T(128)} %pad_add_fusion.refs_0_.refs_1_) | copy-start | bytes 40
  3.3 11.7 %copy-start.9 = (bf16[768,3,384]{2,0,1:T(8,128)(2,1)S(1)}, bf16[768,3,384]{2,0,1:T(8,128)(2,1)}, u32[]{:S(2)}) copy-start(bf16[768,3,384]{2,0,1:T(8,128)(2,1)} %param.24) | copy-start | bytes 5308420
  3.4 11.7 %copy-start.15 = (bf16[384,768]{1,0:T(8,128)(2,1)S(1)}, bf16[384,768]{1,0:T(8,128)(2,1)}, u32[]{:S(2)}) copy-start(bf16[384,768]{1,0:T(8,128)(2,1)} %refs_13_.1) | copy-start | bytes 1769476
  3.4 11.7 %copy-start.20 = (bf16[6,768]{1,0:T(8,128)(2,1)S(1)}, bf16[6,768]{1,0:T(8,128)(2,1)}, u32[]{:S(2)}) copy-start(bf16[6,768]{1,0:T(8,128)(2,1)} %refs_4_.6) | copy-start | bytes 27652
  3.4 11.7 %copy-start.24 = (bf16[2,384]{1,0:T(2,128)(2,1)S(1)}, bf16[2,384]{1,0:T(2,128)(2,1)}, u32[]{:S(2)}) copy-start(bf16[2,384]{1,0:T(2,128)(2,1)} %refs_4_.5) | copy-start | bytes 4612
  7.9 7.1 %collective-permute-start.1 = (bf16[98,768]{1,0:T(8,128)(2,1)S(1)}, bf16[98,768]{1,0:T(8,128)(2,1)S(1)}, u32[]{:S(2)}, u32[]{:S(2)}) collective-permute-start(bf16[98,768]{1,0:T(8,128)(2,1)S(1)} %bitcast.26), channel_id=1, source_target_pairs={{0,1},{1,0},{2,3},{3,2},{4,5},{5,4},{6,7},{7,6},{8,9},{9,8},{10,11... | collective-permute-start | bytes 451592 | tf_op jit(solution)/shard_map/ppermute | solution.py:776
  10.9 7.6 %collective-permute-start = (bf16[128,768]{1,0:T(8,128)(2,1)}, bf16[128,768]{1,0:T(8,128)(2,1)}, u32[]{:S(2)}, u32[]{:S(2)}) collective-permute-start(bf16[128,768]{1,0:T(8,128)(2,1)} %get-tuple-element.169.refs_3_), channel_id=1, source_target_pairs={{0,8},{8,0},{1,9},{9,1},{2,10},{10,2},{3,11},{11,3},{4,12},{12,4},... | collective-permute-start | bytes 589832 | tf_op jit(solution)/shard_map/ppermute | solution.py:49
  18.5 17.9 %copy-start.42 = (bf16[128,768]{1,0:T(8,128)(2,1)}, bf16[128,768]{1,0:T(8,128)(2,1)S(1)}, u32[]{:S(2)}) copy-start(bf16[128,768]{1,0:T(8,128)(2,1)S(1)} %get-tuple-element.183.refs_7_.refs_2_) | copy-start | bytes 589828
  18.5 17.9 %copy-start.44 = (bf16[128,768]{1,0:T(8,128)(2,1)}, bf16[128,768]{1,0:T(8,128)(2,1)S(1)}, u32[]{:S(2)}) copy-start(bf16[128,768]{1,0:T(8,128)(2,1)S(1)} %get-tuple-element.181.refs_1_) | copy-start | bytes 589828
  18.5 17.9 %copy-start.48 = (bf16[128,384]{1,0:T(8,128)(2,1)}, bf16[128,384]{1,0:T(8,128)(2,1)S(1)}, u32[]{:S(2)}) copy-start(bf16[128,384]{1,0:T(8,128)(2,1)S(1)} %get-tuple-element.184.refs_8_.refs_5_) | copy-start | bytes 294916
  18.6 10.9 %copy-start.12 = (bf16[512,3,256]{2,0,1:T(8,128)(2,1)S(1)}, bf16[512,3,256]{2,0,1:T(8,128)(2,1)}, u32[]{:S(2)}) copy-start(bf16[512,3,256]{2,0,1:T(8,128)(2,1)} %param.33) | copy-start | bytes 2359300
  18.6 10.9 %copy-start.14 = (bf16[768,512]{1,0:T(8,128)(2,1)S(1)}, bf16[768,512]{1,0:T(8,128)(2,1)}, u32[]{:S(2)}) copy-start(bf16[768,512]{1,0:T(8,128)(2,1)} %refs_7_.4) | copy-start | bytes 2359300
  18.6 10.9 %copy-start.16 = (bf16[256,512]{1,0:T(8,128)(2,1)S(1)}, bf16[256,512]{1,0:T(8,128)(2,1)}, u32[]{:S(2)}) copy-start(bf16[256,512]{1,0:T(8,128)(2,1)} %refs_9_.3) | copy-start | bytes 786436
  18.6 10.9 %copy-start.18 = (bf16[196,512]{1,0:T(8,128)(2,1)S(1)}, bf16[196,512]{1,0:T(8,128)(2,1)}, u32[]{:S(2)}) copy-start(bf16[196,512]{1,0:T(8,128)(2,1)} %refs_8_.2) | copy-start | bytes 602116
  18.7 10.9 %copy-start.21 = (bf16[8,512]{1,0:T(8,128)(2,1)S(1)}, bf16[8,512]{1,0:T(8,128)(2,1)}, u32[]{:S(2)}) copy-start(bf16[8,512]{1,0:T(8,128)(2,1)} %refs_4_.7) | copy-start | bytes 24580
  18.7 10.9 %copy-start.25 = (bf16[2,256]{1,0:T(2,128)(2,1)S(1)}, bf16[2,256]{1,0:T(2,128)(2,1)}, u32[]{:S(2)}) copy-start(bf16[2,256]{1,0:T(2,128)(2,1)} %refs_10_.1) | copy-start | bytes 3076
  21.7 12.9 %copy-start.32 = (f32[128,768]{1,0:T(8,128)}, f32[128,768]{1,0:T(8,128)S(1)}, u32[]{:S(2)}) copy-start(f32[128,768]{1,0:T(8,128)S(1)} %get-tuple-element.175.refs_2_.refs_1_) | copy-start | bytes 1179652
  21.7 7.8 %collective-permute-start.2 = (bf16[128,768]{1,0:T(8,128)(2,1)S(1)}, bf16[128,768]{1,0:T(8,128)(2,1)S(1)}, u32[]{:S(2)}, u32[]{:S(2)}) collective-permute-start(bf16[128,768]{1,0:T(8,128)(2,1)S(1)} %get-tuple-element.176.refs_3_), channel_id=1, source_target_pairs={{0,8},{8,0},{1,9},{9,1},{2,10},{10,2},{3,11},{11,3},{4,12},{12,4},... | collective-permute-start | bytes 589832 | tf_op jit(solution)/shard_map/ppermute | solution.py:49
  23.4 11.1 %copy-start.2 = (s32[2,64]{1,0:T(2,128)}, s32[2,64]{1,0:T(2,128)S(1)}, u32[]{:S(2)}) copy-start(s32[2,64]{1,0:T(2,128)S(1)} %pad.4.refs_1_) | copy-start | bytes 1540
  23.5 12.9 %collective-permute-start.5 = (bf16[128,768]{1,0:T(8,128)(2,1)}, bf16[128,768]{1,0:T(8,128)(2,1)}, u32[]{:S(2)}, u32[]{:S(2)}) collective-permute-start(bf16[128,768]{1,0:T(8,128)(2,1)} %get-tuple-element.182.refs_3_), channel_id=1, source_target_pairs={{0,8},{8,0},{1,9},{9,1},{2,10},{10,2},{3,11},{11,3},{4,12},{12,4},... | collective-permute-start | bytes 589832 | tf_op jit(solution)/shard_map/ppermute | solution.py:49
  23.9 15.6 %collective-permute-start.6 = (bf16[128,1920]{1,0:T(8,128)(2,1)}, bf16[128,1920]{1,0:T(8,128)(2,1)}, u32[]{:S(2)}, u32[]{:S(2)}) collective-permute-start(bf16[128,1920]{1,0:T(8,128)(2,1)} %get-tuple-element.187), channel_id=1, source_target_pairs={{0,16},{16,0},{1,17},{17,1},{2,18},{18,2},{3,19},{19,3},{4,20},{20... | collective-permute-start | bytes 1474568 | tf_op jit(solution)/shard_map/ppermute | solution.py:49
  34.5 12.7 %copy-start.26 = (f32[416,512]{1,0:T(8,128)}, f32[416,512]{1,0:T(8,128)S(1)}, u32[]{:S(2)}) copy-start(f32[416,512]{1,0:T(8,128)S(1)} %get-tuple-element.179.refs_2_) | copy-start | bytes 2555908
  34.5 30.2 %copy-start.30 = (bf16[416,512]{1,0:T(8,128)(2,1)}, bf16[416,512]{1,0:T(8,128)(2,1)S(1)}, u32[]{:S(2)}) copy-start(bf16[416,512]{1,0:T(8,128)(2,1)S(1)} %get-tuple-element.198.refs_10_.refs_1_) | copy-start | bytes 1277956
  34.5 30.2 %copy-start.35 = (bf16[416,256]{1,0:T(8,128)(2,1)}, bf16[416,256]{1,0:T(8,128)(2,1)S(1)}, u32[]{:S(2)}) copy-start(bf16[416,256]{1,0:T(8,128)(2,1)S(1)} %get-tuple-element.199.refs_11_.refs_3_) | copy-start | bytes 638980
  34.6 20.3 %collective-permute-start.3 = (bf16[98,768]{1,0:T(8,128)(2,1)}, bf16[98,768]{1,0:T(8,128)(2,1)}, u32[]{:S(2)}, u32[]{:S(2)}) collective-permute-start(bf16[98,768]{1,0:T(8,128)(2,1)} %get-tuple-element.178.refs_1_), channel_id=1, source_target_pairs={{0,16},{16,0},{1,17},{17,1},{2,18},{18,2},{3,19},{19,3},{4,20},{20... | collective-permute-start | bytes 451592 | tf_op jit(solution)/shard_map/ppermute | solution.py:49
  34.6 12.5 %collective-permute-start.4 = (bf16[416,512]{1,0:T(8,128)(2,1)}, bf16[416,512]{1,0:T(8,128)(2,1)}, u32[]{:S(2)}, u32[]{:S(2)}) collective-permute-start(bf16[416,512]{1,0:T(8,128)(2,1)} %get-tuple-element.180.refs_3_), channel_id=1, source_target_pairs={{0,8},{8,0},{1,9},{9,1},{2,10},{10,2},{3,11},{11,3},{4,12},{12,4},... | collective-permute-start | bytes 1277960 | tf_op jit(solution)/shard_map/ppermute | solution.py:49
  36.4 10.7 %copy-start.10 = (bf16[512,1024]{1,0:T(8,128)(2,1)S(1)}, bf16[512,1024]{1,0:T(8,128)(2,1)}, u32[]{:S(2)}) copy-start(bf16[512,1024]{1,0:T(8,128)(2,1)} %refs_6_.4) | copy-start | bytes 3145732
  36.5 10.7 %copy-start.11 = (bf16[1024,512]{1,0:T(8,128)(2,1)S(1)}, bf16[1024,512]{1,0:T(8,128)(2,1)}, u32[]{:S(2)}) copy-start(bf16[1024,512]{1,0:T(8,128)(2,1)} %refs_8_.3) | copy-start | bytes 3145732
  39.3 17.7 %collective-permute-start.9 = (bf16[128,1920]{1,0:T(8,128)(2,1)}, bf16[128,1920]{1,0:T(8,128)(2,1)}, u32[]{:S(2)}, u32[]{:S(2)}) collective-permute-start(bf16[128,1920]{1,0:T(8,128)(2,1)} %get-tuple-element.205), channel_id=1, source_target_pairs={{0,16},{16,0},{1,17},{17,1},{2,18},{18,2},{3,19},{19,3},{4,20},{20... | collective-permute-start | bytes 1474568 | tf_op jit(solution)/shard_map/ppermute | solution.py:49
  53.1 11.7 %collective-permute-start.7 = (bf16[416,512]{1,0:T(8,128)(2,1)}, bf16[416,512]{1,0:T(8,128)(2,1)}, u32[]{:S(2)}, u32[]{:S(2)}) collective-permute-start(bf16[416,512]{1,0:T(8,128)(2,1)} %get-tuple-element.195.refs_3_), channel_id=1, source_target_pairs={{0,8},{8,0},{1,9},{9,1},{2,10},{10,2},{3,11},{11,3},{4,12},{12,4},... | collective-permute-start | bytes 1277960 | tf_op jit(solution)/shard_map/ppermute | solution.py:49
  54.8 4.2 %collective-permute-start.8 = (bf16[416,2304]{1,0:T(8,128)(2,1)}, bf16[416,2304]{1,0:T(8,128)(2,1)}, u32[]{:S(2)}, u32[]{:S(2)}) collective-permute-start(bf16[416,2304]{1,0:T(8,128)(2,1)} %get-tuple-element.203), channel_id=1, source_target_pairs={{0,16},{16,0},{1,17},{17,1},{2,18},{18,2},{3,19},{19,3},{4,20},{20... | collective-permute-start | bytes 5750792 | tf_op jit(solution)/shard_map/ppermute | solution.py:49
  62.8 14.3 %collective-permute-start.12 = (bf16[2,256,512]{2,1,0:T(8,128)(2,1)}, bf16[2,256,512]{2,1,0:T(8,128)(2,1)}, u32[]{:S(2)}, u32[]{:S(2)}) collective-permute-start(bf16[2,256,512]{2,1,0:T(8,128)(2,1)} %get-tuple-element.213), channel_id=1, source_target_pairs={{0,1},{1,0},{2,3},{3,2},{4,5},{5,4},{6,7},{7,6},{8,9},{9,8},{10,11... | collective-permute-start | bytes 1572872 | tf_op jit(solution)/shard_map/ppermute | solution.py:776
  71.2 11.5 %collective-permute-start.10 = (bf16[416,512]{1,0:T(8,128)(2,1)}, bf16[416,512]{1,0:T(8,128)(2,1)}, u32[]{:S(2)}, u32[]{:S(2)}) collective-permute-start(bf16[416,512]{1,0:T(8,128)(2,1)} %get-tuple-element.207.refs_3_), channel_id=1, source_target_pairs={{0,8},{8,0},{1,9},{9,1},{2,10},{10,2},{3,11},{11,3},{4,12},{12,4},... | collective-permute-start | bytes 1277960 | tf_op jit(solution)/shard_map/ppermute | solution.py:49
  72.9 5.4 %collective-permute-start.11 = (bf16[416,1536]{1,0:T(8,128)(2,1)}, bf16[416,1536]{1,0:T(8,128)(2,1)}, u32[]{:S(2)}, u32[]{:S(2)}) collective-permute-start(bf16[416,1536]{1,0:T(8,128)(2,1)} %get-tuple-element.211), channel_id=1, source_target_pairs={{0,16},{16,0},{1,17},{17,1},{2,18},{18,2},{3,19},{19,3},{4,20},{20... | collective-permute-start | bytes 3833864 | tf_op jit(solution)/shard_map/ppermute | solution.py:49
  81.2 7.8 %collective-permute-start.14 = (bf16[2,128,512]{2,1,0:T(8,128)(2,1)}, bf16[2,128,512]{2,1,0:T(8,128)(2,1)}, u32[]{:S(2)}, u32[]{:S(2)}) collective-permute-start(bf16[2,128,512]{2,1,0:T(8,128)(2,1)} %get-tuple-element.227), channel_id=1, source_target_pairs={{0,1},{1,0},{2,3},{3,2},{4,5},{5,4},{6,7},{7,6},{8,9},{9,8},{10,11... | collective-permute-start | bytes 786440 | tf_op jit(solution)/shard_map/ppermute | solution.py:776
  86.4 9.5 %collective-permute-start.15 = (bf16[128,768]{1,0:T(8,128)(2,1)}, bf16[128,768]{1,0:T(8,128)(2,1)}, u32[]{:S(2)}, u32[]{:S(2)}) collective-permute-start(bf16[128,768]{1,0:T(8,128)(2,1)} %get-tuple-element.217.refs_1_.refs_3_), channel_id=1, source_target_pairs={{0,16},{16,0},{1,17},{17,1},{2,18},{18,2},{3,19},{19,3},{4,20},{20... | collective-permute-start | bytes 589832 | tf_op jit(solution)/shard_map/ppermute | solution.py:49
  86.4 7.6 %collective-permute-start.13 = (bf16[128,768]{1,0:T(8,128)(2,1)}, bf16[128,768]{1,0:T(8,128)(2,1)}, u32[]{:S(2)}, u32[]{:S(2)}) collective-permute-start(bf16[128,768]{1,0:T(8,128)(2,1)} %get-tuple-element.217.refs_1_.refs_3_), channel_id=1, source_target_pairs={{0,1},{1,0},{2,3},{3,2},{4,5},{5,4},{6,7},{7,6},{8,9},{9,8},{10,11... | collective-permute-start | bytes 589832 | tf_op jit(solution)/shard_map/ppermute | solution.py:776
  94.0 6.4 %collective-permute-start.16 = (bf16[128,768]{1,0:T(8,128)(2,1)}, bf16[128,768]{1,0:T(8,128)(2,1)}, u32[]{:S(2)}, u32[]{:S(2)}) collective-permute-start(bf16[128,768]{1,0:T(8,128)(2,1)} %collective-permute-done.13.refs_2_.refs_4_), channel_id=1, source_target_pairs={{0,16},{16,0},{1,17},{17,1},{2,18},{18,2},{3,19},{19,3},{4,20},{20... | collective-permute-start | bytes 589832 | tf_op jit(solution)/shard_map/ppermute | solution.py:49
  94.0 13.4 %collective-permute-start.20 = (bf16[384,512]{1,0:T(8,128)(2,1)}, bf16[384,512]{1,0:T(8,128)(2,1)}, u32[]{:S(2)}, u32[]{:S(2)}) collective-permute-start(bf16[384,512]{1,0:T(8,128)(2,1)} %get-tuple-element.248), channel_id=1, source_target_pairs={{0,2},{1,3},{2,0},{3,1},{4,6},{5,7},{6,4},{7,5},{8,10},{9,11},{10,... | collective-permute-start | bytes 1179656 | tf_op jit(solution)/shard_map/ppermute | solution.py:776
  95.6 4.8 %collective-permute-start.18 = (bf16[2,2,128,512]{3,2,1,0:T(8,128)(2,1)}, bf16[2,2,128,512]{3,2,1,0:T(8,128)(2,1)}, u32[]{:S(2)}, u32[]{:S(2)}) collective-permute-start(bf16[2,2,128,512]{3,2,1,0:T(8,128)(2,1)} %get-tuple-element.242), channel_id=1, source_target_pairs={{0,16},{16,0},{1,17},{17,1},{2,18},{18,2},{3,19},{19,3},{4,20},{20... | collective-permute-start | bytes 1572872 | tf_op jit(solution)/shard_map/ppermute | solution.py:49
  99.2 4.6 %collective-permute-start.17 = (bf16[256,384]{1,0:T(8,128)(2,1)}, bf16[256,384]{1,0:T(8,128)(2,1)}, u32[]{:S(2)}, u32[]{:S(2)}) collective-permute-start(bf16[256,384]{1,0:T(8,128)(2,1)} %get-tuple-element.240), channel_id=1, source_target_pairs={{0,16},{16,0},{1,17},{17,1},{2,18},{18,2},{3,19},{19,3},{4,20},{20... | collective-permute-start | bytes 589832 | tf_op jit(solution)/shard_map/ppermute | solution.py:49
  99.5 12.9 %collective-permute-start.22 = (bf16[256,768]{1,0:T(8,128)(2,1)}, bf16[256,768]{1,0:T(8,128)(2,1)}, u32[]{:S(2)}, u32[]{:S(2)}) collective-permute-start(bf16[256,768]{1,0:T(8,128)(2,1)} %get-tuple-element.252.refs_5_), channel_id=1, source_target_pairs={{0,8},{8,0},{1,9},{9,1},{2,10},{10,2},{3,11},{11,3},{4,12},{12,4},... | collective-permute-start | bytes 1179656 | tf_op jit(solution)/shard_map/ppermute | solution.py:49
  102.2 10.2 %collective-permute-start.23 = (bf16[2,128,512]{2,1,0:T(8,128)(2,1)}, bf16[2,128,512]{2,1,0:T(8,128)(2,1)}, u32[]{:S(2)}, u32[]{:S(2)}) collective-permute-start(bf16[2,128,512]{2,1,0:T(8,128)(2,1)} %get-tuple-element.258), channel_id=1, source_target_pairs={{0,1},{1,0},{2,3},{3,2},{4,5},{5,4},{6,7},{7,6},{8,9},{9,8},{10,11... | collective-permute-start | bytes 786440 | tf_op jit(solution)/shard_map/ppermute | solution.py:776
  109.4 20.3 %collective-permute-start.21 = (bf16[384,512]{1,0:T(8,128)(2,1)}, bf16[384,512]{1,0:T(8,128)(2,1)}, u32[]{:S(2)}, u32[]{:S(2)}) collective-permute-start(bf16[384,512]{1,0:T(8,128)(2,1)} %get-tuple-element.250.refs_0_), channel_id=1, source_target_pairs={{0,4},{1,5},{2,6},{3,7},{4,0},{5,1},{6,2},{7,3},{8,12},{9,13},{10,... | collective-permute-start | bytes 1179656 | tf_op jit(solution)/shard_map/ppermute | solution.py:776
  112.0 23.6 %collective-permute-start.19 = (bf16[384,768]{1,0:T(8,128)(2,1)}, bf16[384,768]{1,0:T(8,128)(2,1)}, u32[]{:S(2)}, u32[]{:S(2)}) collective-permute-start(bf16[384,768]{1,0:T(8,128)(2,1)} %get-tuple-element.246), channel_id=1, source_target_pairs={{0,2},{1,3},{2,0},{3,1},{4,6},{5,7},{6,4},{7,5},{8,10},{9,11},{10,... | collective-permute-start | bytes 1769480 | tf_op jit(solution)/shard_map/ppermute | solution.py:776
  118.2 17.4 %collective-permute-start.24 = (bf16[256,768]{1,0:T(8,128)(2,1)}, bf16[256,768]{1,0:T(8,128)(2,1)}, u32[]{:S(2)}, u32[]{:S(2)}) collective-permute-start(bf16[256,768]{1,0:T(8,128)(2,1)} %get-tuple-element.261), channel_id=1, source_target_pairs={{0,16},{16,0},{1,17},{17,1},{2,18},{18,2},{3,19},{19,3},{4,20},{20... | collective-permute-start | bytes 1179656 | tf_op jit(solution)/shard_map/ppermute | solution.py:49
  118.2 20.8 %collective-permute-start.29 = (bf16[256,768]{1,0:T(8,128)(2,1)}, bf16[256,768]{1,0:T(8,128)(2,1)}, u32[]{:S(2)}, u32[]{:S(2)}) collective-permute-start(bf16[256,768]{1,0:T(8,128)(2,1)} %get-tuple-element.267.refs_2_), channel_id=1, source_target_pairs={{0,8},{8,0},{1,9},{9,1},{2,10},{10,2},{3,11},{11,3},{4,12},{12,4},... | collective-permute-start | bytes 1179656 | tf_op jit(solution)/shard_map/ppermute | solution.py:49
  131.6 20.0 %collective-permute-start.27 = (bf16[384,512]{1,0:T(8,128)(2,1)}, bf16[384,512]{1,0:T(8,128)(2,1)}, u32[]{:S(2)}, u32[]{:S(2)}) collective-permute-start(bf16[384,512]{1,0:T(8,128)(2,1)} %get-tuple-element.264.refs_1_), channel_id=1, source_target_pairs={{0,1},{1,0},{2,3},{3,2},{4,5},{5,4},{6,7},{7,6},{8,9},{9,8},{10,11... | collective-permute-start | bytes 1179656 | tf_op jit(solution)/shard_map/ppermute | solution.py:776
  132.2 14.9 %collective-permute-start.26 = (bf16[384,512]{1,0:T(8,128)(2,1)}, bf16[384,512]{1,0:T(8,128)(2,1)}, u32[]{:S(2)}, u32[]{:S(2)}) collective-permute-start(bf16[384,512]{1,0:T(8,128)(2,1)} %get-tuple-element.264.refs_1_), channel_id=1, source_target_pairs={{0,2},{1,3},{2,0},{3,1},{4,6},{5,7},{6,4},{7,5},{8,10},{9,11},{10,... | collective-permute-start | bytes 1179656 | tf_op jit(solution)/shard_map/ppermute | solution.py:776
  137.7 22.6 %collective-permute-start.25 = (bf16[416,512]{1,0:T(8,128)(2,1)}, bf16[416,512]{1,0:T(8,128)(2,1)}, u32[]{:S(2)}, u32[]{:S(2)}) collective-permute-start(bf16[416,512]{1,0:T(8,128)(2,1)} %get-tuple-element.263.refs_2_), channel_id=1, source_target_pairs={{0,8},{8,0},{1,9},{9,1},{2,10},{10,2},{3,11},{11,3},{4,12},{12,4},... | collective-permute-start | bytes 1277960 | tf_op jit(solution)/shard_map/ppermute | solution.py:49
  138.0 27.2 %collective-permute-start.31 = (bf16[384,768]{1,0:T(8,128)(2,1)}, bf16[384,768]{1,0:T(8,128)(2,1)}, u32[]{:S(2)}, u32[]{:S(2)}) collective-permute-start(bf16[384,768]{1,0:T(8,128)(2,1)} %get-tuple-element.282.refs_0_), channel_id=1, source_target_pairs={{0,4},{1,5},{2,6},{3,7},{4,0},{5,1},{6,2},{7,3},{8,12},{9,13},{10,... | collective-permute-start | bytes 1769480 | tf_op jit(solution)/shard_map/ppermute | solution.py:776
  147.1 10.5 %collective-permute-start.28 = (bf16[384,512]{1,0:T(8,128)(2,1)}, bf16[384,512]{1,0:T(8,128)(2,1)}, u32[]{:S(2)}, u32[]{:S(2)}) collective-permute-start(bf16[384,512]{1,0:T(8,128)(2,1)} %collective-permute-done.26.refs_14_.refs_2_), channel_id=1, source_target_pairs={{0,1},{1,0},{2,3},{3,2},{4,5},{5,4},{6,7},{7,6},{8,9},{9,8},{10,11... | collective-permute-start | bytes 1179656 | tf_op jit(solution)/shard_map/ppermute | solution.py:776
  151.6 22.1 %collective-permute-start.30 = (bf16[880,256]{1,0:T(8,128)(2,1)}, bf16[880,256]{1,0:T(8,128)(2,1)}, u32[]{:S(2)}, u32[]{:S(2)}) collective-permute-start(bf16[880,256]{1,0:T(8,128)(2,1)} %get-tuple-element.281), channel_id=1, source_target_pairs={{0,2},{1,3},{2,0},{3,1},{4,6},{5,7},{6,4},{7,5},{8,10},{9,11},{10,... | collective-permute-start | bytes 1351688 | tf_op jit(solution)/shard_map/ppermute | solution.py:776
  160.3 31.3 %collective-permute-start.33 = (bf16[2,2,384,512]{3,2,1,0:T(8,128)(2,1)}, bf16[2,2,384,512]{3,2,1,0:T(8,128)(2,1)}, u32[]{:S(2)}, u32[]{:S(2)}) collective-permute-start(bf16[2,2,384,512]{3,2,1,0:T(8,128)(2,1)} %get-tuple-element.286.refs_1_), channel_id=1, source_target_pairs={{0,16},{16,0},{1,17},{17,1},{2,18},{18,2},{3,19},{19,3},{4,20},{20... | collective-permute-start | bytes 4718600 | tf_op jit(solution)/shard_map/ppermute | solution.py:49
  167.5 32.3 %collective-permute-start.38 = (bf16[384,768]{1,0:T(8,128)(2,1)}, bf16[384,768]{1,0:T(8,128)(2,1)}, u32[]{:S(2)}, u32[]{:S(2)}) collective-permute-start(bf16[384,768]{1,0:T(8,128)(2,1)} %get-tuple-element.289.refs_1_), channel_id=1, source_target_pairs={{0,1},{1,0},{2,3},{3,2},{4,5},{5,4},{6,7},{7,6},{8,9},{9,8},{10,11... | collective-permute-start | bytes 1769480 | tf_op jit(solution)/shard_map/ppermute | solution.py:776
  168.1 22.2 %collective-permute-start.34 = (bf16[384,768]{1,0:T(8,128)(2,1)}, bf16[384,768]{1,0:T(8,128)(2,1)}, u32[]{:S(2)}, u32[]{:S(2)}) collective-permute-start(bf16[384,768]{1,0:T(8,128)(2,1)} %get-tuple-element.289.refs_1_), channel_id=1, source_target_pairs={{0,2},{1,3},{2,0},{3,1},{4,6},{5,7},{6,4},{7,5},{8,10},{9,11},{10,... | collective-permute-start | bytes 1769480 | tf_op jit(solution)/shard_map/ppermute | solution.py:776
  175.5 21.4 %collective-permute-start.32 = (bf16[880,256]{1,0:T(8,128)(2,1)}, bf16[880,256]{1,0:T(8,128)(2,1)}, u32[]{:S(2)}, u32[]{:S(2)}) collective-permute-start(bf16[880,256]{1,0:T(8,128)(2,1)} %get-tuple-element.285.refs_0_), channel_id=1, source_target_pairs={{0,4},{1,5},{2,6},{3,7},{4,0},{5,1},{6,2},{7,3},{8,12},{9,13},{10,... | collective-permute-start | bytes 1351688 | tf_op jit(solution)/shard_map/ppermute | solution.py:776
  190.3 16.6 %collective-permute-start.39 = (bf16[384,768]{1,0:T(8,128)(2,1)}, bf16[384,768]{1,0:T(8,128)(2,1)}, u32[]{:S(2)}, u32[]{:S(2)}) collective-permute-start(bf16[384,768]{1,0:T(8,128)(2,1)} %collective-permute-done.34.refs_1_.refs_2_), channel_id=1, source_target_pairs={{0,1},{1,0},{2,3},{3,2},{4,5},{5,4},{6,7},{7,6},{8,9},{9,8},{10,11... | collective-permute-start | bytes 1769480 | tf_op jit(solution)/shard_map/ppermute | solution.py:776
  199.0 22.6 %collective-permute-start.36 = (bf16[880,256]{1,0:T(8,128)(2,1)}, bf16[880,256]{1,0:T(8,128)(2,1)}, u32[]{:S(2)}, u32[]{:S(2)}) collective-permute-start(bf16[880,256]{1,0:T(8,128)(2,1)} %get-tuple-element.291.refs_1_), channel_id=1, source_target_pairs={{0,1},{1,0},{2,3},{3,2},{4,5},{5,4},{6,7},{7,6},{8,9},{9,8},{10,11... | collective-permute-start | bytes 1351688 | tf_op jit(solution)/shard_map/ppermute | solution.py:776
  199.8 10.3 %collective-permute-start.35 = (bf16[880,256]{1,0:T(8,128)(2,1)}, bf16[880,256]{1,0:T(8,128)(2,1)}, u32[]{:S(2)}, u32[]{:S(2)}) collective-permute-start(bf16[880,256]{1,0:T(8,128)(2,1)} %get-tuple-element.291.refs_1_), channel_id=1, source_target_pairs={{0,2},{1,3},{2,0},{3,1},{4,6},{5,7},{6,4},{7,5},{8,10},{9,11},{10,... | collective-permute-start | bytes 1351688 | tf_op jit(solution)/shard_map/ppermute | solution.py:776
  210.0 4.9 %collective-permute-start.40 = (bf16[2,2,384,768]{3,2,1,0:T(8,128)(2,1)}, bf16[2,2,384,768]{3,2,1,0:T(8,128)(2,1)}, u32[]{:S(2)}, u32[]{:S(2)}) collective-permute-start(bf16[2,2,384,768]{3,2,1,0:T(8,128)(2,1)} %get-tuple-element.293.refs_1_), channel_id=1, source_target_pairs={{0,16},{16,0},{1,17},{17,1},{2,18},{18,2},{3,19},{19,3},{4,20},{20... | collective-permute-start | bytes 7077896 | tf_op jit(solution)/shard_map/ppermute | solution.py:49
  210.1 13.4 %collective-permute-start.37 = (bf16[880,256]{1,0:T(8,128)(2,1)}, bf16[880,256]{1,0:T(8,128)(2,1)}, u32[]{:S(2)}, u32[]{:S(2)}) collective-permute-start(bf16[880,256]{1,0:T(8,128)(2,1)} %collective-permute-done.35.refs_1_.refs_2_), channel_id=1, source_target_pairs={{0,1},{1,0},{2,3},{3,2},{4,5},{5,4},{6,7},{7,6},{8,9},{9,8},{10,11... | collective-permute-start | bytes 1351688 | tf_op jit(solution)/shard_map/ppermute | solution.py:776
  225.0 3.8 %collective-permute-start.41 = (bf16[2,2,880,256]{3,2,1,0:T(8,128)(2,1)S(1)}, bf16[2,2,880,256]{3,2,1,0:T(8,128)(2,1)S(1)}, u32[]{:S(2)}, u32[]{:S(2)}) collective-permute-start(bf16[2,2,880,256]{3,2,1,0:T(8,128)(2,1)S(1)} %get-tuple-element.297.refs_1_), channel_id=1, source_target_pairs={{0,16},{16,0},{1,17},{17,1},{2,18},{18,2},{3,19},{19,3},{4,20},{20... | collective-permute-start | bytes 5406728 | tf_op jit(solution)/shard_map/ppermute | solution.py:49
  (34 other events, 173.8 us)

commit v2 on v1

--- a/solution.py
+++ b/solution.py
@@ -168,7 +168,7 @@
         out_specs=[pl.BlockSpec(memory_space=pltpu.VMEM)] * (len(outs) + 1),
         scratch_shapes=scratch,
         compiler_params=pltpu.CompilerParams(vmem_limit_bytes=memory * MIB),
-        cost_estimate=pl.CostEstimate(flops=2 * 10**11, bytes_accessed=1, transcendentals=0),
+        cost_estimate=pl.CostEstimate(flops=30000000000, bytes_accessed=1, transcendentals=0),
         name=name,
     )(*arguments, *before)
     order.append(results[-1])
@@ -917,7 +917,7 @@
     enc_heads, dec_heads = LANES // enc_size, LANES // dec_size
     enc_qkv, dec_qkv = jnp.transpose(enc_qkv, (1, 0, 2)), jnp.transpose(dec_qkv, (1, 0, 2))
     enc_fc1_bias, dec_fc1_bias = enc_fc1_bias[None], dec_fc1_bias[None]
-    own_in = pick(enc_in, core)
+    raw_in = enc_in
     enc_in = jnp.transpose(enc_in, (1, 0, 2))
     keep = jnp.pad(pick(keep_index, core), ((0, 0), (0, PAD_E - VIS)), constant_values=-1)
     cot = pick(dec_cot, core)
@@ -944,8 +944,8 @@
 
     part, x, normed, proj, weights, mix = enc_attend(enc_in, 60)
     part_other = swap(part, "tensor")
-    own_in, x = lax.optimization_barrier((own_in, x))
-    side_in = flip(own_in, 1)
+    raw_in, x = lax.optimization_barrier((raw_in, x))
+    side_in = flip(pick(raw_in, core), 1)
     side_part, side_x, side_normed, side_proj, side_weights, side_mix = enc_attend(side_in)
     part_two, middle, normed_two, hidden, slope, forward_send = call(
         enc_hidden_kernel,

time: 234 us -> 214 us (0.915)
  Pallas kernels: 106 us -> 61.8 us
  waiting for transfers between devices: 88.2 us -> 106 us
  starting transfers between devices: 32.2 us -> 39.8 us
    pallas_call x35, Pallas kernels: 106 us -> 61.8 us  [kernel_call(): pl.pallas_call(run, out_shape=[jax.ShapeDtypeStruct(x.shape, x.dtype) for...]
    ppermute x20, waiting for transfers between devices: 65.9 us -> 79.3 us  [flip(): lax.ppermute(value, 'dp', [(i, i ^ step) for i in range(lax.axis_size('dp...]
    ppermute x22, waiting for transfers between devices: 22.3 us -> 26.6 us  [swap(): lax.ppermute(value, axis, [(i, i ^ 1) for i in range(lax.axis_size(axis))])]
    ppermute x20, starting transfers between devices: 20.7 us -> 24.8 us  [flip(): lax.ppermute(value, 'dp', [(i, i ^ step) for i in range(lax.axis_size('dp...]
    ppermute x22, starting transfers between devices: 11.5 us -> 14.9 us  [swap(): lax.ppermute(value, axis, [(i, i ^ 1) for i in range(lax.axis_size(axis))])]
  transfers between devices with their start and end apart: 42 -> 42, of which waited for: 19 -> 22; matrix products, arithmetic and copies ran while one was open for 0% -> 0% of each run, Pallas kernels for 40% -> 24%
where the time goes in v2:
time: 214 us; the launch traced here: 212 us
  waiting for transfers between devices  106 us (50%)
  Pallas kernels  61.8 us (29%)
  starting transfers between devices  39.8 us (19%)
    ppermute x20, waiting for transfers between devices, flip(): lax.ppermute(value, 'dp', [(i, i ^ step) for i in range(lax.axis_size('dp...  79.3 us
    pallas_call x35, Pallas kernels, kernel_call(): pl.pallas_call(run, out_shape=[jax.ShapeDtypeStruct(x.shape, x.dtype) for...  61.8 us
    ppermute x22, waiting for transfers between devices, swap(): lax.ppermute(value, axis, [(i, i ^ 1) for i in range(lax.axis_size(axis))])  26.6 us
    ppermute x20, starting transfers between devices, flip(): lax.ppermute(value, 'dp', [(i, i ^ step) for i in range(lax.axis_size('dp...  24.8 us
    ppermute x22, starting transfers between devices, swap(): lax.ppermute(value, axis, [(i, i ^ 1) for i in range(lax.axis_size(axis))])  14.9 us
  transfers between devices with their start and end apart: 42, of which 22 were waited for; matrix products, arithmetic and copies ran while one was open for 0% of the time, Pallas kernels for 24%

profile of v2, /device:TPU:0, one launch (start us, length us, event | category | flops | bytes accessed | tf_op | source)
XLA Modules:
  0.0 212.0 jit_solution(8210489550356675937)
XLA Ops:
  1.4 4.5 %enc_attend.2 = (bf16[128,768]{1,0:T(8,128)(2,1)}, bf16[128,768]{1,0:T(8,128)(2,1)}, bf16[128,768]{1,0:T(8,128)(2,1)}, bf16[3,128,384]{2,1,0:T(8,128)(2,1)}, bf1...) custom-call(s32[3]{0:T(128)} %pad_add_fusion.refs_0_.refs_1_, bf16[98,2,768]{2,1,0:T(2,128)(2,1)} %bitcast.24, ...), custom_call_target="tpu_custom_call" | custom-call | flops 30000001024 | bytes 1 | tf_op jit(solution)/shard_map/enc_attend/pallas_call | solution.py:164
  5.9 3.0 %collective-permute-start.1 = (bf16[98,768]{1,0:T(8,128)(2,1)S(1)}, bf16[98,768]{1,0:T(8,128)(2,1)S(1)}, u32[]{:S(2)}, u32[]{:S(2)}) collective-permute-start(bf16[98,768]{1,0:T(8,128)(2,1)S(1)} %dynamic-slice_bitcast_fusion.1), channel_id=1, source_target_pairs={{0,1},{1,0},{2,3},{3,2},{4,5},{5,4},{6,7},{7,6},{8,9},{9,8},{10,11... | collective-permute-start | bytes 451592 | tf_op jit(solution)/shard_map/ppermute | solution.py:776
  8.9 1.5 collective-permute-start
  11.0 2.0 collective-permute-done.1.refs_1_
  13.8 2.1 enc_attend.3
  16.3 1.8 enc_hidden.1
  18.1 1.8 collective-permute-start.2
  20.4 5.6 %collective-permute-done.2.refs_4_ = bf16[128,768]{1,0:T(8,128)(2,1)S(1)} collective-permute-done((bf16[128,768]{1,0:T(8,128)(2,1)S(1)}, bf16[128,768]{1,0:T(8,128)(2,1)S(1)}, u32[]{:S(2)}, u32[]{:S(2)}) %collective-permute-start.2) | collective-permute-done | bytes 196640 | tf_op jit(solution)/shard_map/ppermute | solution.py:49
  26.1 4.2 %dec_attend.1 = (bf16[416,512]{1,0:T(8,128)(2,1)S(1)}, bf16[98,768]{1,0:T(8,128)(2,1)S(1)}, bf16[128,768]{1,0:T(8,128)(2,1)S(1)}, f32[416,512]{1,0:T(8,128)S(1)}...) custom-call(s32[1]{0:T(128)} %bitcast.3.refs_0_, ...), custom_call_target="tpu_custom_call" | custom-call | flops 30000001024 | bytes 1 | tf_op jit(solution)/shard_map/dec_attend/pallas_call | solution.py:164
  30.4 1.8 collective-permute-start.4
  32.2 1.4 enc_side_hidden.1
  33.8 8.8 %collective-permute-done.4.refs_4_ = bf16[416,512]{1,0:T(8,128)(2,1)S(1)} collective-permute-done((bf16[416,512]{1,0:T(8,128)(2,1)S(1)}, bf16[416,512]{1,0:T(8,128)(2,1)S(1)}, u32[]{:S(2)}, u32[]{:S(2)}) %collective-permute-start.4) | collective-permute-done | bytes 426016 | tf_op jit(solution)/shard_map/ppermute | solution.py:49
  42.6 4.4 %dec_hidden.1 = (bf16[416,512]{1,0:T(8,128)(2,1)S(1)}, bf16[416,512]{1,0:T(8,128)(2,1)S(1)}, f32[416,512]{1,0:T(8,128)S(1)}, bf16[416,512]{1,0:T(8,128)(2,1)S(1)...) custom-call(s32[1]{0:T(128)} %bitcast.3.refs_0_, ...), custom_call_target="tpu_custom_call" | custom-call | flops 30000001024 | bytes 1 | tf_op jit(solution)/shard_map/dec_hidden/pallas_call | solution.py:164
  47.0 1.8 collective-permute-start.7
  48.8 1.5 enc_out_both.1
  50.3 2.4 %collective-permute-done.8.refs_5_ = bf16[416,2304]{1,0:T(8,128)(2,1)S(1)} collective-permute-done((bf16[416,2304]{1,0:T(8,128)(2,1)S(1)}, bf16[416,2304]{1,0:T(8,128)(2,1)S(1)}, u32[]{:S(2)}, u32[]{:S(2)}) %collective-permute-start.8) | collective-permute-done | bytes 1916960 | tf_op jit(solution)/shard_map/ppermute | solution.py:49
  52.7 2.0 dec_hidden_weights.1
  54.7 1.6 collective-permute-start.12
  56.3 2.1 %collective-permute-done.7.refs_4_ = bf16[416,512]{1,0:T(8,128)(2,1)S(1)} collective-permute-done((bf16[416,512]{1,0:T(8,128)(2,1)S(1)}, bf16[416,512]{1,0:T(8,128)(2,1)S(1)}, u32[]{:S(2)}, u32[]{:S(2)}) %collective-permute-start.7) | collective-permute-done | bytes 426016 | tf_op jit(solution)/shard_map/ppermute | solution.py:49
  58.4 4.7 %dec_attend_back.1 = (bf16[416,512]{1,0:T(8,128)(2,1)S(1)}, f32[416,512]{1,0:T(8,128)S(1)}, bf16[416,512]{1,0:T(8,128)(2,1)S(1)}, bf16[3,416,256]{2,1,0:T(8,128)...) custom-call(s32[3]{0:T(128)S(1)} %copy-done.4, ...), custom_call_target="tpu_custom_call" | custom-call | flops 30000001024 | bytes 1 | tf_op jit(solution)/shard_map/dec_attend_back/pallas_call | solution.py:164
  63.1 1.8 collective-permute-start.10
  64.9 3.8 %collective-permute-done.12.refs_2_ = bf16[2,256,512]{2,1,0:T(8,128)(2,1)S(1)} collective-permute-done((bf16[2,256,512]{2,1,0:T(8,128)(2,1)S(1)}, bf16[2,256,512]{2,1,0:T(8,128)(2,1)S(1)}, u32[]{:S(2)}, u32[]{:S(2)}) %collective-permute-start.12) | collective-permute-done | bytes 524320 | tf_op jit(solution)/shard_map/ppermute | solution.py:776
  69.5 1.3 dec_head_weights.1
  70.7 1.6 collective-permute-start.14
  72.3 1.3 collective-permute-done.10.refs_4_
  73.7 1.9 dec_start_back.1
  75.7 1.8 collective-permute-start.13
  79.0 0.9 dec_bridge_weights.1
  79.9 3.0 %collective-permute-done.13.refs_2_.refs_4_ = bf16[128,768]{1,0:T(8,128)(2,1)S(1)} collective-permute-done((bf16[128,768]{1,0:T(8,128)(2,1)S(1)}, bf16[128,768]{1,0:T(8,128)(2,1)S(1)}, u32[]{:S(2)}, u32[]{:S(2)}) %collective-permute-start.13) | collective-permute-done | bytes 196640 | tf_op jit(solution)/shard_map/ppermute | solution.py:776
  83.0 1.8 collective-permute-start.20
  85.0 2.1 enc_hidden_back.1
  87.5 1.5 collective-permute-start.22
  89.6 1.6 collective-permute-start.23
  91.2 1.8 enc_hidden_weights.1
  93.0 1.5 collective-permute-done.20.refs_1_
  94.7 2.8 %collective-permute-start.21 = (bf16[384,512]{1,0:T(8,128)(2,1)S(1)}, bf16[384,512]{1,0:T(8,128)(2,1)S(1)}, u32[]{:S(2)}, u32[]{:S(2)}) collective-permute-start(bf16[384,512]{1,0:T(8,128)(2,1)S(1)} %get-tuple-element.250.refs_0_), channel_id=1, source_target_pairs={{0,4},{1,5},{2,6},{3,7},{4,0},{5,1},{6,2},{7,3},{8,12},{9,13},{10,... | collective-permute-start | bytes 1179656 | tf_op jit(solution)/shard_map/ppermute | solution.py:776
  97.5 1.6 collective-permute-start.19
  99.1 4.6 %enc_attend_back.1 = (bf16[256,768]{1,0:T(8,128)(2,1)S(1)}, f32[256,768]{1,0:T(8,128)S(1)}, bf16[256,768]{1,0:T(8,128)(2,1)S(1)}, bf16[3,256,384]{2,1,0:T(8,128)...) custom-call(s32[3]{0:T(128)S(1)} %copy-done.4, ...), custom_call_target="tpu_custom_call" | custom-call | flops 30000001024 | bytes 1 | tf_op jit(solution)/shard_map/enc_attend_back/pallas_call | solution.py:164
  103.8 1.6 collective-permute-start.29
  105.3 9.7 %collective-permute-done.21.refs_1_ = bf16[384,512]{1,0:T(8,128)(2,1)S(1)} collective-permute-done((bf16[384,512]{1,0:T(8,128)(2,1)S(1)}, bf16[384,512]{1,0:T(8,128)(2,1)S(1)}, u32[]{:S(2)}, u32[]{:S(2)}) %collective-permute-start.21) | collective-permute-done | bytes 393248 | tf_op jit(solution)/shard_map/ppermute | solution.py:776
  115.1 1.6 collective-permute-start.27
  117.4 3.3 %collective-permute-done.19.refs_1_ = bf16[384,768]{1,0:T(8,128)(2,1)S(1)} collective-permute-done((bf16[384,768]{1,0:T(8,128)(2,1)S(1)}, bf16[384,768]{1,0:T(8,128)(2,1)S(1)}, u32[]{:S(2)}, u32[]{:S(2)}) %collective-permute-start.19) | collective-permute-done | bytes 589856 | tf_op jit(solution)/shard_map/ppermute | solution.py:776
  120.8 1.7 collective-permute-start.25
  122.6 1.8 enc_start_back.1
  124.4 9.8 %collective-permute-done.26.refs_14_.refs_2_ = bf16[384,512]{1,0:T(8,128)(2,1)S(1)} collective-permute-done((bf16[384,512]{1,0:T(8,128)(2,1)S(1)}, bf16[384,512]{1,0:T(8,128)(2,1)S(1)}, u32[]{:S(2)}, u32[]{:S(2)}) %collective-permute-start.26) | collective-permute-done | bytes 393248 | tf_op jit(solution)/shard_map/ppermute | solution.py:776
  134.2 1.0 collective-permute-start.28
  135.2 1.3 last_weights.1
  136.6 7.3 %collective-permute-done.28.refs_4_ = bf16[384,512]{1,0:T(8,128)(2,1)S(1)} collective-permute-done((bf16[384,512]{1,0:T(8,128)(2,1)S(1)}, bf16[384,512]{1,0:T(8,128)(2,1)S(1)}, u32[]{:S(2)}, u32[]{:S(2)}) %collective-permute-start.28) | collective-permute-done | bytes 393248 | tf_op jit(solution)/shard_map/ppermute | solution.py:776
  144.7 1.9 dec_out.1
  146.6 1.7 collective-permute-done.31.refs_1_
  148.4 1.6 collective-permute-start.38
  150.1 10.9 %collective-permute-done.30.refs_1_ = bf16[880,256]{1,0:T(8,128)(2,1)S(1)} collective-permute-done((bf16[880,256]{1,0:T(8,128)(2,1)S(1)}, bf16[880,256]{1,0:T(8,128)(2,1)S(1)}, u32[]{:S(2)}, u32[]{:S(2)}) %collective-permute-start.30) | collective-permute-done | bytes 450592 | tf_op jit(solution)/shard_map/ppermute | solution.py:776
  161.2 10.3 %collective-permute-done.34.refs_1_.refs_2_ = bf16[384,768]{1,0:T(8,128)(2,1)S(1)} collective-permute-done((bf16[384,768]{1,0:T(8,128)(2,1)S(1)}, bf16[384,768]{1,0:T(8,128)(2,1)S(1)}, u32[]{:S(2)}, u32[]{:S(2)}) %collective-permute-start.34) | collective-permute-done | bytes 589856 | tf_op jit(solution)/shard_map/ppermute | solution.py:776
  171.5 1.3 collective-permute-start.39
  172.9 3.5 %dec_whole.1 = (f32[512,1024]{1,0:T(8,128)}, f32[1024,512]{1,0:T(8,128)}, f32[3,512,256]{2,1,0:T(8,128)}, f32[256,512]{1,0:T(8,128)}, f32[8,128]{1,0:T(8,128)S(1)}) custom-call(s32[3]{0:T(128)S(1)} %copy-done.4, bf16[2,2,384,512]{3,2,1,0:T(8,128)(2,1)S(1)} %get-tuple-element.286.refs_1_, bf16[2,2,384,512]{3,2,1,0:T(8,128)(2,1)S(1)} %collective-permute-done.33.refs_2_, ...), custom_call_target="tpu_custom_call" | custom-call | flops 30000001024 | bytes 1 | tf_op jit(solution)/shard_map/dec_whole/pallas_call | solution.py:164
  177.0 1.5 collective-permute-done.32.refs_1_
  178.5 1.3 collective-permute-start.36
  179.8 8.0 %collective-permute-done.39.refs_4_ = bf16[384,768]{1,0:T(8,128)(2,1)S(1)} collective-permute-done((bf16[384,768]{1,0:T(8,128)(2,1)S(1)}, bf16[384,768]{1,0:T(8,128)(2,1)S(1)}, u32[]{:S(2)}, u32[]{:S(2)}) %collective-permute-start.39) | collective-permute-done | bytes 589856 | tf_op jit(solution)/shard_map/ppermute | solution.py:776
  188.6 1.4 collective-permute-start.37
  190.6 2.5 %collective-permute-done.40.refs_2_ = bf16[2,2,384,768]{3,2,1,0:T(8,128)(2,1)S(1)} collective-permute-done((bf16[2,2,384,768]{3,2,1,0:T(8,128)(2,1)S(1)}, bf16[2,2,384,768]{3,2,1,0:T(8,128)(2,1)S(1)}, u32[]{:S(2)}, u32[]{:S(2)}) %collective-permute-start.40) | collective-permute-done | bytes 2359328 | tf_op jit(solution)/shard_map/ppermute | solution.py:49
  193.1 4.9 %enc_hidden_whole.1 = (f32[768,1536]{1,0:T(8,128)}, f32[1536,768]{1,0:T(8,128)}, f32[8,128]{1,0:T(8,128)S(1)}) custom-call(s32[3]{0:T(128)S(1)} %copy-done.4, bf16[2,2,384,768]{3,2,1,0:T(8,128)(2,1)S(1)} %get-tuple-element.293.refs_1_, bf16[2,2,384,768]{3,2,1,0:T(8,128)(2,1)S(1)} %collective-permute-done.40.refs_2_, f32[8,128]{1,0:T(8,128)S(1)} %get-tuple-element.295.refs_3_), custom_call_target="tpu_custom_call" | custom-call | flops 30000001024 | bytes 1 | tf_op jit(solution)/shard_map/enc_hidden_whole/pallas_call | solution.py:164
  198.0 5.4 %collective-permute-done.37.refs_4_ = bf16[880,256]{1,0:T(8,128)(2,1)S(1)} collective-permute-done((bf16[880,256]{1,0:T(8,128)(2,1)S(1)}, bf16[880,256]{1,0:T(8,128)(2,1)S(1)}, u32[]{:S(2)}, u32[]{:S(2)}) %collective-permute-start.37) | collective-permute-done | bytes 450592 | tf_op jit(solution)/shard_map/ppermute | solution.py:776
  204.2 3.7 %collective-permute-done.41.refs_2_ = bf16[2,2,880,256]{3,2,1,0:T(8,128)(2,1)S(1)} collective-permute-done((bf16[2,2,880,256]{3,2,1,0:T(8,128)(2,1)S(1)}, bf16[2,2,880,256]{3,2,1,0:T(8,128)(2,1)S(1)}, u32[]{:S(2)}, u32[]{:S(2)}) %collective-permute-start.41) | collective-permute-done | bytes 1802272 | tf_op jit(solution)/shard_map/ppermute | solution.py:49
  207.9 3.5 %last_whole.1 = (f32[3,768,384]{2,1,0:T(8,128)}, f32[384,768]{1,0:T(8,128)}, f32[6,768]{1,0:T(8,128)}, f32[1,1536]{1,0:T(1,128)S(1)}, f32[2,384]{1,0:T(2,128)}, ...) custom-call(s32[3]{0:T(128)S(1)} %copy-done.4, ...), custom_call_target="tpu_custom_call" | custom-call | flops 30000001024 | bytes 1 | tf_op jit(solution)/shard_map/last_whole/pallas_call | solution.py:164
  (165 shorter events, 12.3 us)
Async XLA Ops:
  0.7 19.3 %copy-start = (bf16[2,392,512]{2,1,0:T(8,128)(2,1)S(1)}, bf16[2,392,512]{2,1,0:T(8,128)(2,1)}, u32[]{:S(2)}) copy-start(bf16[2,392,512]{2,1,0:T(8,128)(2,1)} %param.39) | copy-start | bytes 2408452
  1.3 11.8 %copy-start.4 = (s32[3]{0:T(128)S(1)}, s32[3]{0:T(128)}, u32[]{:S(2)}) copy-start(s32[3]{0:T(128)} %pad_add_fusion.refs_0_.refs_1_) | copy-start | bytes 40
  1.3 11.8 %copy-start.9 = (bf16[768,3,384]{2,0,1:T(8,128)(2,1)S(1)}, bf16[768,3,384]{2,0,1:T(8,128)(2,1)}, u32[]{:S(2)}) copy-start(bf16[768,3,384]{2,0,1:T(8,128)(2,1)} %param.24) | copy-start | bytes 5308420
  1.3 11.8 %copy-start.15 = (bf16[384,768]{1,0:T(8,128)(2,1)S(1)}, bf16[384,768]{1,0:T(8,128)(2,1)}, u32[]{:S(2)}) copy-start(bf16[384,768]{1,0:T(8,128)(2,1)} %refs_13_.1) | copy-start | bytes 1769476
  1.3 11.8 %copy-start.22 = (bf16[6,768]{1,0:T(8,128)(2,1)S(1)}, bf16[6,768]{1,0:T(8,128)(2,1)}, u32[]{:S(2)}) copy-start(bf16[6,768]{1,0:T(8,128)(2,1)} %refs_4_.6) | copy-start | bytes 27652
  1.3 11.7 %copy-start.24 = (bf16[2,384]{1,0:T(2,128)(2,1)S(1)}, bf16[2,384]{1,0:T(2,128)(2,1)}, u32[]{:S(2)}) copy-start(bf16[2,384]{1,0:T(2,128)(2,1)} %refs_4_.5) | copy-start | bytes 4612
  5.9 7.2 %collective-permute-start.1 = (bf16[98,768]{1,0:T(8,128)(2,1)S(1)}, bf16[98,768]{1,0:T(8,128)(2,1)S(1)}, u32[]{:S(2)}, u32[]{:S(2)}) collective-permute-start(bf16[98,768]{1,0:T(8,128)(2,1)S(1)} %dynamic-slice_bitcast_fusion.1), channel_id=1, source_target_pairs={{0,1},{1,0},{2,3},{3,2},{4,5},{5,4},{6,7},{7,6},{8,9},{9,8},{10,11... | collective-permute-start | bytes 451592 | tf_op jit(solution)/shard_map/ppermute | solution.py:776
  8.9 7.0 %collective-permute-start = (bf16[128,768]{1,0:T(8,128)(2,1)}, bf16[128,768]{1,0:T(8,128)(2,1)S(1)}, u32[]{:S(2)}, u32[]{:S(2)}) collective-permute-start(bf16[128,768]{1,0:T(8,128)(2,1)} %get-tuple-element.169.refs_3_), channel_id=1, source_target_pairs={{0,8},{8,0},{1,9},{9,1},{2,10},{10,2},{3,11},{11,3},{4,12},{12,4},... | collective-permute-start | bytes 589832 | tf_op jit(solution)/shard_map/ppermute | solution.py:49
  15.9 16.2 %copy-start.36 = (bf16[128,768]{1,0:T(8,128)(2,1)}, bf16[128,768]{1,0:T(8,128)(2,1)S(1)}, u32[]{:S(2)}) copy-start(bf16[128,768]{1,0:T(8,128)(2,1)S(1)} %get-tuple-element.183.refs_7_.refs_2_) | copy-start | bytes 589828
  15.9 16.2 %copy-start.38 = (bf16[128,768]{1,0:T(8,128)(2,1)}, bf16[128,768]{1,0:T(8,128)(2,1)S(1)}, u32[]{:S(2)}) copy-start(bf16[128,768]{1,0:T(8,128)(2,1)S(1)} %get-tuple-element.181.refs_1_) | copy-start | bytes 589828
  15.9 16.2 %copy-start.42 = (bf16[128,384]{1,0:T(8,128)(2,1)}, bf16[128,384]{1,0:T(8,128)(2,1)S(1)}, u32[]{:S(2)}) copy-start(bf16[128,384]{1,0:T(8,128)(2,1)S(1)} %get-tuple-element.184.refs_8_.refs_5_) | copy-start | bytes 294916
  16.3 9.7 %copy-start.12 = (bf16[512,3,256]{2,0,1:T(8,128)(2,1)S(1)}, bf16[512,3,256]{2,0,1:T(8,128)(2,1)}, u32[]{:S(2)}) copy-start(bf16[512,3,256]{2,0,1:T(8,128)(2,1)} %param.33) | copy-start | bytes 2359300
  16.3 9.8 %copy-start.13 = (bf16[768,512]{1,0:T(8,128)(2,1)S(1)}, bf16[768,512]{1,0:T(8,128)(2,1)}, u32[]{:S(2)}) copy-start(bf16[768,512]{1,0:T(8,128)(2,1)} %refs_7_.4) | copy-start | bytes 2359300
  16.3 9.7 %copy-start.19 = (bf16[256,512]{1,0:T(8,128)(2,1)S(1)}, bf16[256,512]{1,0:T(8,128)(2,1)}, u32[]{:S(2)}) copy-start(bf16[256,512]{1,0:T(8,128)(2,1)} %refs_9_.3) | copy-start | bytes 786436
  18.1 12.2 %copy-start.28 = (f32[128,768]{1,0:T(8,128)}, f32[128,768]{1,0:T(8,128)S(1)}, u32[]{:S(2)}) copy-start(f32[128,768]{1,0:T(8,128)S(1)} %get-tuple-element.175.refs_2_.refs_1_) | copy-start | bytes 1179652
  18.1 7.9 %collective-permute-start.2 = (bf16[128,768]{1,0:T(8,128)(2,1)S(1)}, bf16[128,768]{1,0:T(8,128)(2,1)S(1)}, u32[]{:S(2)}, u32[]{:S(2)}) collective-permute-start(bf16[128,768]{1,0:T(8,128)(2,1)S(1)} %get-tuple-element.176.refs_3_), channel_id=1, source_target_pairs={{0,8},{8,0},{1,9},{9,1},{2,10},{10,2},{3,11},{11,3},{4,12},{12,4},... | collective-permute-start | bytes 589832 | tf_op jit(solution)/shard_map/ppermute | solution.py:49
  19.9 10.4 %copy-start.2 = (s32[2,64]{1,0:T(2,128)}, s32[2,64]{1,0:T(2,128)S(1)}, u32[]{:S(2)}) copy-start(s32[2,64]{1,0:T(2,128)S(1)} %pad.4.refs_1_) | copy-start | bytes 1540
  20.0 12.2 %collective-permute-start.5 = (bf16[128,768]{1,0:T(8,128)(2,1)S(1)}, bf16[128,768]{1,0:T(8,128)(2,1)S(1)}, u32[]{:S(2)}, u32[]{:S(2)}) collective-permute-start(bf16[128,768]{1,0:T(8,128)(2,1)S(1)} %get-tuple-element.182.refs_3_), channel_id=1, source_target_pairs={{0,8},{8,0},{1,9},{9,1},{2,10},{10,2},{3,11},{11,3},{4,12},{12,4},... | collective-permute-start | bytes 589832 | tf_op jit(solution)/shard_map/ppermute | solution.py:49
  20.4 13.4 %collective-permute-start.6 = (bf16[128,1920]{1,0:T(8,128)(2,1)S(1)}, bf16[128,1920]{1,0:T(8,128)(2,1)S(1)}, u32[]{:S(2)}, u32[]{:S(2)}) collective-permute-start(bf16[128,1920]{1,0:T(8,128)(2,1)S(1)} %get-tuple-element.187), channel_id=1, source_target_pairs={{0,16},{16,0},{1,17},{17,1},{2,18},{18,2},{3,19},{19,3},{4,20},{20... | collective-permute-start | bytes 1474568 | tf_op jit(solution)/shard_map/ppermute | solution.py:49
  30.3 12.3 %copy-start.26 = (f32[416,512]{1,0:T(8,128)}, f32[416,512]{1,0:T(8,128)S(1)}, u32[]{:S(2)}) copy-start(f32[416,512]{1,0:T(8,128)S(1)} %get-tuple-element.179.refs_2_) | copy-start | bytes 2555908
  30.3 18.5 %collective-permute-start.3 = (bf16[98,768]{1,0:T(8,128)(2,1)S(1)}, bf16[98,768]{1,0:T(8,128)(2,1)S(1)}, u32[]{:S(2)}, u32[]{:S(2)}) collective-permute-start(bf16[98,768]{1,0:T(8,128)(2,1)S(1)} %get-tuple-element.178.refs_1_), channel_id=1, source_target_pairs={{0,16},{16,0},{1,17},{17,1},{2,18},{18,2},{3,19},{19,3},{4,20},{20... | collective-permute-start | bytes 451592 | tf_op jit(solution)/shard_map/ppermute | solution.py:49
  30.4 12.2 %collective-permute-start.4 = (bf16[416,512]{1,0:T(8,128)(2,1)S(1)}, bf16[416,512]{1,0:T(8,128)(2,1)S(1)}, u32[]{:S(2)}, u32[]{:S(2)}) collective-permute-start(bf16[416,512]{1,0:T(8,128)(2,1)S(1)} %get-tuple-element.180.refs_3_), channel_id=1, source_target_pairs={{0,8},{8,0},{1,9},{9,1},{2,10},{10,2},{3,11},{11,3},{4,12},{12,4},... | collective-permute-start | bytes 1277960 | tf_op jit(solution)/shard_map/ppermute | solution.py:49
  32.2 10.5 %copy-start.10 = (bf16[512,1024]{1,0:T(8,128)(2,1)S(1)}, bf16[512,1024]{1,0:T(8,128)(2,1)}, u32[]{:S(2)}) copy-start(bf16[512,1024]{1,0:T(8,128)(2,1)} %refs_6_.4) | copy-start | bytes 3145732
  32.2 10.4 %copy-start.11 = (bf16[1024,512]{1,0:T(8,128)(2,1)S(1)}, bf16[1024,512]{1,0:T(8,128)(2,1)}, u32[]{:S(2)}) copy-start(bf16[1024,512]{1,0:T(8,128)(2,1)} %refs_8_.3) | copy-start | bytes 3145732
  33.6 16.7 %collective-permute-start.9 = (bf16[128,1920]{1,0:T(8,128)(2,1)S(1)}, bf16[128,1920]{1,0:T(8,128)(2,1)S(1)}, u32[]{:S(2)}, u32[]{:S(2)}) collective-permute-start(bf16[128,1920]{1,0:T(8,128)(2,1)S(1)} %get-tuple-element.205), channel_id=1, source_target_pairs={{0,16},{16,0},{1,17},{17,1},{2,18},{18,2},{3,19},{19,3},{4,20},{20... | collective-permute-start | bytes 1474568 | tf_op jit(solution)/shard_map/ppermute | solution.py:49
  47.0 11.4 %collective-permute-start.7 = (bf16[416,512]{1,0:T(8,128)(2,1)S(1)}, bf16[416,512]{1,0:T(8,128)(2,1)S(1)}, u32[]{:S(2)}, u32[]{:S(2)}) collective-permute-start(bf16[416,512]{1,0:T(8,128)(2,1)S(1)} %get-tuple-element.195.refs_3_), channel_id=1, source_target_pairs={{0,8},{8,0},{1,9},{9,1},{2,10},{10,2},{3,11},{11,3},{4,12},{12,4},... | collective-permute-start | bytes 1277960 | tf_op jit(solution)/shard_map/ppermute | solution.py:49
  48.8 3.9 %collective-permute-start.8 = (bf16[416,2304]{1,0:T(8,128)(2,1)S(1)}, bf16[416,2304]{1,0:T(8,128)(2,1)S(1)}, u32[]{:S(2)}, u32[]{:S(2)}) collective-permute-start(bf16[416,2304]{1,0:T(8,128)(2,1)S(1)} %get-tuple-element.203), channel_id=1, source_target_pairs={{0,16},{16,0},{1,17},{17,1},{2,18},{18,2},{3,19},{19,3},{4,20},{20... | collective-permute-start | bytes 5750792 | tf_op jit(solution)/shard_map/ppermute | solution.py:49
  54.7 14.0 %collective-permute-start.12 = (bf16[2,256,512]{2,1,0:T(8,128)(2,1)S(1)}, bf16[2,256,512]{2,1,0:T(8,128)(2,1)S(1)}, u32[]{:S(2)}, u32[]{:S(2)}) collective-permute-start(bf16[2,256,512]{2,1,0:T(8,128)(2,1)S(1)} %get-tuple-element.213), channel_id=1, source_target_pairs={{0,1},{1,0},{2,3},{3,2},{4,5},{5,4},{6,7},{7,6},{8,9},{9,8},{10,11... | collective-permute-start | bytes 1572872 | tf_op jit(solution)/shard_map/ppermute | solution.py:776
  63.1 10.5 %collective-permute-start.10 = (bf16[416,512]{1,0:T(8,128)(2,1)S(1)}, bf16[416,512]{1,0:T(8,128)(2,1)S(1)}, u32[]{:S(2)}, u32[]{:S(2)}) collective-permute-start(bf16[416,512]{1,0:T(8,128)(2,1)S(1)} %get-tuple-element.207.refs_3_), channel_id=1, source_target_pairs={{0,8},{8,0},{1,9},{9,1},{2,10},{10,2},{3,11},{11,3},{4,12},{12,4},... | collective-permute-start | bytes 1277960 | tf_op jit(solution)/shard_map/ppermute | solution.py:49
  64.9 4.5 %collective-permute-start.11 = (bf16[416,1536]{1,0:T(8,128)(2,1)S(1)}, bf16[416,1536]{1,0:T(8,128)(2,1)S(1)}, u32[]{:S(2)}, u32[]{:S(2)}) collective-permute-start(bf16[416,1536]{1,0:T(8,128)(2,1)S(1)} %get-tuple-element.211), channel_id=1, source_target_pairs={{0,16},{16,0},{1,17},{17,1},{2,18},{18,2},{3,19},{19,3},{4,20},{20... | collective-permute-start | bytes 3833864 | tf_op jit(solution)/shard_map/ppermute | solution.py:49
  70.7 7.6 %collective-permute-start.14 = (bf16[2,128,512]{2,1,0:T(8,128)(2,1)S(1)}, bf16[2,128,512]{2,1,0:T(8,128)(2,1)S(1)}, u32[]{:S(2)}, u32[]{:S(2)}) collective-permute-start(bf16[2,128,512]{2,1,0:T(8,128)(2,1)S(1)} %get-tuple-element.227), channel_id=1, source_target_pairs={{0,1},{1,0},{2,3},{3,2},{4,5},{5,4},{6,7},{7,6},{8,9},{9,8},{10,11... | collective-permute-start | bytes 786440 | tf_op jit(solution)/shard_map/ppermute | solution.py:776
  75.6 9.4 %collective-permute-start.15 = (bf16[128,768]{1,0:T(8,128)(2,1)S(1)}, bf16[128,768]{1,0:T(8,128)(2,1)S(1)}, u32[]{:S(2)}, u32[]{:S(2)}) collective-permute-start(bf16[128,768]{1,0:T(8,128)(2,1)S(1)} %get-tuple-element.217.refs_1_.refs_3_), channel_id=1, source_target_pairs={{0,16},{16,0},{1,17},{17,1},{2,18},{18,2},{3,19},{19,3},{4,20},{20... | collective-permute-start | bytes 589832 | tf_op jit(solution)/shard_map/ppermute | solution.py:49
  75.7 7.3 %collective-permute-start.13 = (bf16[128,768]{1,0:T(8,128)(2,1)S(1)}, bf16[128,768]{1,0:T(8,128)(2,1)S(1)}, u32[]{:S(2)}, u32[]{:S(2)}) collective-permute-start(bf16[128,768]{1,0:T(8,128)(2,1)S(1)} %get-tuple-element.217.refs_1_.refs_3_), channel_id=1, source_target_pairs={{0,1},{1,0},{2,3},{3,2},{4,5},{5,4},{6,7},{7,6},{8,9},{9,8},{10,11... | collective-permute-start | bytes 589832 | tf_op jit(solution)/shard_map/ppermute | solution.py:776
  83.0 6.0 %collective-permute-start.16 = (bf16[128,768]{1,0:T(8,128)(2,1)S(1)}, bf16[128,768]{1,0:T(8,128)(2,1)S(1)}, u32[]{:S(2)}, u32[]{:S(2)}) collective-permute-start(bf16[128,768]{1,0:T(8,128)(2,1)S(1)} %collective-permute-done.13.refs_2_.refs_4_), channel_id=1, source_target_pairs={{0,16},{16,0},{1,17},{17,1},{2,18},{18,2},{3,19},{19,3},{4,20},{20... | collective-permute-start | bytes 589832 | tf_op jit(solution)/shard_map/ppermute | solution.py:49
  83.0 11.6 %collective-permute-start.20 = (bf16[384,512]{1,0:T(8,128)(2,1)S(1)}, bf16[384,512]{1,0:T(8,128)(2,1)S(1)}, u32[]{:S(2)}, u32[]{:S(2)}) collective-permute-start(bf16[384,512]{1,0:T(8,128)(2,1)S(1)} %get-tuple-element.248), channel_id=1, source_target_pairs={{0,2},{1,3},{2,0},{3,1},{4,6},{5,7},{6,4},{7,5},{8,10},{9,11},{10,... | collective-permute-start | bytes 1179656 | tf_op jit(solution)/shard_map/ppermute | solution.py:776
  84.8 4.2 %collective-permute-start.18 = (bf16[2,2,128,512]{3,2,1,0:T(8,128)(2,1)S(1)}, bf16[2,2,128,512]{3,2,1,0:T(8,128)(2,1)S(1)}, u32[]{:S(2)}, u32[]{:S(2)}) collective-permute-start(bf16[2,2,128,512]{3,2,1,0:T(8,128)(2,1)S(1)} %get-tuple-element.242), channel_id=1, source_target_pairs={{0,16},{16,0},{1,17},{17,1},{2,18},{18,2},{3,19},{19,3},{4,20},{20... | collective-permute-start | bytes 1572872 | tf_op jit(solution)/shard_map/ppermute | solution.py:49
  87.1 4.1 %collective-permute-start.17 = (bf16[256,384]{1,0:T(8,128)(2,1)S(1)}, bf16[256,384]{1,0:T(8,128)(2,1)S(1)}, u32[]{:S(2)}, u32[]{:S(2)}) collective-permute-start(bf16[256,384]{1,0:T(8,128)(2,1)S(1)} %get-tuple-element.240), channel_id=1, source_target_pairs={{0,16},{16,0},{1,17},{17,1},{2,18},{18,2},{3,19},{19,3},{4,20},{20... | collective-permute-start | bytes 589832 | tf_op jit(solution)/shard_map/ppermute | solution.py:49
  87.5 11.6 %collective-permute-start.22 = (bf16[256,768]{1,0:T(8,128)(2,1)S(1)}, bf16[256,768]{1,0:T(8,128)(2,1)S(1)}, u32[]{:S(2)}, u32[]{:S(2)}) collective-permute-start(bf16[256,768]{1,0:T(8,128)(2,1)S(1)} %get-tuple-element.252.refs_5_), channel_id=1, source_target_pairs={{0,8},{8,0},{1,9},{9,1},{2,10},{10,2},{3,11},{11,3},{4,12},{12,4},... | collective-permute-start | bytes 1179656 | tf_op jit(solution)/shard_map/ppermute | solution.py:49
  89.6 9.4 %collective-permute-start.23 = (bf16[2,128,512]{2,1,0:T(8,128)(2,1)S(1)}, bf16[2,128,512]{2,1,0:T(8,128)(2,1)S(1)}, u32[]{:S(2)}, u32[]{:S(2)}) collective-permute-start(bf16[2,128,512]{2,1,0:T(8,128)(2,1)S(1)} %get-tuple-element.258), channel_id=1, source_target_pairs={{0,1},{1,0},{2,3},{3,2},{4,5},{5,4},{6,7},{7,6},{8,9},{9,8},{10,11... | collective-permute-start | bytes 786440 | tf_op jit(solution)/shard_map/ppermute | solution.py:776
  94.7 20.3 %collective-permute-start.21 = (bf16[384,512]{1,0:T(8,128)(2,1)S(1)}, bf16[384,512]{1,0:T(8,128)(2,1)S(1)}, u32[]{:S(2)}, u32[]{:S(2)}) collective-permute-start(bf16[384,512]{1,0:T(8,128)(2,1)S(1)} %get-tuple-element.250.refs_0_), channel_id=1, source_target_pairs={{0,4},{1,5},{2,6},{3,7},{4,0},{5,1},{6,2},{7,3},{8,12},{9,13},{10,... | collective-permute-start | bytes 1179656 | tf_op jit(solution)/shard_map/ppermute | solution.py:776
  97.5 23.2 %collective-permute-start.19 = (bf16[384,768]{1,0:T(8,128)(2,1)S(1)}, bf16[384,768]{1,0:T(8,128)(2,1)S(1)}, u32[]{:S(2)}, u32[]{:S(2)}) collective-permute-start(bf16[384,768]{1,0:T(8,128)(2,1)S(1)} %get-tuple-element.246), channel_id=1, source_target_pairs={{0,2},{1,3},{2,0},{3,1},{4,6},{5,7},{6,4},{7,5},{8,10},{9,11},{10,... | collective-permute-start | bytes 1769480 | tf_op jit(solution)/shard_map/ppermute | solution.py:776
  103.7 17.0 %collective-permute-start.24 = (bf16[256,768]{1,0:T(8,128)(2,1)S(1)}, bf16[256,768]{1,0:T(8,128)(2,1)S(1)}, u32[]{:S(2)}, u32[]{:S(2)}) collective-permute-start(bf16[256,768]{1,0:T(8,128)(2,1)S(1)} %get-tuple-element.261), channel_id=1, source_target_pairs={{0,16},{16,0},{1,17},{17,1},{2,18},{18,2},{3,19},{19,3},{4,20},{20... | collective-permute-start | bytes 1179656 | tf_op jit(solution)/shard_map/ppermute | solution.py:49
  103.8 18.8 %collective-permute-start.29 = (bf16[256,768]{1,0:T(8,128)(2,1)S(1)}, bf16[256,768]{1,0:T(8,128)(2,1)S(1)}, u32[]{:S(2)}, u32[]{:S(2)}) collective-permute-start(bf16[256,768]{1,0:T(8,128)(2,1)S(1)} %get-tuple-element.267.refs_2_), channel_id=1, source_target_pairs={{0,8},{8,0},{1,9},{9,1},{2,10},{10,2},{3,11},{11,3},{4,12},{12,4},... | collective-permute-start | bytes 1179656 | tf_op jit(solution)/shard_map/ppermute | solution.py:49
  115.1 21.5 %collective-permute-start.27 = (bf16[384,512]{1,0:T(8,128)(2,1)S(1)}, bf16[384,512]{1,0:T(8,128)(2,1)S(1)}, u32[]{:S(2)}, u32[]{:S(2)}) collective-permute-start(bf16[384,512]{1,0:T(8,128)(2,1)S(1)} %get-tuple-element.264.refs_1_), channel_id=1, source_target_pairs={{0,1},{1,0},{2,3},{3,2},{4,5},{5,4},{6,7},{7,6},{8,9},{9,8},{10,11... | collective-permute-start | bytes 1179656 | tf_op jit(solution)/shard_map/ppermute | solution.py:776
  116.7 17.4 %collective-permute-start.26 = (bf16[384,512]{1,0:T(8,128)(2,1)S(1)}, bf16[384,512]{1,0:T(8,128)(2,1)S(1)}, u32[]{:S(2)}, u32[]{:S(2)}) collective-permute-start(bf16[384,512]{1,0:T(8,128)(2,1)S(1)} %get-tuple-element.264.refs_1_), channel_id=1, source_target_pairs={{0,2},{1,3},{2,0},{3,1},{4,6},{5,7},{6,4},{7,5},{8,10},{9,11},{10,... | collective-permute-start | bytes 1179656 | tf_op jit(solution)/shard_map/ppermute | solution.py:776
  120.8 23.9 %collective-permute-start.25 = (bf16[416,512]{1,0:T(8,128)(2,1)S(1)}, bf16[416,512]{1,0:T(8,128)(2,1)S(1)}, u32[]{:S(2)}, u32[]{:S(2)}) collective-permute-start(bf16[416,512]{1,0:T(8,128)(2,1)S(1)} %get-tuple-element.263.refs_2_), channel_id=1, source_target_pairs={{0,8},{8,0},{1,9},{9,1},{2,10},{10,2},{3,11},{11,3},{4,12},{12,4},... | collective-permute-start | bytes 1277960 | tf_op jit(solution)/shard_map/ppermute | solution.py:49
  122.5 25.8 %collective-permute-start.31 = (bf16[384,768]{1,0:T(8,128)(2,1)S(1)}, bf16[384,768]{1,0:T(8,128)(2,1)S(1)}, u32[]{:S(2)}, u32[]{:S(2)}) collective-permute-start(bf16[384,768]{1,0:T(8,128)(2,1)S(1)} %get-tuple-element.282.refs_0_), channel_id=1, source_target_pairs={{0,4},{1,5},{2,6},{3,7},{4,0},{5,1},{6,2},{7,3},{8,12},{9,13},{10,... | collective-permute-start | bytes 1769480 | tf_op jit(solution)/shard_map/ppermute | solution.py:776
  122.6 12.7 %copy-start.18 = (bf16[128,1920]{1,0:T(8,128)(2,1)S(1)}, bf16[128,1920]{1,0:T(8,128)(2,1)}, u32[]{:S(2)}) copy-start(bf16[128,1920]{1,0:T(8,128)(2,1)} %copy-done.16) | copy-start | bytes 1474564
  122.6 12.6 %copy-start.33 = (bf16[128,768]{1,0:T(8,128)(2,1)S(1)}, bf16[128,768]{1,0:T(8,128)(2,1)}, u32[]{:S(2)}) copy-start(bf16[128,768]{1,0:T(8,128)(2,1)} %get-tuple-element.170.refs_7_.refs_1_) | copy-start | bytes 589828
  122.6 12.6 %copy-start.37 = (bf16[128,768]{1,0:T(8,128)(2,1)S(1)}, bf16[128,768]{1,0:T(8,128)(2,1)}, u32[]{:S(2)}) copy-start(bf16[128,768]{1,0:T(8,128)(2,1)} %copy-done.36) | copy-start | bytes 589828
  122.6 12.6 %copy-start.41 = (bf16[128,384]{1,0:T(8,128)(2,1)S(1)}, bf16[128,384]{1,0:T(8,128)(2,1)}, u32[]{:S(2)}) copy-start(bf16[128,384]{1,0:T(8,128)(2,1)} %get-tuple-element.171.refs_8_.refs_4_) | copy-start | bytes 294916
  122.6 12.6 %copy-start.43 = (bf16[128,384]{1,0:T(8,128)(2,1)S(1)}, bf16[128,384]{1,0:T(8,128)(2,1)}, u32[]{:S(2)}) copy-start(bf16[128,384]{1,0:T(8,128)(2,1)} %copy-done.42) | copy-start | bytes 294916
  134.2 9.8 %collective-permute-start.28 = (bf16[384,512]{1,0:T(8,128)(2,1)S(1)}, bf16[384,512]{1,0:T(8,128)(2,1)S(1)}, u32[]{:S(2)}, u32[]{:S(2)}) collective-permute-start(bf16[384,512]{1,0:T(8,128)(2,1)S(1)} %collective-permute-done.26.refs_14_.refs_2_), channel_id=1, source_target_pairs={{0,1},{1,0},{2,3},{3,2},{4,5},{5,4},{6,7},{7,6},{8,9},{9,8},{10,11... | collective-permute-start | bytes 1179656 | tf_op jit(solution)/shard_map/ppermute | solution.py:776
  136.6 24.4 %collective-permute-start.30 = (bf16[880,256]{1,0:T(8,128)(2,1)S(1)}, bf16[880,256]{1,0:T(8,128)(2,1)S(1)}, u32[]{:S(2)}, u32[]{:S(2)}) collective-permute-start(bf16[880,256]{1,0:T(8,128)(2,1)S(1)} %get-tuple-element.281), channel_id=1, source_target_pairs={{0,2},{1,3},{2,0},{3,1},{4,6},{5,7},{6,4},{7,5},{8,10},{9,11},{10,... | collective-permute-start | bytes 1351688 | tf_op jit(solution)/shard_map/ppermute | solution.py:776
  144.6 28.2 %collective-permute-start.33 = (bf16[2,2,384,512]{3,2,1,0:T(8,128)(2,1)S(1)}, bf16[2,2,384,512]{3,2,1,0:T(8,128)(2,1)S(1)}, u32[]{:S(2)}, u32[]{:S(2)}) collective-permute-start(bf16[2,2,384,512]{3,2,1,0:T(8,128)(2,1)S(1)} %get-tuple-element.286.refs_1_), channel_id=1, source_target_pairs={{0,16},{16,0},{1,17},{17,1},{2,18},{18,2},{3,19},{19,3},{4,20},{20... | collective-permute-start | bytes 4718600 | tf_op jit(solution)/shard_map/ppermute | solution.py:49
  148.4 31.4 %collective-permute-start.38 = (bf16[384,768]{1,0:T(8,128)(2,1)S(1)}, bf16[384,768]{1,0:T(8,128)(2,1)S(1)}, u32[]{:S(2)}, u32[]{:S(2)}) collective-permute-start(bf16[384,768]{1,0:T(8,128)(2,1)S(1)} %get-tuple-element.289.refs_1_), channel_id=1, source_target_pairs={{0,1},{1,0},{2,3},{3,2},{4,5},{5,4},{6,7},{7,6},{8,9},{9,8},{10,11... | collective-permute-start | bytes 1769480 | tf_op jit(solution)/shard_map/ppermute | solution.py:776
  150.1 21.5 %collective-permute-start.34 = (bf16[384,768]{1,0:T(8,128)(2,1)S(1)}, bf16[384,768]{1,0:T(8,128)(2,1)S(1)}, u32[]{:S(2)}, u32[]{:S(2)}) collective-permute-start(bf16[384,768]{1,0:T(8,128)(2,1)S(1)} %get-tuple-element.289.refs_1_), channel_id=1, source_target_pairs={{0,2},{1,3},{2,0},{3,1},{4,6},{5,7},{6,4},{7,5},{8,10},{9,11},{10,... | collective-permute-start | bytes 1769480 | tf_op jit(solution)/shard_map/ppermute | solution.py:776
  161.1 17.3 %collective-permute-start.32 = (bf16[880,256]{1,0:T(8,128)(2,1)S(1)}, bf16[880,256]{1,0:T(8,128)(2,1)S(1)}, u32[]{:S(2)}, u32[]{:S(2)}) collective-permute-start(bf16[880,256]{1,0:T(8,128)(2,1)S(1)} %get-tuple-element.285.refs_0_), channel_id=1, source_target_pairs={{0,4},{1,5},{2,6},{3,7},{4,0},{5,1},{6,2},{7,3},{8,12},{9,13},{10,... | collective-permute-start | bytes 1351688 | tf_op jit(solution)/shard_map/ppermute | solution.py:776
  171.5 16.3 %collective-permute-start.39 = (bf16[384,768]{1,0:T(8,128)(2,1)S(1)}, bf16[384,768]{1,0:T(8,128)(2,1)S(1)}, u32[]{:S(2)}, u32[]{:S(2)}) collective-permute-start(bf16[384,768]{1,0:T(8,128)(2,1)S(1)} %collective-permute-done.34.refs_1_.refs_2_), channel_id=1, source_target_pairs={{0,1},{1,0},{2,3},{3,2},{4,5},{5,4},{6,7},{7,6},{8,9},{9,8},{10,11... | collective-permute-start | bytes 1769480 | tf_op jit(solution)/shard_map/ppermute | solution.py:776
  178.5 19.4 %collective-permute-start.36 = (bf16[880,256]{1,0:T(8,128)(2,1)S(1)}, bf16[880,256]{1,0:T(8,128)(2,1)S(1)}, u32[]{:S(2)}, u32[]{:S(2)}) collective-permute-start(bf16[880,256]{1,0:T(8,128)(2,1)S(1)} %get-tuple-element.291.refs_1_), channel_id=1, source_target_pairs={{0,1},{1,0},{2,3},{3,2},{4,5},{5,4},{6,7},{7,6},{8,9},{9,8},{10,11... | collective-permute-start | bytes 1351688 | tf_op jit(solution)/shard_map/ppermute | solution.py:776
  179.8 8.8 %collective-permute-start.35 = (bf16[880,256]{1,0:T(8,128)(2,1)S(1)}, bf16[880,256]{1,0:T(8,128)(2,1)S(1)}, u32[]{:S(2)}, u32[]{:S(2)}) collective-permute-start(bf16[880,256]{1,0:T(8,128)(2,1)S(1)} %get-tuple-element.291.refs_1_), channel_id=1, source_target_pairs={{0,2},{1,3},{2,0},{3,1},{4,6},{5,7},{6,4},{7,5},{8,10},{9,11},{10,... | collective-permute-start | bytes 1351688 | tf_op jit(solution)/shard_map/ppermute | solution.py:776
  188.5 4.6 %collective-permute-start.40 = (bf16[2,2,384,768]{3,2,1,0:T(8,128)(2,1)S(1)}, bf16[2,2,384,768]{3,2,1,0:T(8,128)(2,1)S(1)}, u32[]{:S(2)}, u32[]{:S(2)}) collective-permute-start(bf16[2,2,384,768]{3,2,1,0:T(8,128)(2,1)S(1)} %get-tuple-element.293.refs_1_), channel_id=1, source_target_pairs={{0,16},{16,0},{1,17},{17,1},{2,18},{18,2},{3,19},{19,3},{4,20},{20... | collective-permute-start | bytes 7077896 | tf_op jit(solution)/shard_map/ppermute | solution.py:49
  188.6 14.8 %collective-permute-start.37 = (bf16[880,256]{1,0:T(8,128)(2,1)S(1)}, bf16[880,256]{1,0:T(8,128)(2,1)S(1)}, u32[]{:S(2)}, u32[]{:S(2)}) collective-permute-start(bf16[880,256]{1,0:T(8,128)(2,1)S(1)} %collective-permute-done.35.refs_1_.refs_2_), channel_id=1, source_target_pairs={{0,1},{1,0},{2,3},{3,2},{4,5},{5,4},{6,7},{7,6},{8,9},{9,8},{10,11... | collective-permute-start | bytes 1351688 | tf_op jit(solution)/shard_map/ppermute | solution.py:776
  204.1 3.8 %collective-permute-start.41 = (bf16[2,2,880,256]{3,2,1,0:T(8,128)(2,1)S(1)}, bf16[2,2,880,256]{3,2,1,0:T(8,128)(2,1)S(1)}, u32[]{:S(2)}, u32[]{:S(2)}) collective-permute-start(bf16[2,2,880,256]{3,2,1,0:T(8,128)(2,1)S(1)} %get-tuple-element.297.refs_1_), channel_id=1, source_target_pairs={{0,16},{16,0},{1,17},{17,1},{2,18},{18,2},{3,19},{19,3},{4,20},{20... | collective-permute-start | bytes 5406728 | tf_op jit(solution)/shard_map/ppermute | solution.py:49
  (28 other events, 127.5 us)

commit v3 on v2

--- a/solution.py
+++ b/solution.py
@@ -82,6 +82,15 @@
         )
         hit = here if hit is None else hit | here
     return low(jnp.where(hit, 1.0, 0.0))
+
+
+def packed_rows(values, images):
+    return low(matmul(one_hot_rows(PAD_E, VIS, images, True), low(values)))
+
+
+def padded_sum(part_ref, other_ref, images):
+    spread = one_hot_rows(PAD_E, VIS, images)
+    return matmul(spread, part_ref[...]) + matmul(spread, other_ref[...])
 
 
 def head_masks(head_size):
@@ -168,7 +177,7 @@
         out_specs=[pl.BlockSpec(memory_space=pltpu.VMEM)] * (len(outs) + 1),
         scratch_shapes=scratch,
         compiler_params=pltpu.CompilerParams(vmem_limit_bytes=memory * MIB),
-        cost_estimate=pl.CostEstimate(flops=30000000000, bytes_accessed=1, transcendentals=0),
+        cost_estimate=pl.CostEstimate(flops=36000000000, bytes_accessed=1, transcendentals=0),
         name=name,
     )(*arguments, *before)
     order.append(results[-1])
@@ -222,7 +231,7 @@
         )
         weights_ref[group] = weights_low
         mix_ref[:, lanes] = mixture
-    part_ref[...] = low(matmul(mix_ref[...], out_w_ref[...]))
+    part_ref[...] = packed_rows(matmul(mix_ref[...], out_w_ref[...]), images)
 
 
 def mlp_forward(middle, gain, shift, fc1_ref, bias_ref, fc2_ref, normed_ref, hidden_ref, slope_ref):
@@ -254,12 +263,12 @@
     part_two_ref, middle_ref, normed_ref, hidden_ref, slope_ref, send_ref,
 ):
     vec = full(vec_ref[...])
-    middle = full(x_ref[...]) + pair(part_ref[...], other_ref[...]) + vec[2:3]
+    middle = full(x_ref[...]) + padded_sum(part_ref, other_ref, x_ref.shape[0] // PAD_E) + vec[2:3]
     middle_ref[...] = middle
     part, _ = mlp_forward(
         middle, vec[3:4], vec[4:5], fc1_ref, bias_ref, fc2_ref, normed_ref, hidden_ref, slope_ref
     )
-    part_two_ref[...] = part
+    part_two_ref[...] = packed_rows(part, x_ref.shape[0] // PAD_E)
     enc_forward_send(place_ref, first_normed_ref, mix_ref, normed_ref, hidden_ref, send_ref)
 
 
@@ -268,7 +277,7 @@
     middle_ref, normed_ref, hidden_ref, slope_ref, send_ref,
 ):
     vec = full(vec_ref[...])
-    middle = full(x_ref[...]) + pair(part_ref[...], other_ref[...]) + vec[2:3]
+    middle = full(x_ref[...]) + padded_sum(part_ref, other_ref, x_ref.shape[0] // PAD_E) + vec[2:3]
     middle_ref[...] = middle
     mlp_forward(middle, vec[3:4], vec[4:5], fc1_ref, bias_ref, None, normed_ref, hidden_ref, slope_ref)
     enc_forward_send(place_ref, first_normed_ref, mix_ref, normed_ref, hidden_ref, send_ref)
@@ -293,7 +302,7 @@
 ):
     width = qkv_ref.shape[2]
     vec = full(vec_ref[...])
-    encoded = middle_ref[...] + pair(part_ref[...], other_ref[...]) + full(enc_vec_ref[...])[5:6]
+    encoded = middle_ref[...] + padded_sum(part_ref, other_ref, images) + full(enc_vec_ref[...])[5:6]
     enc_pad = low(encoded * live_rows(count_ref[0], images * PAD_E, PAD_E))
     enc_pad_ref[...] = enc_pad
     enc_out_ref[...] = low(matmul(one_hot_rows(PAD_E, VIS, images, True), enc_pad))
@@ -461,7 +470,7 @@
     slope = jnp.concatenate([slope_a[...], slope_b[...]], axis=0)
     up_grad = low(full(slope) * right_product(stacked_rows(cot_a, cot_b), fc2_ref[...]))
     up_ref[...] = up_grad
-    part_ref[...] = low(right_product(up_grad, fc1_ref[...]))
+    part_ref[...] = packed_rows(right_product(up_grad, fc1_ref[...]), up_grad.shape[0] // PAD_E)
     send_ref[...] = up_ref[:, chunk(2 * (1 - place_ref[0]) + place_ref[1], send_ref.shape[1])]
 
 
@@ -473,7 +482,7 @@
     vec = full(vec_ref[...])
     own = middle_a.shape[0]
     cot = full(stacked_rows(cot_a, cot_b))
-    two_grad = pair(part_in_ref[...], other_ref[...])
+    two_grad = padded_sum(part_in_ref, other_ref, 2 * images)
     xhat, scale = normalize(stacked_rows(middle_a, middle_b))
     middle_grad = cot + norm_back(two_grad, vec[3:4], xhat, scale)
     middle_grad_ref[...] = middle_grad
@@ -482,7 +491,7 @@
     mixture_grad = low(right_product(middle_low, out_w_ref[...]))
     attention_back(0, images, PAD_E, True, head_size, mixture_grad, proj_a, weights_a, stacked_ref)
     attention_back(own, images, PAD_E, True, head_size, mixture_grad, proj_b, weights_b, stacked_ref)
-    part_ref[...] = normed_back(stacked_ref, qkv_ref)
+    part_ref[...] = packed_rows(normed_back(stacked_ref, qkv_ref), 2 * images)
     width = qkv_ref.shape[2]
 
     @pl.when(place_ref[1] == 0)
@@ -510,7 +519,7 @@
 ):
     vec = full(vec_ref[...])
     own = x_a.shape[0]
-    one_grad = pair(part_ref[...], other_ref[...])
+    one_grad = padded_sum(part_ref, other_ref, 2 * images)
     xhat, scale = normalize(full(stacked_rows(x_a, x_b)))
     grad = middle_grad_ref[:own] + norm_back(one_grad[:own], vec[0:1], xhat[:own], scale[:own])
     take = full(one_hot_rows(PAD_E, VIS, images, True))
@@ -931,7 +940,7 @@
         return call(
             functools.partial(enc_attend_kernel, images, enc_size),
             [
-                shaped((rows_e, enc_width)),
+                shaped((images * VIS, enc_width)),
                 shaped((rows_e, enc_width)),
                 shaped((rows_e, enc_width)),
                 shaped((3, rows_e, enc_local)),
@@ -950,7 +959,7 @@
     part_two, middle, normed_two, hidden, slope, forward_send = call(
         enc_hidden_kernel,
         [
-            shaped((rows_e, enc_width)),
+            shaped((images * VIS, enc_width)),
             shaped((rows_e, enc_width), FULL),
             shaped((rows_e, enc_width)),
             shaped((rows_e, enc_mlp)),
@@ -1085,11 +1094,10 @@
     d3_other = swap(d3_send, "section")
     side_cot, d3_keep = lax.optimization_barrier((side_cot, d3_keep))
     side_over_cot = swap(side_cot, "section")
-
     part, up, up_send = call(
         enc_hidden_back_kernel,
         [
-            shaped((2 * rows_e, enc_width)),
+            shaped((2 * images * VIS, enc_width)),
             shaped((2 * rows_e, enc_mlp)),
             shaped((2 * rows_e, enc_mlp // 4)),
         ],
@@ -1113,7 +1121,7 @@
     back_part, middle_grad, middle_low, stacked, middle_two_sums, bias_sum, enc_up_sum, e3_send = call(
         functools.partial(enc_attend_back_kernel, images, enc_size),
         [
-            shaped((2 * rows_e, enc_width)),
+            shaped((2 * images * VIS, enc_width)),
             shaped((2 * rows_e, enc_width), FULL),
             shaped((2 * rows_e, enc_width)),
             shaped((3, 2 * rows_e, enc_local)),
@@ -1130,10 +1138,6 @@
     back_part_other = swap(back_part, "tensor")
     d1 = cross_end(order, d1, d1_arrived)
     d1_spread = spread(d1)
-    e1 = add(order, e1_mine, e1_arrived, [e3_over])
-    dec_part_two, e1 = lax.optimization_barrier((dec_part_two, e1))
-    dec_part_two_other = swap(dec_part_two, "tensor")
-    e1_arrived = cross_start(e1)
     few = 32
     grad_in, small = call(
         functools.partial(enc_start_back_kernel, images),
@@ -1141,6 +1145,10 @@
         x, side_x, back_part, back_part_other, enc_vec, middle_grad, middle_two_sums, enc_up_sum, bias_sum,
         scratch=[pltpu.VMEM((few, enc_width), FULL)], name="enc_start_back",
     )
+    e1 = add(order, e1_mine, e1_arrived, after=[e3_over])
+    dec_part_two, e1 = lax.optimization_barrier((dec_part_two, e1))
+    dec_part_two_other = swap(dec_part_two, "tensor")
+    e1_arrived = cross_start(e1)
     e3_mine, e3_theirs = call(
         last_weights_kernel,
         [

time: 214 us -> 213 us (level)
  no operation moved by 1% of the time
where the time goes in v3:
time: 213 us
  waiting for transfers between devices  107 us (50%)
  Pallas kernels  63.1 us (30%)
  starting transfers between devices  38.4 us (18%)
    ppermute x20, waiting for transfers between devices, flip(): lax.ppermute(value, 'dp', [(i, i ^ step) for i in range(lax.axis_size('dp...  80.4 us
    pallas_call x35, Pallas kernels, kernel_call(): pl.pallas_call(run, out_shape=[jax.ShapeDtypeStruct(x.shape, x.dtype) for...  63.1 us
    ppermute x22, waiting for transfers between devices, swap(): lax.ppermute(value, axis, [(i, i ^ 1) for i in range(lax.axis_size(axis))])  26.7 us
    ppermute x20, starting transfers between devices, flip(): lax.ppermute(value, 'dp', [(i, i ^ step) for i in range(lax.axis_size('dp...  24.9 us
    ppermute x22, starting transfers between devices, swap(): lax.ppermute(value, axis, [(i, i ^ 1) for i in range(lax.axis_size(axis))])  13.5 us
  transfers between devices with their start and end apart: 42, of which 22 were waited for; matrix products, arithmetic and copies ran while one was open for 0% of the time, Pallas kernels for 24%

profile of v3, /device:TPU:0, one launch (start us, length us, event | category | flops | bytes accessed | tf_op | source)
XLA Modules:
  0.0 213.0 jit_solution(14987251926774795617)
XLA Ops:
  1.3 4.6 %enc_attend.2 = (bf16[98,768]{1,0:T(8,128)(2,1)}, bf16[128,768]{1,0:T(8,128)(2,1)}, bf16[128,768]{1,0:T(8,128)(2,1)}, bf16[3,128,384]{2,1,0:T(8,128)(2,1)}, bf16...) custom-call(s32[3]{0:T(128)} %pad_add_fusion.refs_0_.refs_1_, bf16[98,2,768]{2,1,0:T(2,128)(2,1)} %bitcast.24, ...), custom_call_target="tpu_custom_call" | custom-call | flops 35999997952 | bytes 1 | tf_op jit(solution)/shard_map/enc_attend/pallas_call | solution.py:173
  6.1 3.0 %collective-permute-start.1 = (bf16[98,768]{1,0:T(8,128)(2,1)S(1)}, bf16[98,768]{1,0:T(8,128)(2,1)S(1)}, u32[]{:S(2)}, u32[]{:S(2)}) collective-permute-start(bf16[98,768]{1,0:T(8,128)(2,1)S(1)} %dynamic-slice_bitcast_fusion.1), channel_id=1, source_target_pairs={{0,1},{1,0},{2,3},{3,2},{4,5},{5,4},{6,7},{7,6},{8,9},{9,8},{10,11... | collective-permute-start | bytes 451592 | tf_op jit(solution)/shard_map/ppermute | solution.py:785
  9.1 1.5 collective-permute-start
  10.6 2.6 %collective-permute-done.1.refs_1_ = bf16[98,768]{1,0:T(8,128)(2,1)S(1)} collective-permute-done((bf16[98,768]{1,0:T(8,128)(2,1)S(1)}, bf16[98,768]{1,0:T(8,128)(2,1)S(1)}, u32[]{:S(2)}, u32[]{:S(2)}) %collective-permute-start.1) | collective-permute-done | bytes 150560 | tf_op jit(solution)/shard_map/ppermute | solution.py:785
  14.0 2.2 %enc_attend.3 = (bf16[98,768]{1,0:T(8,128)(2,1)S(1)}, bf16[128,768]{1,0:T(8,128)(2,1)S(1)}, bf16[128,768]{1,0:T(8,128)(2,1)S(1)}, bf16[3,128,384]{2,1,0:T(8,128)...) custom-call(s32[3]{0:T(128)S(1)} %copy-done.4, ...), custom_call_target="tpu_custom_call" | custom-call | flops 35999997952 | bytes 1 | tf_op jit(solution)/shard_map/enc_attend/pallas_call | solution.py:173
  16.5 2.3 %enc_hidden.1 = (bf16[98,768]{1,0:T(8,128)(2,1)S(1)}, f32[128,768]{1,0:T(8,128)S(1)}, bf16[128,768]{1,0:T(8,128)(2,1)S(1)}, bf16[128,1536]{1,0:T(8,128)(2,1)S(1)...) custom-call(s32[3]{0:T(128)S(1)} %copy-done.4, ...), custom_call_target="tpu_custom_call" | custom-call | flops 35999997952 | bytes 1 | tf_op jit(solution)/shard_map/enc_hidden/pallas_call | solution.py:173
  18.7 1.8 collective-permute-start.2
  21.6 4.1 %collective-permute-done.2.refs_4_ = bf16[98,768]{1,0:T(8,128)(2,1)S(1)} collective-permute-done((bf16[98,768]{1,0:T(8,128)(2,1)S(1)}, bf16[98,768]{1,0:T(8,128)(2,1)S(1)}, u32[]{:S(2)}, u32[]{:S(2)}) %collective-permute-start.2) | collective-permute-done | bytes 150560 | tf_op jit(solution)/shard_map/ppermute | solution.py:49
  25.8 4.4 %dec_attend.1 = (bf16[416,512]{1,0:T(8,128)(2,1)S(1)}, bf16[98,768]{1,0:T(8,128)(2,1)S(1)}, bf16[128,768]{1,0:T(8,128)(2,1)S(1)}, f32[416,512]{1,0:T(8,128)S(1)}...) custom-call(s32[1]{0:T(128)} %bitcast.3.refs_0_, ...), custom_call_target="tpu_custom_call" | custom-call | flops 35999997952 | bytes 1 | tf_op jit(solution)/shard_map/dec_attend/pallas_call | solution.py:173
  30.3 1.6 collective-permute-start.4
  31.9 1.6 enc_side_hidden.1
  33.7 8.8 %collective-permute-done.4.refs_4_ = bf16[416,512]{1,0:T(8,128)(2,1)S(1)} collective-permute-done((bf16[416,512]{1,0:T(8,128)(2,1)S(1)}, bf16[416,512]{1,0:T(8,128)(2,1)S(1)}, u32[]{:S(2)}, u32[]{:S(2)}) %collective-permute-start.4) | collective-permute-done | bytes 426016 | tf_op jit(solution)/shard_map/ppermute | solution.py:49
  42.5 4.5 %dec_hidden.1 = (bf16[416,512]{1,0:T(8,128)(2,1)S(1)}, bf16[416,512]{1,0:T(8,128)(2,1)S(1)}, f32[416,512]{1,0:T(8,128)S(1)}, bf16[416,512]{1,0:T(8,128)(2,1)S(1)...) custom-call(s32[1]{0:T(128)} %bitcast.3.refs_0_, ...), custom_call_target="tpu_custom_call" | custom-call | flops 35999997952 | bytes 1 | tf_op jit(solution)/shard_map/dec_hidden/pallas_call | solution.py:173
  47.0 1.6 collective-permute-start.7
  48.6 1.5 enc_out_both.1
  50.1 2.4 %collective-permute-done.8.refs_5_ = bf16[416,2304]{1,0:T(8,128)(2,1)S(1)} collective-permute-done((bf16[416,2304]{1,0:T(8,128)(2,1)S(1)}, bf16[416,2304]{1,0:T(8,128)(2,1)S(1)}, u32[]{:S(2)}, u32[]{:S(2)}) %collective-permute-start.8) | collective-permute-done | bytes 1916960 | tf_op jit(solution)/shard_map/ppermute | solution.py:49
  52.5 1.8 dec_hidden_weights.1
  54.4 1.6 collective-permute-start.12
  56.0 2.5 %collective-permute-done.7.refs_4_ = bf16[416,512]{1,0:T(8,128)(2,1)S(1)} collective-permute-done((bf16[416,512]{1,0:T(8,128)(2,1)S(1)}, bf16[416,512]{1,0:T(8,128)(2,1)S(1)}, u32[]{:S(2)}, u32[]{:S(2)}) %collective-permute-start.7) | collective-permute-done | bytes 426016 | tf_op jit(solution)/shard_map/ppermute | solution.py:49
  58.5 4.7 %dec_attend_back.1 = (bf16[416,512]{1,0:T(8,128)(2,1)S(1)}, f32[416,512]{1,0:T(8,128)S(1)}, bf16[416,512]{1,0:T(8,128)(2,1)S(1)}, bf16[3,416,256]{2,1,0:T(8,128)...) custom-call(s32[3]{0:T(128)S(1)} %copy-done.4, ...), custom_call_target="tpu_custom_call" | custom-call | flops 35999997952 | bytes 1 | tf_op jit(solution)/shard_map/dec_attend_back/pallas_call | solution.py:173
  63.2 1.6 collective-permute-start.10
  64.8 3.6 %collective-permute-done.12.refs_2_ = bf16[2,256,512]{2,1,0:T(8,128)(2,1)S(1)} collective-permute-done((bf16[2,256,512]{2,1,0:T(8,128)(2,1)S(1)}, bf16[2,256,512]{2,1,0:T(8,128)(2,1)S(1)}, u32[]{:S(2)}, u32[]{:S(2)}) %collective-permute-start.12) | collective-permute-done | bytes 524320 | tf_op jit(solution)/shard_map/ppermute | solution.py:785
  69.1 1.3 dec_head_weights.1
  70.4 1.6 collective-permute-start.14
  72.0 1.7 collective-permute-done.10.refs_4_
  73.8 1.9 dec_start_back.1
  75.7 1.8 collective-permute-start.13
  78.7 0.9 dec_bridge_weights.1
  79.6 3.4 %collective-permute-done.13.refs_2_.refs_4_ = bf16[128,768]{1,0:T(8,128)(2,1)S(1)} collective-permute-done((bf16[128,768]{1,0:T(8,128)(2,1)S(1)}, bf16[128,768]{1,0:T(8,128)(2,1)S(1)}, u32[]{:S(2)}, u32[]{:S(2)}) %collective-permute-start.13) | collective-permute-done | bytes 196640 | tf_op jit(solution)/shard_map/ppermute | solution.py:785
  83.1 1.8 collective-permute-start.21
  85.1 2.3 %enc_hidden_back.1 = (bf16[196,768]{1,0:T(8,128)(2,1)S(1)}, bf16[256,1536]{1,0:T(8,128)(2,1)S(1)}, bf16[256,384]{1,0:T(8,128)(2,1)S(1)}, f32[8,128]{1,0:T(8,128)S(1)}) custom-call(s32[3]{0:T(128)S(1)} %copy-done.4, bf16[128,768]{1,0:T(8,128)(2,1)S(1)} %get-tuple-element.217.refs_1_.refs_3_, bf16[128,768]{1,0:T(8,128)(2,1)S(1)} %collective-permute-done.13.refs_2_.refs_4_, ...), custom_call_target="tpu_custom_call" | custom-call | flops 35999997952 | bytes 1 | tf_op jit(solution)/shard_map/enc_hidden_back/pallas_call | solution.py:173
  87.8 1.3 collective-permute-start.20
  89.0 0.7 fold.3
  89.7 1.6 collective-permute-start.22
  91.3 1.8 enc_hidden_weights.1
  93.1 1.6 collective-permute-done.21.refs_1_
  94.8 2.8 %collective-permute-start.24 = (bf16[384,512]{1,0:T(8,128)(2,1)S(1)}, bf16[384,512]{1,0:T(8,128)(2,1)S(1)}, u32[]{:S(2)}, u32[]{:S(2)}) collective-permute-start(bf16[384,512]{1,0:T(8,128)(2,1)S(1)} %get-tuple-element.263.refs_0_), channel_id=1, source_target_pairs={{0,4},{1,5},{2,6},{3,7},{4,0},{5,1},{6,2},{7,3},{8,12},{9,13},{10,... | collective-permute-start | bytes 1179656 | tf_op jit(solution)/shard_map/ppermute | solution.py:785
  97.6 1.6 collective-permute-start.19
  99.2 4.6 %enc_attend_back.1 = (bf16[196,768]{1,0:T(8,128)(2,1)S(1)}, f32[256,768]{1,0:T(8,128)S(1)}, bf16[256,768]{1,0:T(8,128)(2,1)S(1)}, bf16[3,256,384]{2,1,0:T(8,128)...) custom-call(s32[3]{0:T(128)S(1)} %copy-done.4, ...), custom_call_target="tpu_custom_call" | custom-call | flops 35999997952 | bytes 1 | tf_op jit(solution)/shard_map/enc_attend_back/pallas_call | solution.py:173
  103.8 1.3 collective-permute-start.23
  105.1 10.0 %collective-permute-done.24.refs_1_ = bf16[384,512]{1,0:T(8,128)(2,1)S(1)} collective-permute-done((bf16[384,512]{1,0:T(8,128)(2,1)S(1)}, bf16[384,512]{1,0:T(8,128)(2,1)S(1)}, u32[]{:S(2)}, u32[]{:S(2)}) %collective-permute-start.24) | collective-permute-done | bytes 393248 | tf_op jit(solution)/shard_map/ppermute | solution.py:785
  115.3 1.6 collective-permute-start.28
  117.5 1.8 enc_start_back.1
  119.4 1.6 collective-permute-done.19.refs_1_
  121.1 1.4 collective-permute-start.26
  122.5 1.9 collective-permute-start.31
  124.3 8.7 %collective-permute-done.27.refs_14_.refs_2_ = bf16[384,512]{1,0:T(8,128)(2,1)S(1)} collective-permute-done((bf16[384,512]{1,0:T(8,128)(2,1)S(1)}, bf16[384,512]{1,0:T(8,128)(2,1)S(1)}, u32[]{:S(2)}, u32[]{:S(2)}) %collective-permute-start.27) | collective-permute-done | bytes 393248 | tf_op jit(solution)/shard_map/ppermute | solution.py:785
  133.1 2.0 collective-permute-start.29
  135.1 1.3 last_weights.1
  136.5 6.4 %collective-permute-done.29.refs_4_ = bf16[384,512]{1,0:T(8,128)(2,1)S(1)} collective-permute-done((bf16[384,512]{1,0:T(8,128)(2,1)S(1)}, bf16[384,512]{1,0:T(8,128)(2,1)S(1)}, u32[]{:S(2)}, u32[]{:S(2)}) %collective-permute-start.29) | collective-permute-done | bytes 393248 | tf_op jit(solution)/shard_map/ppermute | solution.py:785
  143.7 1.9 dec_out.1
  145.5 4.2 %collective-permute-done.31.refs_1_ = bf16[384,768]{1,0:T(8,128)(2,1)S(1)} collective-permute-done((bf16[384,768]{1,0:T(8,128)(2,1)S(1)}, bf16[384,768]{1,0:T(8,128)(2,1)S(1)}, u32[]{:S(2)}, u32[]{:S(2)}) %collective-permute-start.31) | collective-permute-done | bytes 589856 | tf_op jit(solution)/shard_map/ppermute | solution.py:785
  150.5 11.6 %collective-permute-done.30.refs_1_ = bf16[880,256]{1,0:T(8,128)(2,1)S(1)} collective-permute-done((bf16[880,256]{1,0:T(8,128)(2,1)S(1)}, bf16[880,256]{1,0:T(8,128)(2,1)S(1)}, u32[]{:S(2)}, u32[]{:S(2)}) %collective-permute-start.30) | collective-permute-done | bytes 450592 | tf_op jit(solution)/shard_map/ppermute | solution.py:785
  162.4 10.2 %collective-permute-done.34.refs_1_.refs_2_ = bf16[384,768]{1,0:T(8,128)(2,1)S(1)} collective-permute-done((bf16[384,768]{1,0:T(8,128)(2,1)S(1)}, bf16[384,768]{1,0:T(8,128)(2,1)S(1)}, u32[]{:S(2)}, u32[]{:S(2)}) %collective-permute-start.34) | collective-permute-done | bytes 589856 | tf_op jit(solution)/shard_map/ppermute | solution.py:785
  173.1 3.5 %dec_whole.1 = (f32[512,1024]{1,0:T(8,128)}, f32[1024,512]{1,0:T(8,128)}, f32[3,512,256]{2,1,0:T(8,128)}, f32[256,512]{1,0:T(8,128)}, f32[8,128]{1,0:T(8,128)S(1)}) custom-call(s32[3]{0:T(128)S(1)} %copy-done.4, bf16[2,2,384,512]{3,2,1,0:T(8,128)(2,1)S(1)} %get-tuple-element.286.refs_1_, bf16[2,2,384,512]{3,2,1,0:T(8,128)(2,1)S(1)} %collective-permute-done.33.refs_2_, ...), custom_call_target="tpu_custom_call" | custom-call | flops 35999997952 | bytes 1 | tf_op jit(solution)/shard_map/dec_whole/pallas_call | solution.py:173
  177.2 1.4 collective-permute-done.32.refs_1_
  178.7 0.9 collective-permute-start.36
  179.6 9.2 %collective-permute-done.39.refs_4_ = bf16[384,768]{1,0:T(8,128)(2,1)S(1)} collective-permute-done((bf16[384,768]{1,0:T(8,128)(2,1)S(1)}, bf16[384,768]{1,0:T(8,128)(2,1)S(1)}, u32[]{:S(2)}, u32[]{:S(2)}) %collective-permute-start.39) | collective-permute-done | bytes 589856 | tf_op jit(solution)/shard_map/ppermute | solution.py:785
  188.8 0.7 pack.4
  190.8 3.3 %collective-permute-done.40.refs_2_ = bf16[2,2,384,768]{3,2,1,0:T(8,128)(2,1)S(1)} collective-permute-done((bf16[2,2,384,768]{3,2,1,0:T(8,128)(2,1)S(1)}, bf16[2,2,384,768]{3,2,1,0:T(8,128)(2,1)S(1)}, u32[]{:S(2)}, u32[]{:S(2)}) %collective-permute-start.40) | collective-permute-done | bytes 2359328 | tf_op jit(solution)/shard_map/ppermute | solution.py:49
  194.1 4.9 %enc_hidden_whole.1 = (f32[768,1536]{1,0:T(8,128)}, f32[1536,768]{1,0:T(8,128)}, f32[8,128]{1,0:T(8,128)S(1)}) custom-call(s32[3]{0:T(128)S(1)} %copy-done.4, bf16[2,2,384,768]{3,2,1,0:T(8,128)(2,1)S(1)} %get-tuple-element.293.refs_1_, bf16[2,2,384,768]{3,2,1,0:T(8,128)(2,1)S(1)} %collective-permute-done.40.refs_2_, f32[8,128]{1,0:T(8,128)S(1)} %get-tuple-element.295.refs_3_), custom_call_target="tpu_custom_call" | custom-call | flops 35999997952 | bytes 1 | tf_op jit(solution)/shard_map/enc_hidden_whole/pallas_call | solution.py:173
  199.0 5.4 %collective-permute-done.37.refs_4_ = bf16[880,256]{1,0:T(8,128)(2,1)S(1)} collective-permute-done((bf16[880,256]{1,0:T(8,128)(2,1)S(1)}, bf16[880,256]{1,0:T(8,128)(2,1)S(1)}, u32[]{:S(2)}, u32[]{:S(2)}) %collective-permute-start.37) | collective-permute-done | bytes 450592 | tf_op jit(solution)/shard_map/ppermute | solution.py:785
  205.2 3.7 %collective-permute-done.41.refs_2_ = bf16[2,2,880,256]{3,2,1,0:T(8,128)(2,1)S(1)} collective-permute-done((bf16[2,2,880,256]{3,2,1,0:T(8,128)(2,1)S(1)}, bf16[2,2,880,256]{3,2,1,0:T(8,128)(2,1)S(1)}, u32[]{:S(2)}, u32[]{:S(2)}) %collective-permute-start.41) | collective-permute-done | bytes 1802272 | tf_op jit(solution)/shard_map/ppermute | solution.py:49
  208.9 3.5 %last_whole.1 = (f32[3,768,384]{2,1,0:T(8,128)}, f32[384,768]{1,0:T(8,128)}, f32[6,768]{1,0:T(8,128)}, f32[1,1536]{1,0:T(1,128)S(1)}, f32[2,384]{1,0:T(2,128)}, ...) custom-call(s32[3]{0:T(128)S(1)} %copy-done.4, ...), custom_call_target="tpu_custom_call" | custom-call | flops 35999997952 | bytes 1 | tf_op jit(solution)/shard_map/last_whole/pallas_call | solution.py:173
  (165 shorter events, 12.1 us)
Async XLA Ops:
  0.7 20.5 %copy-start = (bf16[2,392,512]{2,1,0:T(8,128)(2,1)S(1)}, bf16[2,392,512]{2,1,0:T(8,128)(2,1)}, u32[]{:S(2)}) copy-start(bf16[2,392,512]{2,1,0:T(8,128)(2,1)} %param.39) | copy-start | bytes 2408452
  1.3 11.9 %copy-start.4 = (s32[3]{0:T(128)S(1)}, s32[3]{0:T(128)}, u32[]{:S(2)}) copy-start(s32[3]{0:T(128)} %pad_add_fusion.refs_0_.refs_1_) | copy-start | bytes 40
  1.3 11.9 %copy-start.9 = (bf16[768,3,384]{2,0,1:T(8,128)(2,1)S(1)}, bf16[768,3,384]{2,0,1:T(8,128)(2,1)}, u32[]{:S(2)}) copy-start(bf16[768,3,384]{2,0,1:T(8,128)(2,1)} %param.24) | copy-start | bytes 5308420
  1.3 11.9 %copy-start.15 = (bf16[384,768]{1,0:T(8,128)(2,1)S(1)}, bf16[384,768]{1,0:T(8,128)(2,1)}, u32[]{:S(2)}) copy-start(bf16[384,768]{1,0:T(8,128)(2,1)} %refs_13_.1) | copy-start | bytes 1769476
  1.3 11.9 %copy-start.22 = (bf16[6,768]{1,0:T(8,128)(2,1)S(1)}, bf16[6,768]{1,0:T(8,128)(2,1)}, u32[]{:S(2)}) copy-start(bf16[6,768]{1,0:T(8,128)(2,1)} %refs_4_.6) | copy-start | bytes 27652
  1.3 11.9 %copy-start.24 = (bf16[2,384]{1,0:T(2,128)(2,1)S(1)}, bf16[2,384]{1,0:T(2,128)(2,1)}, u32[]{:S(2)}) copy-start(bf16[2,384]{1,0:T(2,128)(2,1)} %refs_4_.5) | copy-start | bytes 4612
  6.1 7.1 %collective-permute-start.1 = (bf16[98,768]{1,0:T(8,128)(2,1)S(1)}, bf16[98,768]{1,0:T(8,128)(2,1)S(1)}, u32[]{:S(2)}, u32[]{:S(2)}) collective-permute-start(bf16[98,768]{1,0:T(8,128)(2,1)S(1)} %dynamic-slice_bitcast_fusion.1), channel_id=1, source_target_pairs={{0,1},{1,0},{2,3},{3,2},{4,5},{5,4},{6,7},{7,6},{8,9},{9,8},{10,11... | collective-permute-start | bytes 451592 | tf_op jit(solution)/shard_map/ppermute | solution.py:785
  9.1 7.1 %collective-permute-start = (bf16[98,768]{1,0:T(8,128)(2,1)}, bf16[98,768]{1,0:T(8,128)(2,1)S(1)}, u32[]{:S(2)}, u32[]{:S(2)}) collective-permute-start(bf16[98,768]{1,0:T(8,128)(2,1)} %get-tuple-element.169.refs_3_), channel_id=1, source_target_pairs={{0,8},{8,0},{1,9},{9,1},{2,10},{10,2},{3,11},{11,3},{4,12},{12,4},... | collective-permute-start | bytes 451592 | tf_op jit(solution)/shard_map/ppermute | solution.py:49
  16.2 15.7 %copy-start.36 = (bf16[128,768]{1,0:T(8,128)(2,1)}, bf16[128,768]{1,0:T(8,128)(2,1)S(1)}, u32[]{:S(2)}) copy-start(bf16[128,768]{1,0:T(8,128)(2,1)S(1)} %get-tuple-element.183.refs_7_.refs_2_) | copy-start | bytes 589828
  16.2 15.6 %copy-start.38 = (bf16[128,768]{1,0:T(8,128)(2,1)}, bf16[128,768]{1,0:T(8,128)(2,1)S(1)}, u32[]{:S(2)}) copy-start(bf16[128,768]{1,0:T(8,128)(2,1)S(1)} %get-tuple-element.181.refs_1_) | copy-start | bytes 589828
  16.2 15.6 %copy-start.42 = (bf16[128,384]{1,0:T(8,128)(2,1)}, bf16[128,384]{1,0:T(8,128)(2,1)S(1)}, u32[]{:S(2)}) copy-start(bf16[128,384]{1,0:T(8,128)(2,1)S(1)} %get-tuple-element.184.refs_8_.refs_5_) | copy-start | bytes 294916
  16.4 9.3 %copy-start.12 = (bf16[512,3,256]{2,0,1:T(8,128)(2,1)S(1)}, bf16[512,3,256]{2,0,1:T(8,128)(2,1)}, u32[]{:S(2)}) copy-start(bf16[512,3,256]{2,0,1:T(8,128)(2,1)} %param.33) | copy-start | bytes 2359300
  16.4 9.3 %copy-start.13 = (bf16[768,512]{1,0:T(8,128)(2,1)S(1)}, bf16[768,512]{1,0:T(8,128)(2,1)}, u32[]{:S(2)}) copy-start(bf16[768,512]{1,0:T(8,128)(2,1)} %refs_7_.4) | copy-start | bytes 2359300
  16.4 9.3 %copy-start.19 = (bf16[256,512]{1,0:T(8,128)(2,1)S(1)}, bf16[256,512]{1,0:T(8,128)(2,1)}, u32[]{:S(2)}) copy-start(bf16[256,512]{1,0:T(8,128)(2,1)} %refs_9_.3) | copy-start | bytes 786436
  16.4 9.3 %copy-start.20 = (bf16[196,512]{1,0:T(8,128)(2,1)S(1)}, bf16[196,512]{1,0:T(8,128)(2,1)}, u32[]{:S(2)}) copy-start(bf16[196,512]{1,0:T(8,128)(2,1)} %refs_8_.2) | copy-start | bytes 602116
  18.7 11.4 %copy-start.28 = (f32[128,768]{1,0:T(8,128)}, f32[128,768]{1,0:T(8,128)S(1)}, u32[]{:S(2)}) copy-start(f32[128,768]{1,0:T(8,128)S(1)} %get-tuple-element.175.refs_2_.refs_1_) | copy-start | bytes 1179652
  18.7 7.0 %collective-permute-start.2 = (bf16[98,768]{1,0:T(8,128)(2,1)S(1)}, bf16[98,768]{1,0:T(8,128)(2,1)S(1)}, u32[]{:S(2)}, u32[]{:S(2)}) collective-permute-start(bf16[98,768]{1,0:T(8,128)(2,1)S(1)} %get-tuple-element.176.refs_3_), channel_id=1, source_target_pairs={{0,8},{8,0},{1,9},{9,1},{2,10},{10,2},{3,11},{11,3},{4,12},{12,4},... | collective-permute-start | bytes 451592 | tf_op jit(solution)/shard_map/ppermute | solution.py:49
  21.2 10.6 %collective-permute-start.5 = (bf16[98,768]{1,0:T(8,128)(2,1)S(1)}, bf16[98,768]{1,0:T(8,128)(2,1)S(1)}, u32[]{:S(2)}, u32[]{:S(2)}) collective-permute-start(bf16[98,768]{1,0:T(8,128)(2,1)S(1)} %get-tuple-element.182.refs_3_), channel_id=1, source_target_pairs={{0,8},{8,0},{1,9},{9,1},{2,10},{10,2},{3,11},{11,3},{4,12},{12,4},... | collective-permute-start | bytes 451592 | tf_op jit(solution)/shard_map/ppermute | solution.py:49
  21.6 12.1 %collective-permute-start.6 = (bf16[128,1920]{1,0:T(8,128)(2,1)S(1)}, bf16[128,1920]{1,0:T(8,128)(2,1)S(1)}, u32[]{:S(2)}, u32[]{:S(2)}) collective-permute-start(bf16[128,1920]{1,0:T(8,128)(2,1)S(1)} %get-tuple-element.187), channel_id=1, source_target_pairs={{0,16},{16,0},{1,17},{17,1},{2,18},{18,2},{3,19},{19,3},{4,20},{20... | collective-permute-start | bytes 1474568 | tf_op jit(solution)/shard_map/ppermute | solution.py:49
  30.2 12.3 %copy-start.26 = (f32[416,512]{1,0:T(8,128)}, f32[416,512]{1,0:T(8,128)S(1)}, u32[]{:S(2)}) copy-start(f32[416,512]{1,0:T(8,128)S(1)} %get-tuple-element.179.refs_2_) | copy-start | bytes 2555908
  30.2 18.4 %collective-permute-start.3 = (bf16[98,768]{1,0:T(8,128)(2,1)S(1)}, bf16[98,768]{1,0:T(8,128)(2,1)S(1)}, u32[]{:S(2)}, u32[]{:S(2)}) collective-permute-start(bf16[98,768]{1,0:T(8,128)(2,1)S(1)} %get-tuple-element.178.refs_1_), channel_id=1, source_target_pairs={{0,16},{16,0},{1,17},{17,1},{2,18},{18,2},{3,19},{19,3},{4,20},{20... | collective-permute-start | bytes 451592 | tf_op jit(solution)/shard_map/ppermute | solution.py:49
  30.3 12.2 %collective-permute-start.4 = (bf16[416,512]{1,0:T(8,128)(2,1)S(1)}, bf16[416,512]{1,0:T(8,128)(2,1)S(1)}, u32[]{:S(2)}, u32[]{:S(2)}) collective-permute-start(bf16[416,512]{1,0:T(8,128)(2,1)S(1)} %get-tuple-element.180.refs_3_), channel_id=1, source_target_pairs={{0,8},{8,0},{1,9},{9,1},{2,10},{10,2},{3,11},{11,3},{4,12},{12,4},... | collective-permute-start | bytes 1277960 | tf_op jit(solution)/shard_map/ppermute | solution.py:49
  31.9 10.7 %copy-start.10 = (bf16[512,1024]{1,0:T(8,128)(2,1)S(1)}, bf16[512,1024]{1,0:T(8,128)(2,1)}, u32[]{:S(2)}) copy-start(bf16[512,1024]{1,0:T(8,128)(2,1)} %refs_6_.4) | copy-start | bytes 3145732
  31.9 10.6 %copy-start.11 = (bf16[1024,512]{1,0:T(8,128)(2,1)S(1)}, bf16[1024,512]{1,0:T(8,128)(2,1)}, u32[]{:S(2)}) copy-start(bf16[1024,512]{1,0:T(8,128)(2,1)} %refs_8_.3) | copy-start | bytes 3145732
  33.4 16.7 %collective-permute-start.9 = (bf16[128,1920]{1,0:T(8,128)(2,1)S(1)}, bf16[128,1920]{1,0:T(8,128)(2,1)S(1)}, u32[]{:S(2)}, u32[]{:S(2)}) collective-permute-start(bf16[128,1920]{1,0:T(8,128)(2,1)S(1)} %get-tuple-element.205), channel_id=1, source_target_pairs={{0,16},{16,0},{1,17},{17,1},{2,18},{18,2},{3,19},{19,3},{4,20},{20... | collective-permute-start | bytes 1474568 | tf_op jit(solution)/shard_map/ppermute | solution.py:49
  47.0 11.5 %collective-permute-start.7 = (bf16[416,512]{1,0:T(8,128)(2,1)S(1)}, bf16[416,512]{1,0:T(8,128)(2,1)S(1)}, u32[]{:S(2)}, u32[]{:S(2)}) collective-permute-start(bf16[416,512]{1,0:T(8,128)(2,1)S(1)} %get-tuple-element.195.refs_3_), channel_id=1, source_target_pairs={{0,8},{8,0},{1,9},{9,1},{2,10},{10,2},{3,11},{11,3},{4,12},{12,4},... | collective-permute-start | bytes 1277960 | tf_op jit(solution)/shard_map/ppermute | solution.py:49
  48.6 3.9 %collective-permute-start.8 = (bf16[416,2304]{1,0:T(8,128)(2,1)S(1)}, bf16[416,2304]{1,0:T(8,128)(2,1)S(1)}, u32[]{:S(2)}, u32[]{:S(2)}) collective-permute-start(bf16[416,2304]{1,0:T(8,128)(2,1)S(1)} %get-tuple-element.203), channel_id=1, source_target_pairs={{0,16},{16,0},{1,17},{17,1},{2,18},{18,2},{3,19},{19,3},{4,20},{20... | collective-permute-start | bytes 5750792 | tf_op jit(solution)/shard_map/ppermute | solution.py:49
  54.4 14.0 %collective-permute-start.12 = (bf16[2,256,512]{2,1,0:T(8,128)(2,1)S(1)}, bf16[2,256,512]{2,1,0:T(8,128)(2,1)S(1)}, u32[]{:S(2)}, u32[]{:S(2)}) collective-permute-start(bf16[2,256,512]{2,1,0:T(8,128)(2,1)S(1)} %get-tuple-element.213), channel_id=1, source_target_pairs={{0,1},{1,0},{2,3},{3,2},{4,5},{5,4},{6,7},{7,6},{8,9},{9,8},{10,11... | collective-permute-start | bytes 1572872 | tf_op jit(solution)/shard_map/ppermute | solution.py:785
  63.2 10.6 %collective-permute-start.10 = (bf16[416,512]{1,0:T(8,128)(2,1)S(1)}, bf16[416,512]{1,0:T(8,128)(2,1)S(1)}, u32[]{:S(2)}, u32[]{:S(2)}) collective-permute-start(bf16[416,512]{1,0:T(8,128)(2,1)S(1)} %get-tuple-element.207.refs_3_), channel_id=1, source_target_pairs={{0,8},{8,0},{1,9},{9,1},{2,10},{10,2},{3,11},{11,3},{4,12},{12,4},... | collective-permute-start | bytes 1277960 | tf_op jit(solution)/shard_map/ppermute | solution.py:49
  64.8 4.3 %collective-permute-start.11 = (bf16[416,1536]{1,0:T(8,128)(2,1)S(1)}, bf16[416,1536]{1,0:T(8,128)(2,1)S(1)}, u32[]{:S(2)}, u32[]{:S(2)}) collective-permute-start(bf16[416,1536]{1,0:T(8,128)(2,1)S(1)} %get-tuple-element.211), channel_id=1, source_target_pairs={{0,16},{16,0},{1,17},{17,1},{2,18},{18,2},{3,19},{19,3},{4,20},{20... | collective-permute-start | bytes 3833864 | tf_op jit(solution)/shard_map/ppermute | solution.py:49
  70.4 7.6 %collective-permute-start.14 = (bf16[2,128,512]{2,1,0:T(8,128)(2,1)S(1)}, bf16[2,128,512]{2,1,0:T(8,128)(2,1)S(1)}, u32[]{:S(2)}, u32[]{:S(2)}) collective-permute-start(bf16[2,128,512]{2,1,0:T(8,128)(2,1)S(1)} %get-tuple-element.227), channel_id=1, source_target_pairs={{0,1},{1,0},{2,3},{3,2},{4,5},{5,4},{6,7},{7,6},{8,9},{9,8},{10,11... | collective-permute-start | bytes 786440 | tf_op jit(solution)/shard_map/ppermute | solution.py:785
  75.7 9.5 %collective-permute-start.15 = (bf16[128,768]{1,0:T(8,128)(2,1)S(1)}, bf16[128,768]{1,0:T(8,128)(2,1)S(1)}, u32[]{:S(2)}, u32[]{:S(2)}) collective-permute-start(bf16[128,768]{1,0:T(8,128)(2,1)S(1)} %get-tuple-element.217.refs_1_.refs_3_), channel_id=1, source_target_pairs={{0,16},{16,0},{1,17},{17,1},{2,18},{18,2},{3,19},{19,3},{4,20},{20... | collective-permute-start | bytes 589832 | tf_op jit(solution)/shard_map/ppermute | solution.py:49
  75.7 7.3 %collective-permute-start.13 = (bf16[128,768]{1,0:T(8,128)(2,1)S(1)}, bf16[128,768]{1,0:T(8,128)(2,1)S(1)}, u32[]{:S(2)}, u32[]{:S(2)}) collective-permute-start(bf16[128,768]{1,0:T(8,128)(2,1)S(1)} %get-tuple-element.217.refs_1_.refs_3_), channel_id=1, source_target_pairs={{0,1},{1,0},{2,3},{3,2},{4,5},{5,4},{6,7},{7,6},{8,9},{9,8},{10,11... | collective-permute-start | bytes 589832 | tf_op jit(solution)/shard_map/ppermute | solution.py:785
  83.1 5.9 %collective-permute-start.16 = (bf16[128,768]{1,0:T(8,128)(2,1)S(1)}, bf16[128,768]{1,0:T(8,128)(2,1)S(1)}, u32[]{:S(2)}, u32[]{:S(2)}) collective-permute-start(bf16[128,768]{1,0:T(8,128)(2,1)S(1)} %collective-permute-done.13.refs_2_.refs_4_), channel_id=1, source_target_pairs={{0,16},{16,0},{1,17},{17,1},{2,18},{18,2},{3,19},{19,3},{4,20},{20... | collective-permute-start | bytes 589832 | tf_op jit(solution)/shard_map/ppermute | solution.py:49
  83.1 11.6 %collective-permute-start.21 = (bf16[384,512]{1,0:T(8,128)(2,1)S(1)}, bf16[384,512]{1,0:T(8,128)(2,1)S(1)}, u32[]{:S(2)}, u32[]{:S(2)}) collective-permute-start(bf16[384,512]{1,0:T(8,128)(2,1)S(1)} %get-tuple-element.254), channel_id=1, source_target_pairs={{0,2},{1,3},{2,0},{3,1},{4,6},{5,7},{6,4},{7,5},{8,10},{9,11},{10,... | collective-permute-start | bytes 1179656 | tf_op jit(solution)/shard_map/ppermute | solution.py:785
  84.9 4.1 %collective-permute-start.18 = (bf16[2,2,128,512]{3,2,1,0:T(8,128)(2,1)S(1)}, bf16[2,2,128,512]{3,2,1,0:T(8,128)(2,1)S(1)}, u32[]{:S(2)}, u32[]{:S(2)}) collective-permute-start(bf16[2,2,128,512]{3,2,1,0:T(8,128)(2,1)S(1)} %get-tuple-element.242), channel_id=1, source_target_pairs={{0,16},{16,0},{1,17},{17,1},{2,18},{18,2},{3,19},{19,3},{4,20},{20... | collective-permute-start | bytes 1572872 | tf_op jit(solution)/shard_map/ppermute | solution.py:49
  87.4 3.9 %collective-permute-start.17 = (bf16[256,384]{1,0:T(8,128)(2,1)S(1)}, bf16[256,384]{1,0:T(8,128)(2,1)S(1)}, u32[]{:S(2)}, u32[]{:S(2)}) collective-permute-start(bf16[256,384]{1,0:T(8,128)(2,1)S(1)} %get-tuple-element.240), channel_id=1, source_target_pairs={{0,16},{16,0},{1,17},{17,1},{2,18},{18,2},{3,19},{19,3},{4,20},{20... | collective-permute-start | bytes 589832 | tf_op jit(solution)/shard_map/ppermute | solution.py:49
  87.8 11.4 %collective-permute-start.20 = (bf16[196,768]{1,0:T(8,128)(2,1)S(1)}, bf16[196,768]{1,0:T(8,128)(2,1)S(1)}, u32[]{:S(2)}, u32[]{:S(2)}) collective-permute-start(bf16[196,768]{1,0:T(8,128)(2,1)S(1)} %get-tuple-element.248.refs_5_), channel_id=1, source_target_pairs={{0,8},{8,0},{1,9},{9,1},{2,10},{10,2},{3,11},{11,3},{4,12},{12,4},... | collective-permute-start | bytes 903176 | tf_op jit(solution)/shard_map/ppermute | solution.py:49
  89.7 9.5 %collective-permute-start.22 = (bf16[2,128,512]{2,1,0:T(8,128)(2,1)S(1)}, bf16[2,128,512]{2,1,0:T(8,128)(2,1)S(1)}, u32[]{:S(2)}, u32[]{:S(2)}) collective-permute-start(bf16[2,128,512]{2,1,0:T(8,128)(2,1)S(1)} %get-tuple-element.257), channel_id=1, source_target_pairs={{0,1},{1,0},{2,3},{3,2},{4,5},{5,4},{6,7},{7,6},{8,9},{9,8},{10,11... | collective-permute-start | bytes 786440 | tf_op jit(solution)/shard_map/ppermute | solution.py:785
  94.8 20.4 %collective-permute-start.24 = (bf16[384,512]{1,0:T(8,128)(2,1)S(1)}, bf16[384,512]{1,0:T(8,128)(2,1)S(1)}, u32[]{:S(2)}, u32[]{:S(2)}) collective-permute-start(bf16[384,512]{1,0:T(8,128)(2,1)S(1)} %get-tuple-element.263.refs_0_), channel_id=1, source_target_pairs={{0,4},{1,5},{2,6},{3,7},{4,0},{5,1},{6,2},{7,3},{8,12},{9,13},{10,... | collective-permute-start | bytes 1179656 | tf_op jit(solution)/shard_map/ppermute | solution.py:785
  97.6 23.3 %collective-permute-start.19 = (bf16[384,768]{1,0:T(8,128)(2,1)S(1)}, bf16[384,768]{1,0:T(8,128)(2,1)S(1)}, u32[]{:S(2)}, u32[]{:S(2)}) collective-permute-start(bf16[384,768]{1,0:T(8,128)(2,1)S(1)} %get-tuple-element.246), channel_id=1, source_target_pairs={{0,2},{1,3},{2,0},{3,1},{4,6},{5,7},{6,4},{7,5},{8,10},{9,11},{10,... | collective-permute-start | bytes 1769480 | tf_op jit(solution)/shard_map/ppermute | solution.py:785
  103.8 13.7 %collective-permute-start.23 = (bf16[196,768]{1,0:T(8,128)(2,1)S(1)}, bf16[196,768]{1,0:T(8,128)(2,1)S(1)}, u32[]{:S(2)}, u32[]{:S(2)}) collective-permute-start(bf16[196,768]{1,0:T(8,128)(2,1)S(1)} %get-tuple-element.258.refs_2_), channel_id=1, source_target_pairs={{0,8},{8,0},{1,9},{9,1},{2,10},{10,2},{3,11},{11,3},{4,12},{12,4},... | collective-permute-start | bytes 903176 | tf_op jit(solution)/shard_map/ppermute | solution.py:49
  105.1 15.8 %collective-permute-start.25 = (bf16[256,768]{1,0:T(8,128)(2,1)S(1)}, bf16[256,768]{1,0:T(8,128)(2,1)S(1)}, u32[]{:S(2)}, u32[]{:S(2)}) collective-permute-start(bf16[256,768]{1,0:T(8,128)(2,1)S(1)} %get-tuple-element.267), channel_id=1, source_target_pairs={{0,16},{16,0},{1,17},{17,1},{2,18},{18,2},{3,19},{19,3},{4,20},{20... | collective-permute-start | bytes 1179656 | tf_op jit(solution)/shard_map/ppermute | solution.py:49
  115.3 21.3 %collective-permute-start.28 = (bf16[384,512]{1,0:T(8,128)(2,1)S(1)}, bf16[384,512]{1,0:T(8,128)(2,1)S(1)}, u32[]{:S(2)}, u32[]{:S(2)}) collective-permute-start(bf16[384,512]{1,0:T(8,128)(2,1)S(1)} %get-tuple-element.270.refs_1_), channel_id=1, source_target_pairs={{0,1},{1,0},{2,3},{3,2},{4,5},{5,4},{6,7},{7,6},{8,9},{9,8},{10,11... | collective-permute-start | bytes 1179656 | tf_op jit(solution)/shard_map/ppermute | solution.py:785
  116.9 16.2 %collective-permute-start.27 = (bf16[384,512]{1,0:T(8,128)(2,1)S(1)}, bf16[384,512]{1,0:T(8,128)(2,1)S(1)}, u32[]{:S(2)}, u32[]{:S(2)}) collective-permute-start(bf16[384,512]{1,0:T(8,128)(2,1)S(1)} %get-tuple-element.270.refs_1_), channel_id=1, source_target_pairs={{0,2},{1,3},{2,0},{3,1},{4,6},{5,7},{6,4},{7,5},{8,10},{9,11},{10,... | collective-permute-start | bytes 1179656 | tf_op jit(solution)/shard_map/ppermute | solution.py:785
  120.9 14.2 %copy-start.18 = (bf16[128,1920]{1,0:T(8,128)(2,1)S(1)}, bf16[128,1920]{1,0:T(8,128)(2,1)}, u32[]{:S(2)}) copy-start(bf16[128,1920]{1,0:T(8,128)(2,1)} %copy-done.16) | copy-start | bytes 1474564
  120.9 14.2 %copy-start.33 = (bf16[128,768]{1,0:T(8,128)(2,1)S(1)}, bf16[128,768]{1,0:T(8,128)(2,1)}, u32[]{:S(2)}) copy-start(bf16[128,768]{1,0:T(8,128)(2,1)} %get-tuple-element.170.refs_7_.refs_1_) | copy-start | bytes 589828
  120.9 14.2 %copy-start.37 = (bf16[128,768]{1,0:T(8,128)(2,1)S(1)}, bf16[128,768]{1,0:T(8,128)(2,1)}, u32[]{:S(2)}) copy-start(bf16[128,768]{1,0:T(8,128)(2,1)} %copy-done.36) | copy-start | bytes 589828
  120.9 14.2 %copy-start.41 = (bf16[128,384]{1,0:T(8,128)(2,1)S(1)}, bf16[128,384]{1,0:T(8,128)(2,1)}, u32[]{:S(2)}) copy-start(bf16[128,384]{1,0:T(8,128)(2,1)} %get-tuple-element.171.refs_8_.refs_4_) | copy-start | bytes 294916
  121.0 14.2 %copy-start.43 = (bf16[128,384]{1,0:T(8,128)(2,1)S(1)}, bf16[128,384]{1,0:T(8,128)(2,1)}, u32[]{:S(2)}) copy-start(bf16[128,384]{1,0:T(8,128)(2,1)} %copy-done.42) | copy-start | bytes 294916
  121.1 22.5 %collective-permute-start.26 = (bf16[416,512]{1,0:T(8,128)(2,1)S(1)}, bf16[416,512]{1,0:T(8,128)(2,1)S(1)}, u32[]{:S(2)}, u32[]{:S(2)}) collective-permute-start(bf16[416,512]{1,0:T(8,128)(2,1)S(1)} %get-tuple-element.269.refs_2_), channel_id=1, source_target_pairs={{0,8},{8,0},{1,9},{9,1},{2,10},{10,2},{3,11},{11,3},{4,12},{12,4},... | collective-permute-start | bytes 1277960 | tf_op jit(solution)/shard_map/ppermute | solution.py:49
  122.5 27.2 %collective-permute-start.31 = (bf16[384,768]{1,0:T(8,128)(2,1)S(1)}, bf16[384,768]{1,0:T(8,128)(2,1)S(1)}, u32[]{:S(2)}, u32[]{:S(2)}) collective-permute-start(bf16[384,768]{1,0:T(8,128)(2,1)S(1)} %get-tuple-element.282.refs_0_), channel_id=1, source_target_pairs={{0,4},{1,5},{2,6},{3,7},{4,0},{5,1},{6,2},{7,3},{8,12},{9,13},{10,... | collective-permute-start | bytes 1769480 | tf_op jit(solution)/shard_map/ppermute | solution.py:785
  133.1 9.8 %collective-permute-start.29 = (bf16[384,512]{1,0:T(8,128)(2,1)S(1)}, bf16[384,512]{1,0:T(8,128)(2,1)S(1)}, u32[]{:S(2)}, u32[]{:S(2)}) collective-permute-start(bf16[384,512]{1,0:T(8,128)(2,1)S(1)} %collective-permute-done.27.refs_14_.refs_2_), channel_id=1, source_target_pairs={{0,1},{1,0},{2,3},{3,2},{4,5},{5,4},{6,7},{7,6},{8,9},{9,8},{10,11... | collective-permute-start | bytes 1179656 | tf_op jit(solution)/shard_map/ppermute | solution.py:785
  136.4 25.7 %collective-permute-start.30 = (bf16[880,256]{1,0:T(8,128)(2,1)S(1)}, bf16[880,256]{1,0:T(8,128)(2,1)S(1)}, u32[]{:S(2)}, u32[]{:S(2)}) collective-permute-start(bf16[880,256]{1,0:T(8,128)(2,1)S(1)} %get-tuple-element.281), channel_id=1, source_target_pairs={{0,2},{1,3},{2,0},{3,1},{4,6},{5,7},{6,4},{7,5},{8,10},{9,11},{10,... | collective-permute-start | bytes 1351688 | tf_op jit(solution)/shard_map/ppermute | solution.py:785
  143.6 29.5 %collective-permute-start.33 = (bf16[2,2,384,512]{3,2,1,0:T(8,128)(2,1)S(1)}, bf16[2,2,384,512]{3,2,1,0:T(8,128)(2,1)S(1)}, u32[]{:S(2)}, u32[]{:S(2)}) collective-permute-start(bf16[2,2,384,512]{3,2,1,0:T(8,128)(2,1)S(1)} %get-tuple-element.286.refs_1_), channel_id=1, source_target_pairs={{0,16},{16,0},{1,17},{17,1},{2,18},{18,2},{3,19},{19,3},{4,20},{20... | collective-permute-start | bytes 4718600 | tf_op jit(solution)/shard_map/ppermute | solution.py:49
  149.9 29.7 %collective-permute-start.38 = (bf16[384,768]{1,0:T(8,128)(2,1)S(1)}, bf16[384,768]{1,0:T(8,128)(2,1)S(1)}, u32[]{:S(2)}, u32[]{:S(2)}) collective-permute-start(bf16[384,768]{1,0:T(8,128)(2,1)S(1)} %get-tuple-element.289.refs_1_), channel_id=1, source_target_pairs={{0,1},{1,0},{2,3},{3,2},{4,5},{5,4},{6,7},{7,6},{8,9},{9,8},{10,11... | collective-permute-start | bytes 1769480 | tf_op jit(solution)/shard_map/ppermute | solution.py:785
  150.4 22.1 %collective-permute-start.34 = (bf16[384,768]{1,0:T(8,128)(2,1)S(1)}, bf16[384,768]{1,0:T(8,128)(2,1)S(1)}, u32[]{:S(2)}, u32[]{:S(2)}) collective-permute-start(bf16[384,768]{1,0:T(8,128)(2,1)S(1)} %get-tuple-element.289.refs_1_), channel_id=1, source_target_pairs={{0,2},{1,3},{2,0},{3,1},{4,6},{5,7},{6,4},{7,5},{8,10},{9,11},{10,... | collective-permute-start | bytes 1769480 | tf_op jit(solution)/shard_map/ppermute | solution.py:785
  162.3 16.3 %collective-permute-start.32 = (bf16[880,256]{1,0:T(8,128)(2,1)S(1)}, bf16[880,256]{1,0:T(8,128)(2,1)S(1)}, u32[]{:S(2)}, u32[]{:S(2)}) collective-permute-start(bf16[880,256]{1,0:T(8,128)(2,1)S(1)} %get-tuple-element.285.refs_0_), channel_id=1, source_target_pairs={{0,4},{1,5},{2,6},{3,7},{4,0},{5,1},{6,2},{7,3},{8,12},{9,13},{10,... | collective-permute-start | bytes 1351688 | tf_op jit(solution)/shard_map/ppermute | solution.py:785
  172.5 16.3 %collective-permute-start.39 = (bf16[384,768]{1,0:T(8,128)(2,1)S(1)}, bf16[384,768]{1,0:T(8,128)(2,1)S(1)}, u32[]{:S(2)}, u32[]{:S(2)}) collective-permute-start(bf16[384,768]{1,0:T(8,128)(2,1)S(1)} %collective-permute-done.34.refs_1_.refs_2_), channel_id=1, source_target_pairs={{0,1},{1,0},{2,3},{3,2},{4,5},{5,4},{6,7},{7,6},{8,9},{9,8},{10,11... | collective-permute-start | bytes 1769480 | tf_op jit(solution)/shard_map/ppermute | solution.py:785
  178.7 20.3 %collective-permute-start.36 = (bf16[880,256]{1,0:T(8,128)(2,1)S(1)}, bf16[880,256]{1,0:T(8,128)(2,1)S(1)}, u32[]{:S(2)}, u32[]{:S(2)}) collective-permute-start(bf16[880,256]{1,0:T(8,128)(2,1)S(1)} %get-tuple-element.291.refs_1_), channel_id=1, source_target_pairs={{0,1},{1,0},{2,3},{3,2},{4,5},{5,4},{6,7},{7,6},{8,9},{9,8},{10,11... | collective-permute-start | bytes 1351688 | tf_op jit(solution)/shard_map/ppermute | solution.py:785
  179.6 10.0 %collective-permute-start.35 = (bf16[880,256]{1,0:T(8,128)(2,1)S(1)}, bf16[880,256]{1,0:T(8,128)(2,1)S(1)}, u32[]{:S(2)}, u32[]{:S(2)}) collective-permute-start(bf16[880,256]{1,0:T(8,128)(2,1)S(1)} %get-tuple-element.291.refs_1_), channel_id=1, source_target_pairs={{0,2},{1,3},{2,0},{3,1},{4,6},{5,7},{6,4},{7,5},{8,10},{9,11},{10,... | collective-permute-start | bytes 1351688 | tf_op jit(solution)/shard_map/ppermute | solution.py:785
  189.5 4.6 %collective-permute-start.40 = (bf16[2,2,384,768]{3,2,1,0:T(8,128)(2,1)S(1)}, bf16[2,2,384,768]{3,2,1,0:T(8,128)(2,1)S(1)}, u32[]{:S(2)}, u32[]{:S(2)}) collective-permute-start(bf16[2,2,384,768]{3,2,1,0:T(8,128)(2,1)S(1)} %get-tuple-element.293.refs_1_), channel_id=1, source_target_pairs={{0,16},{16,0},{1,17},{17,1},{2,18},{18,2},{3,19},{19,3},{4,20},{20... | collective-permute-start | bytes 7077896 | tf_op jit(solution)/shard_map/ppermute | solution.py:49
  189.6 14.8 %collective-permute-start.37 = (bf16[880,256]{1,0:T(8,128)(2,1)S(1)}, bf16[880,256]{1,0:T(8,128)(2,1)S(1)}, u32[]{:S(2)}, u32[]{:S(2)}) collective-permute-start(bf16[880,256]{1,0:T(8,128)(2,1)S(1)} %collective-permute-done.35.refs_1_.refs_2_), channel_id=1, source_target_pairs={{0,1},{1,0},{2,3},{3,2},{4,5},{5,4},{6,7},{7,6},{8,9},{9,8},{10,11... | collective-permute-start | bytes 1351688 | tf_op jit(solution)/shard_map/ppermute | solution.py:785
  205.1 3.8 %collective-permute-start.41 = (bf16[2,2,880,256]{3,2,1,0:T(8,128)(2,1)S(1)}, bf16[2,2,880,256]{3,2,1,0:T(8,128)(2,1)S(1)}, u32[]{:S(2)}, u32[]{:S(2)}) collective-permute-start(bf16[2,2,880,256]{3,2,1,0:T(8,128)(2,1)S(1)} %get-tuple-element.297.refs_1_), channel_id=1, source_target_pairs={{0,16},{16,0},{1,17},{17,1},{2,18},{18,2},{3,19},{19,3},{4,20},{20... | collective-permute-start | bytes 5406728 | tf_op jit(solution)/shard_map/ppermute | solution.py:49
  (28 other events, 125.5 us)

commit v4 on v3

--- a/solution.py
+++ b/solution.py
@@ -598,9 +598,10 @@
 
 def take_rows(rows_ref, row, up_sum_ref, bias_sum_ref):
     cols = rows_ref.shape[1]
-    for piece in range(up_sum_ref.shape[1] // cols):
-        up_sum_ref[:, piece * cols : (piece + 1) * cols] = rows_ref[row : row + 1]
-        row += 1
+    for line in range(up_sum_ref.shape[0]):
+        here, lane = row + line * LANES // cols, line * LANES % cols
+        up_sum_ref[line : line + 1] = rows_ref[here : here + 1, lane : lane + LANES]
+    row += up_sum_ref.shape[0] * LANES // cols
     width = bias_sum_ref.shape[1]
     for piece in range(2):
         here, lane = row + piece * width // cols, piece * width % cols
@@ -1200,8 +1201,8 @@
         [
             shaped(x.shape, FULL)
             for x in (
-                enc_qkv, enc_out_w, enc_vec, enc_fc1_bias, enc_qv_bias,
-                bridge_w, dec_pos, dec_vec, dec_fc1_bias, dec_qv_bias,
+                enc_qkv, enc_out_w, enc_vec, shaped((enc_mlp // LANES, LANES)), enc_qv_bias,
+                bridge_w, dec_pos, dec_vec, shaped((dec_mlp // LANES, LANES)), dec_qv_bias,
             )
         ],
         place, *e3_packed, scalars=1,

time: 213 us -> 213 us (level)
  transfers between devices with their start and end apart: 42 -> 42, of which waited for: 22 -> 22; matrix products, arithmetic and copies ran while one was open for 0% -> 0% of each run, Pallas kernels for 24% -> 25%
where the time goes in v4:
time: 213 us; the launch traced here: 212 us
  waiting for transfers between devices  107 us (50%)
  Pallas kernels  63.1 us (30%)
  starting transfers between devices  38.5 us (18%)
    ppermute x20, waiting for transfers between devices, flip(): lax.ppermute(value, 'dp', [(i, i ^ step) for i in range(lax.axis_size('dp...  80.4 us
    pallas_call x35, Pallas kernels, kernel_call(): pl.pallas_call(run, out_shape=[jax.ShapeDtypeStruct(x.shape, x.dtype) for...  63.1 us
    ppermute x22, waiting for transfers between devices, swap(): lax.ppermute(value, axis, [(i, i ^ 1) for i in range(lax.axis_size(axis))])  26.5 us
    ppermute x20, starting transfers between devices, flip(): lax.ppermute(value, 'dp', [(i, i ^ step) for i in range(lax.axis_size('dp...  25 us
    ppermute x22, starting transfers between devices, swap(): lax.ppermute(value, axis, [(i, i ^ 1) for i in range(lax.axis_size(axis))])  13.5 us
  transfers between devices with their start and end apart: 42, of which 22 were waited for; matrix products, arithmetic and copies ran while one was open for 0% of the time, Pallas kernels for 25%

profile of v4, /device:TPU:0, one launch (start us, length us, event | category | flops | bytes accessed | tf_op | source)
XLA Modules:
  0.0 212.4 jit_solution(9927780357965248280)
XLA Ops:
  1.3 4.6 %enc_attend.2 = (bf16[98,768]{1,0:T(8,128)(2,1)}, bf16[128,768]{1,0:T(8,128)(2,1)}, bf16[128,768]{1,0:T(8,128)(2,1)}, bf16[3,128,384]{2,1,0:T(8,128)(2,1)}, bf16...) custom-call(s32[3]{0:T(128)} %pad_add_fusion.refs_0_.refs_1_, bf16[98,2,768]{2,1,0:T(2,128)(2,1)} %bitcast.25, ...), custom_call_target="tpu_custom_call" | custom-call | flops 35999997952 | bytes 1 | tf_op jit(solution)/shard_map/enc_attend/pallas_call | solution.py:173
  6.1 3.0 %collective-permute-start.1 = (bf16[98,768]{1,0:T(8,128)(2,1)S(1)}, bf16[98,768]{1,0:T(8,128)(2,1)S(1)}, u32[]{:S(2)}, u32[]{:S(2)}) collective-permute-start(bf16[98,768]{1,0:T(8,128)(2,1)S(1)} %dynamic-slice_bitcast_fusion.1), channel_id=1, source_target_pairs={{0,1},{1,0},{2,3},{3,2},{4,5},{5,4},{6,7},{7,6},{8,9},{9,8},{10,11... | collective-permute-start | bytes 451592 | tf_op jit(solution)/shard_map/ppermute | solution.py:786
  9.1 1.5 collective-permute-start
  10.6 2.6 %collective-permute-done.1.refs_1_ = bf16[98,768]{1,0:T(8,128)(2,1)S(1)} collective-permute-done((bf16[98,768]{1,0:T(8,128)(2,1)S(1)}, bf16[98,768]{1,0:T(8,128)(2,1)S(1)}, u32[]{:S(2)}, u32[]{:S(2)}) %collective-permute-start.1) | collective-permute-done | bytes 150560 | tf_op jit(solution)/shard_map/ppermute | solution.py:786
  14.0 2.2 %enc_attend.3 = (bf16[98,768]{1,0:T(8,128)(2,1)S(1)}, bf16[128,768]{1,0:T(8,128)(2,1)S(1)}, bf16[128,768]{1,0:T(8,128)(2,1)S(1)}, bf16[3,128,384]{2,1,0:T(8,128)...) custom-call(s32[3]{0:T(128)S(1)} %copy-done.4, ...), custom_call_target="tpu_custom_call" | custom-call | flops 35999997952 | bytes 1 | tf_op jit(solution)/shard_map/enc_attend/pallas_call | solution.py:173
  16.5 2.3 %enc_hidden.1 = (bf16[98,768]{1,0:T(8,128)(2,1)S(1)}, f32[128,768]{1,0:T(8,128)S(1)}, bf16[128,768]{1,0:T(8,128)(2,1)S(1)}, bf16[128,1536]{1,0:T(8,128)(2,1)S(1)...) custom-call(s32[3]{0:T(128)S(1)} %copy-done.4, ...), custom_call_target="tpu_custom_call" | custom-call | flops 35999997952 | bytes 1 | tf_op jit(solution)/shard_map/enc_hidden/pallas_call | solution.py:173
  18.8 1.8 collective-permute-start.2
  21.6 4.1 %collective-permute-done.2.refs_4_ = bf16[98,768]{1,0:T(8,128)(2,1)S(1)} collective-permute-done((bf16[98,768]{1,0:T(8,128)(2,1)S(1)}, bf16[98,768]{1,0:T(8,128)(2,1)S(1)}, u32[]{:S(2)}, u32[]{:S(2)}) %collective-permute-start.2) | collective-permute-done | bytes 150560 | tf_op jit(solution)/shard_map/ppermute | solution.py:49
  25.8 4.4 %dec_attend.1 = (bf16[416,512]{1,0:T(8,128)(2,1)S(1)}, bf16[98,768]{1,0:T(8,128)(2,1)S(1)}, bf16[128,768]{1,0:T(8,128)(2,1)S(1)}, f32[416,512]{1,0:T(8,128)S(1)}...) custom-call(s32[1]{0:T(128)} %bitcast.3.refs_0_, ...), custom_call_target="tpu_custom_call" | custom-call | flops 35999997952 | bytes 1 | tf_op jit(solution)/shard_map/dec_attend/pallas_call | solution.py:173
  30.2 1.6 collective-permute-start.4
  31.8 1.6 enc_side_hidden.1
  33.7 8.8 %collective-permute-done.4.refs_4_ = bf16[416,512]{1,0:T(8,128)(2,1)S(1)} collective-permute-done((bf16[416,512]{1,0:T(8,128)(2,1)S(1)}, bf16[416,512]{1,0:T(8,128)(2,1)S(1)}, u32[]{:S(2)}, u32[]{:S(2)}) %collective-permute-start.4) | collective-permute-done | bytes 426016 | tf_op jit(solution)/shard_map/ppermute | solution.py:49
  42.5 4.5 %dec_hidden.1 = (bf16[416,512]{1,0:T(8,128)(2,1)S(1)}, bf16[416,512]{1,0:T(8,128)(2,1)S(1)}, f32[416,512]{1,0:T(8,128)S(1)}, bf16[416,512]{1,0:T(8,128)(2,1)S(1)...) custom-call(s32[1]{0:T(128)} %bitcast.3.refs_0_, ...), custom_call_target="tpu_custom_call" | custom-call | flops 35999997952 | bytes 1 | tf_op jit(solution)/shard_map/dec_hidden/pallas_call | solution.py:173
  47.0 1.6 collective-permute-start.7
  48.6 1.5 enc_out_both.1
  50.1 2.4 %collective-permute-done.8.refs_5_ = bf16[416,2304]{1,0:T(8,128)(2,1)S(1)} collective-permute-done((bf16[416,2304]{1,0:T(8,128)(2,1)S(1)}, bf16[416,2304]{1,0:T(8,128)(2,1)S(1)}, u32[]{:S(2)}, u32[]{:S(2)}) %collective-permute-start.8) | collective-permute-done | bytes 1916960 | tf_op jit(solution)/shard_map/ppermute | solution.py:49
  52.5 1.8 dec_hidden_weights.1
  54.4 1.6 collective-permute-start.12
  56.0 2.5 %collective-permute-done.7.refs_4_ = bf16[416,512]{1,0:T(8,128)(2,1)S(1)} collective-permute-done((bf16[416,512]{1,0:T(8,128)(2,1)S(1)}, bf16[416,512]{1,0:T(8,128)(2,1)S(1)}, u32[]{:S(2)}, u32[]{:S(2)}) %collective-permute-start.7) | collective-permute-done | bytes 426016 | tf_op jit(solution)/shard_map/ppermute | solution.py:49
  58.5 4.7 %dec_attend_back.1 = (bf16[416,512]{1,0:T(8,128)(2,1)S(1)}, f32[416,512]{1,0:T(8,128)S(1)}, bf16[416,512]{1,0:T(8,128)(2,1)S(1)}, bf16[3,416,256]{2,1,0:T(8,128)...) custom-call(s32[3]{0:T(128)S(1)} %copy-done.4, ...), custom_call_target="tpu_custom_call" | custom-call | flops 35999997952 | bytes 1 | tf_op jit(solution)/shard_map/dec_attend_back/pallas_call | solution.py:173
  63.1 1.6 collective-permute-start.10
  64.7 3.7 %collective-permute-done.12.refs_2_ = bf16[2,256,512]{2,1,0:T(8,128)(2,1)S(1)} collective-permute-done((bf16[2,256,512]{2,1,0:T(8,128)(2,1)S(1)}, bf16[2,256,512]{2,1,0:T(8,128)(2,1)S(1)}, u32[]{:S(2)}, u32[]{:S(2)}) %collective-permute-start.12) | collective-permute-done | bytes 524320 | tf_op jit(solution)/shard_map/ppermute | solution.py:786
  69.1 1.3 dec_head_weights.1
  70.4 1.6 collective-permute-start.14
  72.0 1.6 collective-permute-done.10.refs_4_
  73.7 1.9 dec_start_back.1
  75.6 1.8 collective-permute-start.13
  78.6 0.9 dec_bridge_weights.1
  79.6 3.4 %collective-permute-done.13.refs_2_.refs_4_ = bf16[128,768]{1,0:T(8,128)(2,1)S(1)} collective-permute-done((bf16[128,768]{1,0:T(8,128)(2,1)S(1)}, bf16[128,768]{1,0:T(8,128)(2,1)S(1)}, u32[]{:S(2)}, u32[]{:S(2)}) %collective-permute-start.13) | collective-permute-done | bytes 196640 | tf_op jit(solution)/shard_map/ppermute | solution.py:786
  83.0 1.8 collective-permute-start.21
  85.0 2.3 %enc_hidden_back.1 = (bf16[196,768]{1,0:T(8,128)(2,1)S(1)}, bf16[256,1536]{1,0:T(8,128)(2,1)S(1)}, bf16[256,384]{1,0:T(8,128)(2,1)S(1)}, f32[8,128]{1,0:T(8,128)S(1)}) custom-call(s32[3]{0:T(128)S(1)} %copy-done.4, bf16[128,768]{1,0:T(8,128)(2,1)S(1)} %get-tuple-element.217.refs_1_.refs_3_, bf16[128,768]{1,0:T(8,128)(2,1)S(1)} %collective-permute-done.13.refs_2_.refs_4_, ...), custom_call_target="tpu_custom_call" | custom-call | flops 35999997952 | bytes 1 | tf_op jit(solution)/shard_map/enc_hidden_back/pallas_call | solution.py:173
  87.6 1.3 collective-permute-start.20
  88.9 0.7 fold.3
  89.6 1.6 collective-permute-start.22
  91.2 1.8 enc_hidden_weights.1
  93.0 1.5 collective-permute-done.21.refs_1_
  94.7 2.8 %collective-permute-start.24 = (bf16[384,512]{1,0:T(8,128)(2,1)S(1)}, bf16[384,512]{1,0:T(8,128)(2,1)S(1)}, u32[]{:S(2)}, u32[]{:S(2)}) collective-permute-start(bf16[384,512]{1,0:T(8,128)(2,1)S(1)} %get-tuple-element.263.refs_0_), channel_id=1, source_target_pairs={{0,4},{1,5},{2,6},{3,7},{4,0},{5,1},{6,2},{7,3},{8,12},{9,13},{10,... | collective-permute-start | bytes 1179656 | tf_op jit(solution)/shard_map/ppermute | solution.py:786
  97.5 1.6 collective-permute-start.19
  99.1 4.6 %enc_attend_back.1 = (bf16[196,768]{1,0:T(8,128)(2,1)S(1)}, f32[256,768]{1,0:T(8,128)S(1)}, bf16[256,768]{1,0:T(8,128)(2,1)S(1)}, bf16[3,256,384]{2,1,0:T(8,128)...) custom-call(s32[3]{0:T(128)S(1)} %copy-done.4, ...), custom_call_target="tpu_custom_call" | custom-call | flops 35999997952 | bytes 1 | tf_op jit(solution)/shard_map/enc_attend_back/pallas_call | solution.py:173
  103.7 1.3 collective-permute-start.23
  105.0 10.0 %collective-permute-done.24.refs_1_ = bf16[384,512]{1,0:T(8,128)(2,1)S(1)} collective-permute-done((bf16[384,512]{1,0:T(8,128)(2,1)S(1)}, bf16[384,512]{1,0:T(8,128)(2,1)S(1)}, u32[]{:S(2)}, u32[]{:S(2)}) %collective-permute-start.24) | collective-permute-done | bytes 393248 | tf_op jit(solution)/shard_map/ppermute | solution.py:786
  115.1 1.7 collective-permute-start.28
  117.4 1.8 enc_start_back.1
  119.2 1.5 collective-permute-done.19.refs_1_
  120.9 1.4 collective-permute-start.26
  122.3 1.9 collective-permute-start.31
  124.2 8.7 %collective-permute-done.27.refs_14_.refs_2_ = bf16[384,512]{1,0:T(8,128)(2,1)S(1)} collective-permute-done((bf16[384,512]{1,0:T(8,128)(2,1)S(1)}, bf16[384,512]{1,0:T(8,128)(2,1)S(1)}, u32[]{:S(2)}, u32[]{:S(2)}) %collective-permute-start.27) | collective-permute-done | bytes 393248 | tf_op jit(solution)/shard_map/ppermute | solution.py:786
  132.9 2.1 collective-permute-start.29
  135.0 1.3 last_weights.1
  136.4 6.4 %collective-permute-done.29.refs_4_ = bf16[384,512]{1,0:T(8,128)(2,1)S(1)} collective-permute-done((bf16[384,512]{1,0:T(8,128)(2,1)S(1)}, bf16[384,512]{1,0:T(8,128)(2,1)S(1)}, u32[]{:S(2)}, u32[]{:S(2)}) %collective-permute-start.29) | collective-permute-done | bytes 393248 | tf_op jit(solution)/shard_map/ppermute | solution.py:786
  143.6 1.9 dec_out.1
  145.4 4.2 %collective-permute-done.31.refs_1_ = bf16[384,768]{1,0:T(8,128)(2,1)S(1)} collective-permute-done((bf16[384,768]{1,0:T(8,128)(2,1)S(1)}, bf16[384,768]{1,0:T(8,128)(2,1)S(1)}, u32[]{:S(2)}, u32[]{:S(2)}) %collective-permute-start.31) | collective-permute-done | bytes 589856 | tf_op jit(solution)/shard_map/ppermute | solution.py:786
  150.4 11.6 %collective-permute-done.30.refs_1_ = bf16[880,256]{1,0:T(8,128)(2,1)S(1)} collective-permute-done((bf16[880,256]{1,0:T(8,128)(2,1)S(1)}, bf16[880,256]{1,0:T(8,128)(2,1)S(1)}, u32[]{:S(2)}, u32[]{:S(2)}) %collective-permute-start.30) | collective-permute-done | bytes 450592 | tf_op jit(solution)/shard_map/ppermute | solution.py:786
  162.2 10.2 %collective-permute-done.34.refs_1_.refs_2_ = bf16[384,768]{1,0:T(8,128)(2,1)S(1)} collective-permute-done((bf16[384,768]{1,0:T(8,128)(2,1)S(1)}, bf16[384,768]{1,0:T(8,128)(2,1)S(1)}, u32[]{:S(2)}, u32[]{:S(2)}) %collective-permute-start.34) | collective-permute-done | bytes 589856 | tf_op jit(solution)/shard_map/ppermute | solution.py:786
  173.0 3.5 %dec_whole.1 = (f32[512,1024]{1,0:T(8,128)}, f32[1024,512]{1,0:T(8,128)}, f32[3,512,256]{2,1,0:T(8,128)}, f32[256,512]{1,0:T(8,128)}, f32[8,128]{1,0:T(8,128)S(1)}) custom-call(s32[3]{0:T(128)S(1)} %copy-done.4, bf16[2,2,384,512]{3,2,1,0:T(8,128)(2,1)S(1)} %get-tuple-element.286.refs_1_, bf16[2,2,384,512]{3,2,1,0:T(8,128)(2,1)S(1)} %collective-permute-done.33.refs_2_, ...), custom_call_target="tpu_custom_call" | custom-call | flops 35999997952 | bytes 1 | tf_op jit(solution)/shard_map/dec_whole/pallas_call | solution.py:173
  177.1 1.4 collective-permute-done.32.refs_1_
  178.5 0.9 collective-permute-start.36
  179.5 9.2 %collective-permute-done.39.refs_4_ = bf16[384,768]{1,0:T(8,128)(2,1)S(1)} collective-permute-done((bf16[384,768]{1,0:T(8,128)(2,1)S(1)}, bf16[384,768]{1,0:T(8,128)(2,1)S(1)}, u32[]{:S(2)}, u32[]{:S(2)}) %collective-permute-start.39) | collective-permute-done | bytes 589856 | tf_op jit(solution)/shard_map/ppermute | solution.py:786
  188.7 0.7 pack.4
  190.7 3.3 %collective-permute-done.40.refs_2_ = bf16[2,2,384,768]{3,2,1,0:T(8,128)(2,1)S(1)} collective-permute-done((bf16[2,2,384,768]{3,2,1,0:T(8,128)(2,1)S(1)}, bf16[2,2,384,768]{3,2,1,0:T(8,128)(2,1)S(1)}, u32[]{:S(2)}, u32[]{:S(2)}) %collective-permute-start.40) | collective-permute-done | bytes 2359328 | tf_op jit(solution)/shard_map/ppermute | solution.py:49
  194.0 4.9 %enc_hidden_whole.1 = (f32[768,1536]{1,0:T(8,128)}, f32[1536,768]{1,0:T(8,128)}, f32[8,128]{1,0:T(8,128)S(1)}) custom-call(s32[3]{0:T(128)S(1)} %copy-done.4, bf16[2,2,384,768]{3,2,1,0:T(8,128)(2,1)S(1)} %get-tuple-element.293.refs_1_, bf16[2,2,384,768]{3,2,1,0:T(8,128)(2,1)S(1)} %collective-permute-done.40.refs_2_, f32[8,128]{1,0:T(8,128)S(1)} %get-tuple-element.295.refs_3_), custom_call_target="tpu_custom_call" | custom-call | flops 35999997952 | bytes 1 | tf_op jit(solution)/shard_map/enc_hidden_whole/pallas_call | solution.py:173
  198.9 5.4 %collective-permute-done.37.refs_4_ = bf16[880,256]{1,0:T(8,128)(2,1)S(1)} collective-permute-done((bf16[880,256]{1,0:T(8,128)(2,1)S(1)}, bf16[880,256]{1,0:T(8,128)(2,1)S(1)}, u32[]{:S(2)}, u32[]{:S(2)}) %collective-permute-start.37) | collective-permute-done | bytes 450592 | tf_op jit(solution)/shard_map/ppermute | solution.py:786
  205.0 3.7 %collective-permute-done.41.refs_2_ = bf16[2,2,880,256]{3,2,1,0:T(8,128)(2,1)S(1)} collective-permute-done((bf16[2,2,880,256]{3,2,1,0:T(8,128)(2,1)S(1)}, bf16[2,2,880,256]{3,2,1,0:T(8,128)(2,1)S(1)}, u32[]{:S(2)}, u32[]{:S(2)}) %collective-permute-start.41) | collective-permute-done | bytes 1802272 | tf_op jit(solution)/shard_map/ppermute | solution.py:49
  208.8 3.5 %last_whole.1 = (f32[3,768,384]{2,1,0:T(8,128)}, f32[384,768]{1,0:T(8,128)}, f32[6,768]{1,0:T(8,128)}, f32[12,128]{1,0:T(8,128)}, f32[2,384]{1,0:T(2,128)}, /*in...) custom-call(s32[3]{0:T(128)S(1)} %copy-done.4, ...), custom_call_target="tpu_custom_call" | custom-call | flops 35999997952 | bytes 1 | tf_op jit(solution)/shard_map/last_whole/pallas_call | solution.py:173
  (164 shorter events, 11.5 us)
Async XLA Ops:
  0.7 20.5 %copy-start = (bf16[2,392,512]{2,1,0:T(8,128)(2,1)S(1)}, bf16[2,392,512]{2,1,0:T(8,128)(2,1)}, u32[]{:S(2)}) copy-start(bf16[2,392,512]{2,1,0:T(8,128)(2,1)} %param.39) | copy-start | bytes 2408452
  1.3 11.9 %copy-start.4 = (s32[3]{0:T(128)S(1)}, s32[3]{0:T(128)}, u32[]{:S(2)}) copy-start(s32[3]{0:T(128)} %pad_add_fusion.refs_0_.refs_1_) | copy-start | bytes 40
  1.3 11.9 %copy-start.9 = (bf16[768,3,384]{2,0,1:T(8,128)(2,1)S(1)}, bf16[768,3,384]{2,0,1:T(8,128)(2,1)}, u32[]{:S(2)}) copy-start(bf16[768,3,384]{2,0,1:T(8,128)(2,1)} %param.24) | copy-start | bytes 5308420
  1.3 11.9 %copy-start.15 = (bf16[384,768]{1,0:T(8,128)(2,1)S(1)}, bf16[384,768]{1,0:T(8,128)(2,1)}, u32[]{:S(2)}) copy-start(bf16[384,768]{1,0:T(8,128)(2,1)} %refs_13_.1) | copy-start | bytes 1769476
  1.3 11.9 %copy-start.22 = (bf16[6,768]{1,0:T(8,128)(2,1)S(1)}, bf16[6,768]{1,0:T(8,128)(2,1)}, u32[]{:S(2)}) copy-start(bf16[6,768]{1,0:T(8,128)(2,1)} %refs_4_.6) | copy-start | bytes 27652
  1.3 11.9 %copy-start.24 = (bf16[2,384]{1,0:T(2,128)(2,1)S(1)}, bf16[2,384]{1,0:T(2,128)(2,1)}, u32[]{:S(2)}) copy-start(bf16[2,384]{1,0:T(2,128)(2,1)} %refs_4_.5) | copy-start | bytes 4612
  6.1 7.1 %collective-permute-start.1 = (bf16[98,768]{1,0:T(8,128)(2,1)S(1)}, bf16[98,768]{1,0:T(8,128)(2,1)S(1)}, u32[]{:S(2)}, u32[]{:S(2)}) collective-permute-start(bf16[98,768]{1,0:T(8,128)(2,1)S(1)} %dynamic-slice_bitcast_fusion.1), channel_id=1, source_target_pairs={{0,1},{1,0},{2,3},{3,2},{4,5},{5,4},{6,7},{7,6},{8,9},{9,8},{10,11... | collective-permute-start | bytes 451592 | tf_op jit(solution)/shard_map/ppermute | solution.py:786
  9.1 7.1 %collective-permute-start = (bf16[98,768]{1,0:T(8,128)(2,1)}, bf16[98,768]{1,0:T(8,128)(2,1)S(1)}, u32[]{:S(2)}, u32[]{:S(2)}) collective-permute-start(bf16[98,768]{1,0:T(8,128)(2,1)} %get-tuple-element.169.refs_3_), channel_id=1, source_target_pairs={{0,8},{8,0},{1,9},{9,1},{2,10},{10,2},{3,11},{11,3},{4,12},{12,4},... | collective-permute-start | bytes 451592 | tf_op jit(solution)/shard_map/ppermute | solution.py:49
  16.2 15.6 %copy-start.36 = (bf16[128,768]{1,0:T(8,128)(2,1)}, bf16[128,768]{1,0:T(8,128)(2,1)S(1)}, u32[]{:S(2)}) copy-start(bf16[128,768]{1,0:T(8,128)(2,1)S(1)} %get-tuple-element.183.refs_7_.refs_2_) | copy-start | bytes 589828
  16.2 15.6 %copy-start.38 = (bf16[128,768]{1,0:T(8,128)(2,1)}, bf16[128,768]{1,0:T(8,128)(2,1)S(1)}, u32[]{:S(2)}) copy-start(bf16[128,768]{1,0:T(8,128)(2,1)S(1)} %get-tuple-element.181.refs_1_) | copy-start | bytes 589828
  16.2 15.6 %copy-start.42 = (bf16[128,384]{1,0:T(8,128)(2,1)}, bf16[128,384]{1,0:T(8,128)(2,1)S(1)}, u32[]{:S(2)}) copy-start(bf16[128,384]{1,0:T(8,128)(2,1)S(1)} %get-tuple-element.184.refs_8_.refs_5_) | copy-start | bytes 294916
  16.4 9.3 %copy-start.12 = (bf16[512,3,256]{2,0,1:T(8,128)(2,1)S(1)}, bf16[512,3,256]{2,0,1:T(8,128)(2,1)}, u32[]{:S(2)}) copy-start(bf16[512,3,256]{2,0,1:T(8,128)(2,1)} %param.33) | copy-start | bytes 2359300
  16.4 9.3 %copy-start.13 = (bf16[768,512]{1,0:T(8,128)(2,1)S(1)}, bf16[768,512]{1,0:T(8,128)(2,1)}, u32[]{:S(2)}) copy-start(bf16[768,512]{1,0:T(8,128)(2,1)} %refs_7_.4) | copy-start | bytes 2359300
  16.4 9.3 %copy-start.19 = (bf16[256,512]{1,0:T(8,128)(2,1)S(1)}, bf16[256,512]{1,0:T(8,128)(2,1)}, u32[]{:S(2)}) copy-start(bf16[256,512]{1,0:T(8,128)(2,1)} %refs_9_.3) | copy-start | bytes 786436
  16.4 9.3 %copy-start.20 = (bf16[196,512]{1,0:T(8,128)(2,1)S(1)}, bf16[196,512]{1,0:T(8,128)(2,1)}, u32[]{:S(2)}) copy-start(bf16[196,512]{1,0:T(8,128)(2,1)} %refs_8_.2) | copy-start | bytes 602116
  18.7 11.4 %copy-start.28 = (f32[128,768]{1,0:T(8,128)}, f32[128,768]{1,0:T(8,128)S(1)}, u32[]{:S(2)}) copy-start(f32[128,768]{1,0:T(8,128)S(1)} %get-tuple-element.175.refs_2_.refs_1_) | copy-start | bytes 1179652
  18.8 7.0 %collective-permute-start.2 = (bf16[98,768]{1,0:T(8,128)(2,1)S(1)}, bf16[98,768]{1,0:T(8,128)(2,1)S(1)}, u32[]{:S(2)}, u32[]{:S(2)}) collective-permute-start(bf16[98,768]{1,0:T(8,128)(2,1)S(1)} %get-tuple-element.176.refs_3_), channel_id=1, source_target_pairs={{0,8},{8,0},{1,9},{9,1},{2,10},{10,2},{3,11},{11,3},{4,12},{12,4},... | collective-permute-start | bytes 451592 | tf_op jit(solution)/shard_map/ppermute | solution.py:49
  21.2 10.6 %collective-permute-start.5 = (bf16[98,768]{1,0:T(8,128)(2,1)S(1)}, bf16[98,768]{1,0:T(8,128)(2,1)S(1)}, u32[]{:S(2)}, u32[]{:S(2)}) collective-permute-start(bf16[98,768]{1,0:T(8,128)(2,1)S(1)} %get-tuple-element.182.refs_3_), channel_id=1, source_target_pairs={{0,8},{8,0},{1,9},{9,1},{2,10},{10,2},{3,11},{11,3},{4,12},{12,4},... | collective-permute-start | bytes 451592 | tf_op jit(solution)/shard_map/ppermute | solution.py:49
  21.6 12.1 %collective-permute-start.6 = (bf16[128,1920]{1,0:T(8,128)(2,1)S(1)}, bf16[128,1920]{1,0:T(8,128)(2,1)S(1)}, u32[]{:S(2)}, u32[]{:S(2)}) collective-permute-start(bf16[128,1920]{1,0:T(8,128)(2,1)S(1)} %get-tuple-element.187), channel_id=1, source_target_pairs={{0,16},{16,0},{1,17},{17,1},{2,18},{18,2},{3,19},{19,3},{4,20},{20... | collective-permute-start | bytes 1474568 | tf_op jit(solution)/shard_map/ppermute | solution.py:49
  30.2 12.3 %copy-start.26 = (f32[416,512]{1,0:T(8,128)}, f32[416,512]{1,0:T(8,128)S(1)}, u32[]{:S(2)}) copy-start(f32[416,512]{1,0:T(8,128)S(1)} %get-tuple-element.179.refs_2_) | copy-start | bytes 2555908
  30.2 18.4 %collective-permute-start.3 = (bf16[98,768]{1,0:T(8,128)(2,1)S(1)}, bf16[98,768]{1,0:T(8,128)(2,1)S(1)}, u32[]{:S(2)}, u32[]{:S(2)}) collective-permute-start(bf16[98,768]{1,0:T(8,128)(2,1)S(1)} %get-tuple-element.178.refs_1_), channel_id=1, source_target_pairs={{0,16},{16,0},{1,17},{17,1},{2,18},{18,2},{3,19},{19,3},{4,20},{20... | collective-permute-start | bytes 451592 | tf_op jit(solution)/shard_map/ppermute | solution.py:49
  30.2 12.2 %collective-permute-start.4 = (bf16[416,512]{1,0:T(8,128)(2,1)S(1)}, bf16[416,512]{1,0:T(8,128)(2,1)S(1)}, u32[]{:S(2)}, u32[]{:S(2)}) collective-permute-start(bf16[416,512]{1,0:T(8,128)(2,1)S(1)} %get-tuple-element.180.refs_3_), channel_id=1, source_target_pairs={{0,8},{8,0},{1,9},{9,1},{2,10},{10,2},{3,11},{11,3},{4,12},{12,4},... | collective-permute-start | bytes 1277960 | tf_op jit(solution)/shard_map/ppermute | solution.py:49
  31.8 10.7 %copy-start.10 = (bf16[512,1024]{1,0:T(8,128)(2,1)S(1)}, bf16[512,1024]{1,0:T(8,128)(2,1)}, u32[]{:S(2)}) copy-start(bf16[512,1024]{1,0:T(8,128)(2,1)} %refs_6_.4) | copy-start | bytes 3145732
  31.8 10.7 %copy-start.11 = (bf16[1024,512]{1,0:T(8,128)(2,1)S(1)}, bf16[1024,512]{1,0:T(8,128)(2,1)}, u32[]{:S(2)}) copy-start(bf16[1024,512]{1,0:T(8,128)(2,1)} %refs_8_.3) | copy-start | bytes 3145732
  33.4 16.7 %collective-permute-start.9 = (bf16[128,1920]{1,0:T(8,128)(2,1)S(1)}, bf16[128,1920]{1,0:T(8,128)(2,1)S(1)}, u32[]{:S(2)}, u32[]{:S(2)}) collective-permute-start(bf16[128,1920]{1,0:T(8,128)(2,1)S(1)} %get-tuple-element.205), channel_id=1, source_target_pairs={{0,16},{16,0},{1,17},{17,1},{2,18},{18,2},{3,19},{19,3},{4,20},{20... | collective-permute-start | bytes 1474568 | tf_op jit(solution)/shard_map/ppermute | solution.py:49
  47.0 11.4 %collective-permute-start.7 = (bf16[416,512]{1,0:T(8,128)(2,1)S(1)}, bf16[416,512]{1,0:T(8,128)(2,1)S(1)}, u32[]{:S(2)}, u32[]{:S(2)}) collective-permute-start(bf16[416,512]{1,0:T(8,128)(2,1)S(1)} %get-tuple-element.195.refs_3_), channel_id=1, source_target_pairs={{0,8},{8,0},{1,9},{9,1},{2,10},{10,2},{3,11},{11,3},{4,12},{12,4},... | collective-permute-start | bytes 1277960 | tf_op jit(solution)/shard_map/ppermute | solution.py:49
  48.6 3.9 %collective-permute-start.8 = (bf16[416,2304]{1,0:T(8,128)(2,1)S(1)}, bf16[416,2304]{1,0:T(8,128)(2,1)S(1)}, u32[]{:S(2)}, u32[]{:S(2)}) collective-permute-start(bf16[416,2304]{1,0:T(8,128)(2,1)S(1)} %get-tuple-element.203), channel_id=1, source_target_pairs={{0,16},{16,0},{1,17},{17,1},{2,18},{18,2},{3,19},{19,3},{4,20},{20... | collective-permute-start | bytes 5750792 | tf_op jit(solution)/shard_map/ppermute | solution.py:49
  54.4 14.0 %collective-permute-start.12 = (bf16[2,256,512]{2,1,0:T(8,128)(2,1)S(1)}, bf16[2,256,512]{2,1,0:T(8,128)(2,1)S(1)}, u32[]{:S(2)}, u32[]{:S(2)}) collective-permute-start(bf16[2,256,512]{2,1,0:T(8,128)(2,1)S(1)} %get-tuple-element.213), channel_id=1, source_target_pairs={{0,1},{1,0},{2,3},{3,2},{4,5},{5,4},{6,7},{7,6},{8,9},{9,8},{10,11... | collective-permute-start | bytes 1572872 | tf_op jit(solution)/shard_map/ppermute | solution.py:786
  63.1 10.5 %collective-permute-start.10 = (bf16[416,512]{1,0:T(8,128)(2,1)S(1)}, bf16[416,512]{1,0:T(8,128)(2,1)S(1)}, u32[]{:S(2)}, u32[]{:S(2)}) collective-permute-start(bf16[416,512]{1,0:T(8,128)(2,1)S(1)} %get-tuple-element.207.refs_3_), channel_id=1, source_target_pairs={{0,8},{8,0},{1,9},{9,1},{2,10},{10,2},{3,11},{11,3},{4,12},{12,4},... | collective-permute-start | bytes 1277960 | tf_op jit(solution)/shard_map/ppermute | solution.py:49
  64.7 4.4 %collective-permute-start.11 = (bf16[416,1536]{1,0:T(8,128)(2,1)S(1)}, bf16[416,1536]{1,0:T(8,128)(2,1)S(1)}, u32[]{:S(2)}, u32[]{:S(2)}) collective-permute-start(bf16[416,1536]{1,0:T(8,128)(2,1)S(1)} %get-tuple-element.211), channel_id=1, source_target_pairs={{0,16},{16,0},{1,17},{17,1},{2,18},{18,2},{3,19},{19,3},{4,20},{20... | collective-permute-start | bytes 3833864 | tf_op jit(solution)/shard_map/ppermute | solution.py:49
  70.4 7.6 %collective-permute-start.14 = (bf16[2,128,512]{2,1,0:T(8,128)(2,1)S(1)}, bf16[2,128,512]{2,1,0:T(8,128)(2,1)S(1)}, u32[]{:S(2)}, u32[]{:S(2)}) collective-permute-start(bf16[2,128,512]{2,1,0:T(8,128)(2,1)S(1)} %get-tuple-element.227), channel_id=1, source_target_pairs={{0,1},{1,0},{2,3},{3,2},{4,5},{5,4},{6,7},{7,6},{8,9},{9,8},{10,11... | collective-permute-start | bytes 786440 | tf_op jit(solution)/shard_map/ppermute | solution.py:786
  75.5 9.5 %collective-permute-start.15 = (bf16[128,768]{1,0:T(8,128)(2,1)S(1)}, bf16[128,768]{1,0:T(8,128)(2,1)S(1)}, u32[]{:S(2)}, u32[]{:S(2)}) collective-permute-start(bf16[128,768]{1,0:T(8,128)(2,1)S(1)} %get-tuple-element.217.refs_1_.refs_3_), channel_id=1, source_target_pairs={{0,16},{16,0},{1,17},{17,1},{2,18},{18,2},{3,19},{19,3},{4,20},{20... | collective-permute-start | bytes 589832 | tf_op jit(solution)/shard_map/ppermute | solution.py:49
  75.6 7.3 %collective-permute-start.13 = (bf16[128,768]{1,0:T(8,128)(2,1)S(1)}, bf16[128,768]{1,0:T(8,128)(2,1)S(1)}, u32[]{:S(2)}, u32[]{:S(2)}) collective-permute-start(bf16[128,768]{1,0:T(8,128)(2,1)S(1)} %get-tuple-element.217.refs_1_.refs_3_), channel_id=1, source_target_pairs={{0,1},{1,0},{2,3},{3,2},{4,5},{5,4},{6,7},{7,6},{8,9},{9,8},{10,11... | collective-permute-start | bytes 589832 | tf_op jit(solution)/shard_map/ppermute | solution.py:786
  83.0 5.9 %collective-permute-start.16 = (bf16[128,768]{1,0:T(8,128)(2,1)S(1)}, bf16[128,768]{1,0:T(8,128)(2,1)S(1)}, u32[]{:S(2)}, u32[]{:S(2)}) collective-permute-start(bf16[128,768]{1,0:T(8,128)(2,1)S(1)} %collective-permute-done.13.refs_2_.refs_4_), channel_id=1, source_target_pairs={{0,16},{16,0},{1,17},{17,1},{2,18},{18,2},{3,19},{19,3},{4,20},{20... | collective-permute-start | bytes 589832 | tf_op jit(solution)/shard_map/ppermute | solution.py:49
  83.0 11.6 %collective-permute-start.21 = (bf16[384,512]{1,0:T(8,128)(2,1)S(1)}, bf16[384,512]{1,0:T(8,128)(2,1)S(1)}, u32[]{:S(2)}, u32[]{:S(2)}) collective-permute-start(bf16[384,512]{1,0:T(8,128)(2,1)S(1)} %get-tuple-element.254), channel_id=1, source_target_pairs={{0,2},{1,3},{2,0},{3,1},{4,6},{5,7},{6,4},{7,5},{8,10},{9,11},{10,... | collective-permute-start | bytes 1179656 | tf_op jit(solution)/shard_map/ppermute | solution.py:786
  84.8 4.1 %collective-permute-start.18 = (bf16[2,2,128,512]{3,2,1,0:T(8,128)(2,1)S(1)}, bf16[2,2,128,512]{3,2,1,0:T(8,128)(2,1)S(1)}, u32[]{:S(2)}, u32[]{:S(2)}) collective-permute-start(bf16[2,2,128,512]{3,2,1,0:T(8,128)(2,1)S(1)} %get-tuple-element.242), channel_id=1, source_target_pairs={{0,16},{16,0},{1,17},{17,1},{2,18},{18,2},{3,19},{19,3},{4,20},{20... | collective-permute-start | bytes 1572872 | tf_op jit(solution)/shard_map/ppermute | solution.py:49
  87.3 3.9 %collective-permute-start.17 = (bf16[256,384]{1,0:T(8,128)(2,1)S(1)}, bf16[256,384]{1,0:T(8,128)(2,1)S(1)}, u32[]{:S(2)}, u32[]{:S(2)}) collective-permute-start(bf16[256,384]{1,0:T(8,128)(2,1)S(1)} %get-tuple-element.240), channel_id=1, source_target_pairs={{0,16},{16,0},{1,17},{17,1},{2,18},{18,2},{3,19},{19,3},{4,20},{20... | collective-permute-start | bytes 589832 | tf_op jit(solution)/shard_map/ppermute | solution.py:49
  87.6 11.4 %collective-permute-start.20 = (bf16[196,768]{1,0:T(8,128)(2,1)S(1)}, bf16[196,768]{1,0:T(8,128)(2,1)S(1)}, u32[]{:S(2)}, u32[]{:S(2)}) collective-permute-start(bf16[196,768]{1,0:T(8,128)(2,1)S(1)} %get-tuple-element.248.refs_5_), channel_id=1, source_target_pairs={{0,8},{8,0},{1,9},{9,1},{2,10},{10,2},{3,11},{11,3},{4,12},{12,4},... | collective-permute-start | bytes 903176 | tf_op jit(solution)/shard_map/ppermute | solution.py:49
  89.6 9.5 %collective-permute-start.22 = (bf16[2,128,512]{2,1,0:T(8,128)(2,1)S(1)}, bf16[2,128,512]{2,1,0:T(8,128)(2,1)S(1)}, u32[]{:S(2)}, u32[]{:S(2)}) collective-permute-start(bf16[2,128,512]{2,1,0:T(8,128)(2,1)S(1)} %get-tuple-element.257), channel_id=1, source_target_pairs={{0,1},{1,0},{2,3},{3,2},{4,5},{5,4},{6,7},{7,6},{8,9},{9,8},{10,11... | collective-permute-start | bytes 786440 | tf_op jit(solution)/shard_map/ppermute | solution.py:786
  94.7 20.4 %collective-permute-start.24 = (bf16[384,512]{1,0:T(8,128)(2,1)S(1)}, bf16[384,512]{1,0:T(8,128)(2,1)S(1)}, u32[]{:S(2)}, u32[]{:S(2)}) collective-permute-start(bf16[384,512]{1,0:T(8,128)(2,1)S(1)} %get-tuple-element.263.refs_0_), channel_id=1, source_target_pairs={{0,4},{1,5},{2,6},{3,7},{4,0},{5,1},{6,2},{7,3},{8,12},{9,13},{10,... | collective-permute-start | bytes 1179656 | tf_op jit(solution)/shard_map/ppermute | solution.py:786
  97.5 23.3 %collective-permute-start.19 = (bf16[384,768]{1,0:T(8,128)(2,1)S(1)}, bf16[384,768]{1,0:T(8,128)(2,1)S(1)}, u32[]{:S(2)}, u32[]{:S(2)}) collective-permute-start(bf16[384,768]{1,0:T(8,128)(2,1)S(1)} %get-tuple-element.246), channel_id=1, source_target_pairs={{0,2},{1,3},{2,0},{3,1},{4,6},{5,7},{6,4},{7,5},{8,10},{9,11},{10,... | collective-permute-start | bytes 1769480 | tf_op jit(solution)/shard_map/ppermute | solution.py:786
  103.7 13.7 %collective-permute-start.23 = (bf16[196,768]{1,0:T(8,128)(2,1)S(1)}, bf16[196,768]{1,0:T(8,128)(2,1)S(1)}, u32[]{:S(2)}, u32[]{:S(2)}) collective-permute-start(bf16[196,768]{1,0:T(8,128)(2,1)S(1)} %get-tuple-element.258.refs_2_), channel_id=1, source_target_pairs={{0,8},{8,0},{1,9},{9,1},{2,10},{10,2},{3,11},{11,3},{4,12},{12,4},... | collective-permute-start | bytes 903176 | tf_op jit(solution)/shard_map/ppermute | solution.py:49
  105.0 15.7 %collective-permute-start.25 = (bf16[256,768]{1,0:T(8,128)(2,1)S(1)}, bf16[256,768]{1,0:T(8,128)(2,1)S(1)}, u32[]{:S(2)}, u32[]{:S(2)}) collective-permute-start(bf16[256,768]{1,0:T(8,128)(2,1)S(1)} %get-tuple-element.267), channel_id=1, source_target_pairs={{0,16},{16,0},{1,17},{17,1},{2,18},{18,2},{3,19},{19,3},{4,20},{20... | collective-permute-start | bytes 1179656 | tf_op jit(solution)/shard_map/ppermute | solution.py:49
  115.1 21.3 %collective-permute-start.28 = (bf16[384,512]{1,0:T(8,128)(2,1)S(1)}, bf16[384,512]{1,0:T(8,128)(2,1)S(1)}, u32[]{:S(2)}, u32[]{:S(2)}) collective-permute-start(bf16[384,512]{1,0:T(8,128)(2,1)S(1)} %get-tuple-element.270.refs_1_), channel_id=1, source_target_pairs={{0,1},{1,0},{2,3},{3,2},{4,5},{5,4},{6,7},{7,6},{8,9},{9,8},{10,11... | collective-permute-start | bytes 1179656 | tf_op jit(solution)/shard_map/ppermute | solution.py:786
  116.8 16.1 %collective-permute-start.27 = (bf16[384,512]{1,0:T(8,128)(2,1)S(1)}, bf16[384,512]{1,0:T(8,128)(2,1)S(1)}, u32[]{:S(2)}, u32[]{:S(2)}) collective-permute-start(bf16[384,512]{1,0:T(8,128)(2,1)S(1)} %get-tuple-element.270.refs_1_), channel_id=1, source_target_pairs={{0,2},{1,3},{2,0},{3,1},{4,6},{5,7},{6,4},{7,5},{8,10},{9,11},{10,... | collective-permute-start | bytes 1179656 | tf_op jit(solution)/shard_map/ppermute | solution.py:786
  120.7 14.3 %copy-start.18 = (bf16[128,1920]{1,0:T(8,128)(2,1)S(1)}, bf16[128,1920]{1,0:T(8,128)(2,1)}, u32[]{:S(2)}) copy-start(bf16[128,1920]{1,0:T(8,128)(2,1)} %copy-done.16) | copy-start | bytes 1474564
  120.7 14.3 %copy-start.33 = (bf16[128,768]{1,0:T(8,128)(2,1)S(1)}, bf16[128,768]{1,0:T(8,128)(2,1)}, u32[]{:S(2)}) copy-start(bf16[128,768]{1,0:T(8,128)(2,1)} %get-tuple-element.170.refs_7_.refs_1_) | copy-start | bytes 589828
  120.7 14.3 %copy-start.37 = (bf16[128,768]{1,0:T(8,128)(2,1)S(1)}, bf16[128,768]{1,0:T(8,128)(2,1)}, u32[]{:S(2)}) copy-start(bf16[128,768]{1,0:T(8,128)(2,1)} %copy-done.36) | copy-start | bytes 589828
  120.7 14.3 %copy-start.41 = (bf16[128,384]{1,0:T(8,128)(2,1)S(1)}, bf16[128,384]{1,0:T(8,128)(2,1)}, u32[]{:S(2)}) copy-start(bf16[128,384]{1,0:T(8,128)(2,1)} %get-tuple-element.171.refs_8_.refs_4_) | copy-start | bytes 294916
  120.8 14.3 %copy-start.43 = (bf16[128,384]{1,0:T(8,128)(2,1)S(1)}, bf16[128,384]{1,0:T(8,128)(2,1)}, u32[]{:S(2)}) copy-start(bf16[128,384]{1,0:T(8,128)(2,1)} %copy-done.42) | copy-start | bytes 294916
  120.9 22.6 %collective-permute-start.26 = (bf16[416,512]{1,0:T(8,128)(2,1)S(1)}, bf16[416,512]{1,0:T(8,128)(2,1)S(1)}, u32[]{:S(2)}, u32[]{:S(2)}) collective-permute-start(bf16[416,512]{1,0:T(8,128)(2,1)S(1)} %get-tuple-element.269.refs_2_), channel_id=1, source_target_pairs={{0,8},{8,0},{1,9},{9,1},{2,10},{10,2},{3,11},{11,3},{4,12},{12,4},... | collective-permute-start | bytes 1277960 | tf_op jit(solution)/shard_map/ppermute | solution.py:49
  122.3 27.3 %collective-permute-start.31 = (bf16[384,768]{1,0:T(8,128)(2,1)S(1)}, bf16[384,768]{1,0:T(8,128)(2,1)S(1)}, u32[]{:S(2)}, u32[]{:S(2)}) collective-permute-start(bf16[384,768]{1,0:T(8,128)(2,1)S(1)} %get-tuple-element.282.refs_0_), channel_id=1, source_target_pairs={{0,4},{1,5},{2,6},{3,7},{4,0},{5,1},{6,2},{7,3},{8,12},{9,13},{10,... | collective-permute-start | bytes 1769480 | tf_op jit(solution)/shard_map/ppermute | solution.py:786
  132.9 9.9 %collective-permute-start.29 = (bf16[384,512]{1,0:T(8,128)(2,1)S(1)}, bf16[384,512]{1,0:T(8,128)(2,1)S(1)}, u32[]{:S(2)}, u32[]{:S(2)}) collective-permute-start(bf16[384,512]{1,0:T(8,128)(2,1)S(1)} %collective-permute-done.27.refs_14_.refs_2_), channel_id=1, source_target_pairs={{0,1},{1,0},{2,3},{3,2},{4,5},{5,4},{6,7},{7,6},{8,9},{9,8},{10,11... | collective-permute-start | bytes 1179656 | tf_op jit(solution)/shard_map/ppermute | solution.py:786
  136.3 25.7 %collective-permute-start.30 = (bf16[880,256]{1,0:T(8,128)(2,1)S(1)}, bf16[880,256]{1,0:T(8,128)(2,1)S(1)}, u32[]{:S(2)}, u32[]{:S(2)}) collective-permute-start(bf16[880,256]{1,0:T(8,128)(2,1)S(1)} %get-tuple-element.281), channel_id=1, source_target_pairs={{0,2},{1,3},{2,0},{3,1},{4,6},{5,7},{6,4},{7,5},{8,10},{9,11},{10,... | collective-permute-start | bytes 1351688 | tf_op jit(solution)/shard_map/ppermute | solution.py:786
  143.5 29.5 %collective-permute-start.33 = (bf16[2,2,384,512]{3,2,1,0:T(8,128)(2,1)S(1)}, bf16[2,2,384,512]{3,2,1,0:T(8,128)(2,1)S(1)}, u32[]{:S(2)}, u32[]{:S(2)}) collective-permute-start(bf16[2,2,384,512]{3,2,1,0:T(8,128)(2,1)S(1)} %get-tuple-element.286.refs_1_), channel_id=1, source_target_pairs={{0,16},{16,0},{1,17},{17,1},{2,18},{18,2},{3,19},{19,3},{4,20},{20... | collective-permute-start | bytes 4718600 | tf_op jit(solution)/shard_map/ppermute | solution.py:49
  149.8 29.7 %collective-permute-start.38 = (bf16[384,768]{1,0:T(8,128)(2,1)S(1)}, bf16[384,768]{1,0:T(8,128)(2,1)S(1)}, u32[]{:S(2)}, u32[]{:S(2)}) collective-permute-start(bf16[384,768]{1,0:T(8,128)(2,1)S(1)} %get-tuple-element.289.refs_1_), channel_id=1, source_target_pairs={{0,1},{1,0},{2,3},{3,2},{4,5},{5,4},{6,7},{7,6},{8,9},{9,8},{10,11... | collective-permute-start | bytes 1769480 | tf_op jit(solution)/shard_map/ppermute | solution.py:786
  150.3 22.1 %collective-permute-start.34 = (bf16[384,768]{1,0:T(8,128)(2,1)S(1)}, bf16[384,768]{1,0:T(8,128)(2,1)S(1)}, u32[]{:S(2)}, u32[]{:S(2)}) collective-permute-start(bf16[384,768]{1,0:T(8,128)(2,1)S(1)} %get-tuple-element.289.refs_1_), channel_id=1, source_target_pairs={{0,2},{1,3},{2,0},{3,1},{4,6},{5,7},{6,4},{7,5},{8,10},{9,11},{10,... | collective-permute-start | bytes 1769480 | tf_op jit(solution)/shard_map/ppermute | solution.py:786
  162.2 16.3 %collective-permute-start.32 = (bf16[880,256]{1,0:T(8,128)(2,1)S(1)}, bf16[880,256]{1,0:T(8,128)(2,1)S(1)}, u32[]{:S(2)}, u32[]{:S(2)}) collective-permute-start(bf16[880,256]{1,0:T(8,128)(2,1)S(1)} %get-tuple-element.285.refs_0_), channel_id=1, source_target_pairs={{0,4},{1,5},{2,6},{3,7},{4,0},{5,1},{6,2},{7,3},{8,12},{9,13},{10,... | collective-permute-start | bytes 1351688 | tf_op jit(solution)/shard_map/ppermute | solution.py:786
  172.4 16.3 %collective-permute-start.39 = (bf16[384,768]{1,0:T(8,128)(2,1)S(1)}, bf16[384,768]{1,0:T(8,128)(2,1)S(1)}, u32[]{:S(2)}, u32[]{:S(2)}) collective-permute-start(bf16[384,768]{1,0:T(8,128)(2,1)S(1)} %collective-permute-done.34.refs_1_.refs_2_), channel_id=1, source_target_pairs={{0,1},{1,0},{2,3},{3,2},{4,5},{5,4},{6,7},{7,6},{8,9},{9,8},{10,11... | collective-permute-start | bytes 1769480 | tf_op jit(solution)/shard_map/ppermute | solution.py:786
  178.5 20.3 %collective-permute-start.36 = (bf16[880,256]{1,0:T(8,128)(2,1)S(1)}, bf16[880,256]{1,0:T(8,128)(2,1)S(1)}, u32[]{:S(2)}, u32[]{:S(2)}) collective-permute-start(bf16[880,256]{1,0:T(8,128)(2,1)S(1)} %get-tuple-element.291.refs_1_), channel_id=1, source_target_pairs={{0,1},{1,0},{2,3},{3,2},{4,5},{5,4},{6,7},{7,6},{8,9},{9,8},{10,11... | collective-permute-start | bytes 1351688 | tf_op jit(solution)/shard_map/ppermute | solution.py:786
  179.5 10.0 %collective-permute-start.35 = (bf16[880,256]{1,0:T(8,128)(2,1)S(1)}, bf16[880,256]{1,0:T(8,128)(2,1)S(1)}, u32[]{:S(2)}, u32[]{:S(2)}) collective-permute-start(bf16[880,256]{1,0:T(8,128)(2,1)S(1)} %get-tuple-element.291.refs_1_), channel_id=1, source_target_pairs={{0,2},{1,3},{2,0},{3,1},{4,6},{5,7},{6,4},{7,5},{8,10},{9,11},{10,... | collective-permute-start | bytes 1351688 | tf_op jit(solution)/shard_map/ppermute | solution.py:786
  189.4 4.6 %collective-permute-start.40 = (bf16[2,2,384,768]{3,2,1,0:T(8,128)(2,1)S(1)}, bf16[2,2,384,768]{3,2,1,0:T(8,128)(2,1)S(1)}, u32[]{:S(2)}, u32[]{:S(2)}) collective-permute-start(bf16[2,2,384,768]{3,2,1,0:T(8,128)(2,1)S(1)} %get-tuple-element.293.refs_1_), channel_id=1, source_target_pairs={{0,16},{16,0},{1,17},{17,1},{2,18},{18,2},{3,19},{19,3},{4,20},{20... | collective-permute-start | bytes 7077896 | tf_op jit(solution)/shard_map/ppermute | solution.py:49
  189.5 14.8 %collective-permute-start.37 = (bf16[880,256]{1,0:T(8,128)(2,1)S(1)}, bf16[880,256]{1,0:T(8,128)(2,1)S(1)}, u32[]{:S(2)}, u32[]{:S(2)}) collective-permute-start(bf16[880,256]{1,0:T(8,128)(2,1)S(1)} %collective-permute-done.35.refs_1_.refs_2_), channel_id=1, source_target_pairs={{0,1},{1,0},{2,3},{3,2},{4,5},{5,4},{6,7},{7,6},{8,9},{9,8},{10,11... | collective-permute-start | bytes 1351688 | tf_op jit(solution)/shard_map/ppermute | solution.py:786
  205.0 3.8 %collective-permute-start.41 = (bf16[2,2,880,256]{3,2,1,0:T(8,128)(2,1)S(1)}, bf16[2,2,880,256]{3,2,1,0:T(8,128)(2,1)S(1)}, u32[]{:S(2)}, u32[]{:S(2)}) collective-permute-start(bf16[2,2,880,256]{3,2,1,0:T(8,128)(2,1)S(1)} %get-tuple-element.297.refs_1_), channel_id=1, source_target_pairs={{0,16},{16,0},{1,17},{17,1},{2,18},{18,2},{3,19},{19,3},{4,20},{20... | collective-permute-start | bytes 5406728 | tf_op jit(solution)/shard_map/ppermute | solution.py:49
  (28 other events, 124.4 us)
